TPU v7x, 512 devices: a whole 4x8x8 slice. The times are simulated.
512 devices in a mesh: member: 16 (over z, core), domain: 32 (over y, x).
Axes of the slice: x: 4, y: 8, z: 8, core: 2. Of those that a mesh axis runs over, the one named last changes fastest.
Arguments:
- initial_realizations: float32 [64, 6, 2048, 256], P('member', None, 'domain'), may hold values from -6 to 6
- land_mask: int32 [2048, 256], P('domain'), may hold values 0 or 1
- obs_index: int32 [32, 16, 256], P('domain', 'member'), may hold values from 0 to 6143
- obs_count: int32 [32, 16], P('domain', 'member'), may hold values from 1 to 256, 2048 in all within a row
- obs_value: float32 [32, 16, 256], P('domain', 'member'), may hold values from -6 to 6
- obs_error: float32 [32, 16, 256], P('domain', 'member'), may hold values from 0.1 to 2
Outputs:
- increments: float32 [64, 6, 2048, 256], P('member', None, 'domain')
Inputs may be any that keep to these rules, and one draw needn't show every extreme that they name: `obs_count`: in every tile one region has exactly 256 observations, and the counts of a tile's regions sum to 2048.
All inputs are finite; a program needn't handle non-finite values. No bound on the sum of `land_mask` or of `obs_count` on one device may be relied on, other than what follows from the above.
Results may differ from a plain program's by a relative error of at most 0.0003.
Values sent between devices are 32-bit elements; how exact they have to be, the bound alone decides.
No kernel may reach another device: no remote copies, remote signals or barrier semaphores. Data moves between devices by JAX's collectives and lax.ppermute only.
A program may use at most 192 MiB of HBM per device.

v0:
```python
import math

import jax
import jax.numpy as jnp
from jax import lax
from jax.sharding import PartitionSpec as P

PATCH_WIDTH = 32
NS_ITERS = 8


COURANT = 0.25
CORIOLIS = 0.1
DEPTH_TOP = 1.0
DEPTH_DEEP = 0.5
STRATIFY = 1.5


def with_halo(block, sides, width):
    for axis, dim in sides:
        count = lax.axis_size(axis)
        forward = [(i, i + 1) for i in range(count - 1)]
        forward.append((count - 1, 0))
        backward = [(target, source) for source, target in forward]
        low = lax.ppermute(
            lax.slice_in_dim(block, block.shape[dim] - width, None, axis=dim), axis, forward
        )
        high = lax.ppermute(lax.slice_in_dim(block, 0, width, axis=dim), axis, backward)
        block = jnp.concatenate([low, block, high], axis=dim)
    return block


def diff_east(field):
    return (field[..., 2:, :] - field[..., :-2, :]) * 0.5


def diff_north(field):
    padded = jnp.pad(field, [(0, 0)] * (field.ndim - 1) + [(1, 1)])
    return (padded[..., 2:] - padded[..., :-2]) * 0.5


def momentum(zonal, merid, pressure, mask_rows):
    zonal_new = (
        zonal[..., 2:-2, :] + CORIOLIS * merid[..., 2:-2, :] - COURANT * diff_east(pressure)
    ) * mask_rows
    merid_new = (
        merid[..., 2:-2, :]
        - CORIOLIS * zonal[..., 2:-2, :]
        - COURANT * diff_north(pressure)[..., 1:-1, :]
    ) * mask_rows
    return (zonal_new, merid_new)


def advance(state, mask_rows):
    zonal_top = state[..., 0, :, :]
    merid_top = state[..., 1, :, :]
    thick_top = state[..., 2, :, :]
    zonal_deep = state[..., 3, :, :]
    merid_deep = state[..., 4, :, :]
    thick_deep = state[..., 5, :, :]
    new_top = thick_top[..., 1:-1, :] - COURANT * DEPTH_TOP * (
        diff_east(zonal_top) + diff_north(merid_top)[..., 1:-1, :]
    )
    new_deep = thick_deep[..., 1:-1, :] - COURANT * DEPTH_DEEP * (
        diff_east(zonal_deep) + diff_north(merid_deep)[..., 1:-1, :]
    )
    press_top = new_top + new_deep
    press_deep = new_top + STRATIFY * new_deep
    zonal_top_new, merid_top_new = momentum(zonal_top, merid_top, press_top, mask_rows)
    zonal_deep_new, merid_deep_new = momentum(zonal_deep, merid_deep, press_deep, mask_rows)
    return jnp.stack(
        [
            zonal_top_new,
            merid_top_new,
            new_top[..., 1:-1, :],
            zonal_deep_new,
            merid_deep_new,
            new_deep[..., 1:-1, :],
        ],
        axis=-3,
    )


def weights(observed, values, errors, count):
    highest = lax.Precision.HIGHEST
    ensemble_size = observed.shape[0]
    obs_mean = jnp.mean(observed, axis=0)
    spread = observed - obs_mean
    slots = jnp.arange(observed.shape[1], dtype=jnp.int32)
    precision_w = jnp.where(slots < count, 1.0 / errors, 0.0)
    innovation = values - obs_mean
    scaled = spread * precision_w
    identity = jnp.eye(ensemble_size, dtype=observed.dtype)
    system = (ensemble_size - 1.0) * identity + jnp.dot(scaled, spread.T, precision=highest)
    norm_frob = jnp.sqrt(jnp.sum(system * system))
    root = system / norm_frob
    inverse_root = identity
    for sweep_index in range(NS_ITERS):
        factor = 1.5 * identity - 0.5 * jnp.dot(inverse_root, root, precision=highest)
        root = jnp.dot(root, factor, precision=highest)
        inverse_root = jnp.dot(factor, inverse_root, precision=highest)
    sqrt_inv = inverse_root / jnp.sqrt(norm_frob)
    covariance = jnp.dot(sqrt_inv, sqrt_inv, precision=highest)
    mean_weights = jnp.dot(
        covariance, jnp.dot(scaled, innovation, precision=highest), precision=highest
    )
    return mean_weights[:, None] + math.sqrt(ensemble_size - 1.0) * sqrt_inv - identity


def pick_columns(block, chosen):
    return jnp.take(block, chosen, axis=1)


def apply_transform(matrices, grouped):
    deviations = grouped - jnp.mean(grouped, axis=1, keepdims=True)
    return jnp.einsum("rjk,rjvc->rkvc", matrices, deviations, precision=lax.Precision.HIGHEST)


def local(initial_realizations, land_mask, obs_index, obs_count, obs_value, obs_error):
    mask_rows = land_mask.astype(jnp.float32)
    states = initial_realizations
    for sweep_index in range(2):
        widened = with_halo(states, (("domain", 2),), 2)
        states = advance(widened, mask_rows)
    member_local, nvar_local, tile_rows, tile_cols = states.shape
    regions_x = tile_rows // PATCH_WIDTH
    regions_y = tile_cols // PATCH_WIDTH
    regions = states.reshape(
        member_local, nvar_local, regions_x, PATCH_WIDTH, regions_y, PATCH_WIDTH
    )
    regions = regions.transpose(2, 4, 0, 1, 3, 5).reshape(
        regions_x * regions_y, member_local, nvar_local, PATCH_WIDTH * PATCH_WIDTH
    )
    chosen_local = obs_index[0]
    counts = obs_count[0]
    values = obs_value[0]
    errors = obs_error[0]
    grouped = lax.all_to_all(regions, "member", split_axis=0, concat_axis=1, tiled=True)
    region_count, ensemble_size = (grouped.shape[0], grouped.shape[1])
    flat = grouped.reshape(region_count, ensemble_size, nvar_local * PATCH_WIDTH * PATCH_WIDTH)
    observed = jax.vmap(pick_columns)(flat, chosen_local)
    matrices = jax.vmap(weights)(observed, values, errors, counts)
    increment = apply_transform(matrices, grouped)
    returned = lax.all_to_all(increment, "member", split_axis=1, concat_axis=0, tiled=True)
    returned = returned.reshape(
        regions_x, regions_y, member_local, nvar_local, PATCH_WIDTH, PATCH_WIDTH
    )
    returned = returned.transpose(2, 3, 0, 4, 1, 5).reshape(
        member_local, nvar_local, tile_rows, tile_cols
    )
    return returned * mask_rows


def solution(mesh):
    in_specs = (
        P("member", None, "domain", None),
        P("domain", None),
        P("domain", "member", None),
        P("domain", "member"),
        P("domain", "member", None),
        P("domain", "member", None),
    )
    out_specs = P("member", None, "domain", None)
    return jax.shard_map(local, mesh=mesh, in_specs=in_specs, out_specs=out_specs, check_vma=False)
```

profile of v0, /device:TPU:1, one launch (start us, length us, event | category | flops | bytes accessed | tf_op | source)
XLA Modules:
  0.0 186.6 jit_solution(1192029698061890995)
XLA Ops:
  0.0 1.1 fusion.105
  1.1 3.9 %collective-permute-start = (f32[4,6,2,256]{3,2,1,0:T(2,128)S(1)}, f32[4,6,2,256]{3,2,1,0:T(2,128)S(1)}, u32[]{:S(2)}, u32[]{:S(2)}) collective-permute-start(f32[4,6,2,256]{3,2,1,0:T(2,128)S(1)} %get-tuple-element.25), channel_id=1, source_target_pairs={{0,1},{1,2},{2,3},{3,4},{4,5},{5,6},{6,7},{7,8},{8,9},{9,10},{10,1... | collective-permute-start | bytes 147464 | tf_op jit(solution)/shard_map/ppermute | solution.py:25
  5.0 6.1 %collective-permute-start.1 = (f32[4,6,2,256]{3,2,1,0:T(2,128)S(1)}, f32[4,6,2,256]{3,2,1,0:T(2,128)S(1)}, u32[]{:S(2)}, u32[]{:S(2)}) collective-permute-start(f32[4,6,2,256]{3,2,1,0:T(2,128)S(1)} %get-tuple-element.26), channel_id=1, source_target_pairs={{1,0},{2,1},{3,2},{4,3},{5,4},{6,5},{7,6},{8,7},{9,8},{10,9},{11,1... | collective-permute-start | bytes 147464 | tf_op jit(solution)/shard_map/ppermute | solution.py:28
  11.1 0.8 convert_element_type.16
  12.0 0.3 collective-permute-done.1
  12.3 1.6 pad_maximum_fusion
  14.0 0.4 pad_slice_fusion.13
  14.4 0.3 multiply_add_fusion.1
  14.8 0.2 pad_slice_fusion.11
  15.3 0.2 pad_slice_fusion.9
  15.9 1.9 %collective-permute-start.2 = (f32[4,6,2,256]{3,2,0,1:T(2,128)S(1)}, f32[4,6,2,256]{3,2,0,1:T(2,128)S(1)}, u32[]{:S(2)}, u32[]{:S(2)}) collective-permute-start(f32[4,6,2,256]{3,2,0,1:T(2,128)S(1)} %get-tuple-element.23), channel_id=1, source_target_pairs={{0,1},{1,2},{2,3},{3,4},{4,5},{5,6},{6,7},{7,8},{8,9},{9,10},{10,1... | collective-permute-start | bytes 147464 | tf_op jit(solution)/shard_map/ppermute | solution.py:25
  17.8 7.0 %collective-permute-start.3 = (f32[4,6,2,256]{3,2,0,1:T(2,128)S(1)}, f32[4,6,2,256]{3,2,0,1:T(2,128)S(1)}, u32[]{:S(2)}, u32[]{:S(2)}) collective-permute-start(f32[4,6,2,256]{3,2,0,1:T(2,128)S(1)} %get-tuple-element.24), channel_id=1, source_target_pairs={{1,0},{2,1},{3,2},{4,3},{5,4},{6,5},{7,6},{8,7},{9,8},{10,9},{11,1... | collective-permute-start | bytes 147464 | tf_op jit(solution)/shard_map/ppermute | solution.py:28
  24.8 1.1 collective-permute-done.3
  26.0 0.2 pad_maximum_fusion.1
  26.4 0.2 pad_slice_fusion.7
  26.6 0.2 pad_slice_fusion.5
  26.8 0.3 multiply_add_fusion
  27.2 0.7 slice.359
  27.9 0.2 pad_slice_fusion.3
  28.1 0.2 pad_slice_fusion.1
  28.3 0.4 fusion.31
  28.8 0.3 stack.49
  29.0 1.2 copy_dynamic-update-slice_fusion.5
  30.2 1.2 stack.50
  31.5 1.3 stack.51
  32.7 0.3 stack.52
  33.0 0.3 stack.53
  33.3 1.2 stack.54
  34.5 2.5 %copy_dynamic-update-slice_fusion.4 = f32[4,6,2,32,8,32]{5,3,4,2,1,0:T(8,128)} fusion(f32[4,6,2,32,8,32]{5,3,4,2,1,0:T(8,128)} %copy_dynamic-update-slice_fusion.5, f32[4,1,2,32,8,32]{5,4,3,2,0,1:T(8,128)} %stack.50), kind=kLoop, calls=%fused_computation.28 | loop fusion | bytes 2097152
  37.0 1.2 copy_dynamic-update-slice_fusion.3
  38.2 1.2 copy_dynamic-update-slice_fusion.2
  39.4 1.2 copy_dynamic-update-slice_fusion.1
  40.6 1.2 copy_dynamic-update-slice_fusion
  41.8 5.0 %reshape.565 = f32[16,4,6,1024]{3,0,2,1:T(8,128)S(1)} reshape(f32[2,8,4,6,32,32]{5,4,1,0,3,2:T(8,128)} %bitcast.178) | data formatting | bytes 3145728 | tf_op jit(solution)/shard_map/reshape | solution.py:131
  46.8 2.2 %copy.120 = f32[16,4,6,1024]{3,1,2,0:T(4,128)} copy(f32[16,4,6,1024]{3,0,2,1:T(8,128)S(1)} %reshape.565) | data formatting | bytes 3145728 | tf_op jit(solution)/shard_map/reshape | solution.py:131
  49.0 13.1 %all-to-all-start = ((f32[16,4,6,1024]{3,1,2,0:T(4,128)}), f32[16,4,6,1024]{3,1,2,0:T(4,128)S(1)}, u32[]{:S(2)}, u32[]{:S(2)}) async-start(f32[16,4,6,1024]{3,1,2,0:T(4,128)} %copy.120), calls=%async_computation | async-start | bytes 3145728 | tf_op jit(solution)/shard_map/all_to_all | solution.py:138
  62.9 37.7 %all-to-all-done = f32[16,4,6,1024]{3,1,2,0:T(4,128)S(1)} async-done(((f32[16,4,6,1024]{3,1,2,0:T(4,128)}), f32[16,4,6,1024]{3,1,2,0:T(4,128)S(1)}, u32[]{:S(2)}, u32[]{:S(2)}) %all-to-all-start) | async-done | bytes 1572896 | tf_op jit(solution)/shard_map/all_to_all | solution.py:138
  100.6 2.4 %copy.121 = f32[16,4,6,1024]{3,2,1,0:T(8,128)} copy(f32[16,4,6,1024]{3,1,2,0:T(4,128)S(1)} %all-to-all-done) | data formatting | bytes 3145728 | tf_op jit(solution)/shard_map/all_to_all | solution.py:138
  103.0 2.2 %reshape.566 = f32[1,64,6144]{2,1,0:T(8,128)S(1)} reshape(f32[16,4,6,1024]{3,2,1,0:T(8,128)} %copy.121) | data formatting | bytes 3145728 | tf_op jit(solution)/shard_map/reshape | solution.py:140
  105.2 2.3 %copy.122 = f32[1,64,6144]{1,2,0:T(8,128)} copy(f32[1,64,6144]{2,1,0:T(8,128)S(1)} %reshape.566) | data formatting | bytes 3145728 | tf_op jit(solution)/shard_map/reshape | solution.py:140
  107.4 2.3 %gather_fusion = f32[256,64]{1,0:T(8,128)S(1)} fusion(f32[1,64,6144]{1,2,0:T(8,128)} %copy.122, s32[256]{0:T(256)S(1)} %bitcast.177), kind=kCustom, calls=%fused_computation | custom fusion | bytes 133120 | tf_op jit(solution)/shard_map/vmap(jit(_take))/gather | solution.py:111
  109.8 0.2 fusion.72
  110.0 1.2 multiply_reduce_fusion
  112.0 0.2 fusion.91
  112.3 0.2 fusion.6
  112.8 0.2 fusion.5
  113.3 0.2 fusion.4
  113.9 0.2 fusion.3
  114.4 0.2 fusion.2
  114.9 0.2 fusion.1
  115.4 0.2 fusion
  115.6 0.2 convolution_divide_fusion
  115.9 0.4 reduce_sum.29
  116.3 0.4 broadcast_subtract_fusion
  116.9 0.5 sub.241
  117.5 0.3 convolution_bitcast_fusion.2
  118.0 1.6 convolution_bitcast_fusion
  119.6 1.6 copy.125
  121.2 43.9 %all_to_all.8 = f32[1,64,6,1024]{3,0,2,1:T(1,128)S(1)} all-to-all(f32[1,64,6,1024]{3,0,2,1:T(1,128)S(1)} %copy.125), channel_id=1, replica_groups=mesh['member'=16,'domain'=32] {'member'}, dimensions={1} | all-to-all | bytes 3145728 | tf_op jit(solution)/shard_map/all_to_all | solution.py:144
  165.0 0.5 copy.126
  165.6 4.1 %reshape.567 = f32[2,8,4,6,32,32]{5,4,2,1,0,3:T(8,128)} reshape(f32[1,64,6,1024]{3,1,2,0:T(8,128)S(1)} %copy.126) | data formatting | bytes 3145728 | tf_op jit(solution)/shard_map/reshape | solution.py:145
  169.6 11.4 %copy.127 = f32[4,6,2,32,8,32]{5,4,3,2,1,0:T(8,128)} copy(f32[4,6,2,32,8,32]{5,3,0,4,2,1:T(8,128)} %bitcast.176) | data formatting | bytes 3145728 | tf_op jit(solution)/shard_map/transpose | solution.py:148
  181.0 4.3 %reshape.568 = f32[4,6,64,256]{3,2,1,0:T(8,128)S(1)} reshape(f32[4,6,2,32,8,32]{5,4,3,2,1,0:T(8,128)} %copy.127) | data formatting | bytes 3145728 | tf_op jit(solution)/shard_map/reshape | solution.py:148
  185.3 1.3 broadcast_multiply_fusion
  (46 shorter events, 3.9 us)
Async XLA Ops:
  1.1 10.9 %collective-permute-start = (f32[4,6,2,256]{3,2,1,0:T(2,128)S(1)}, f32[4,6,2,256]{3,2,1,0:T(2,128)S(1)}, u32[]{:S(2)}, u32[]{:S(2)}) collective-permute-start(f32[4,6,2,256]{3,2,1,0:T(2,128)S(1)} %get-tuple-element.25), channel_id=1, source_target_pairs={{0,1},{1,2},{2,3},{3,4},{4,5},{5,6},{6,7},{7,8},{8,9},{9,10},{10,1... | collective-permute-start | bytes 147464 | tf_op jit(solution)/shard_map/ppermute | solution.py:25
  5.0 7.3 %collective-permute-start.1 = (f32[4,6,2,256]{3,2,1,0:T(2,128)S(1)}, f32[4,6,2,256]{3,2,1,0:T(2,128)S(1)}, u32[]{:S(2)}, u32[]{:S(2)}) collective-permute-start(f32[4,6,2,256]{3,2,1,0:T(2,128)S(1)} %get-tuple-element.26), channel_id=1, source_target_pairs={{1,0},{2,1},{3,2},{4,3},{5,4},{6,5},{7,6},{8,7},{9,8},{10,9},{11,1... | collective-permute-start | bytes 147464 | tf_op jit(solution)/shard_map/ppermute | solution.py:28
  15.9 8.9 %collective-permute-start.2 = (f32[4,6,2,256]{3,2,0,1:T(2,128)S(1)}, f32[4,6,2,256]{3,2,0,1:T(2,128)S(1)}, u32[]{:S(2)}, u32[]{:S(2)}) collective-permute-start(f32[4,6,2,256]{3,2,0,1:T(2,128)S(1)} %get-tuple-element.23), channel_id=1, source_target_pairs={{0,1},{1,2},{2,3},{3,4},{4,5},{5,6},{6,7},{7,8},{8,9},{9,10},{10,1... | collective-permute-start | bytes 147464 | tf_op jit(solution)/shard_map/ppermute | solution.py:25
  17.8 8.2 %collective-permute-start.3 = (f32[4,6,2,256]{3,2,0,1:T(2,128)S(1)}, f32[4,6,2,256]{3,2,0,1:T(2,128)S(1)}, u32[]{:S(2)}, u32[]{:S(2)}) collective-permute-start(f32[4,6,2,256]{3,2,0,1:T(2,128)S(1)} %get-tuple-element.24), channel_id=1, source_target_pairs={{1,0},{2,1},{3,2},{4,3},{5,4},{6,5},{7,6},{8,7},{9,8},{10,9},{11,1... | collective-permute-start | bytes 147464 | tf_op jit(solution)/shard_map/ppermute | solution.py:28
  34.5 2.5 %copy-start = (f32[4,1,2,32,8,32]{5,4,3,2,0,1:T(8,128)S(1)}, f32[4,1,2,32,8,32]{5,4,3,2,0,1:T(8,128)}, u32[]{:S(2)}) copy-start(f32[4,1,2,32,8,32]{5,4,3,2,0,1:T(8,128)} %stack.51) | copy-start | bytes 786436
  49.0 13.8 %copy-start.1 = (s32[1,1,256]{2,1,0:T(1,128)S(1)}, s32[1,1,256]{2,1,0:T(1,128)}, u32[]{:S(2)}) copy-start(s32[1,1,256]{2,1,0:T(1,128)} %param.8) | copy-start | bytes 3076
  49.0 13.8 %copy-start.2 = (f32[1,1,256]{2,1,0:T(1,128)S(1)}, f32[1,1,256]{2,1,0:T(1,128)}, u32[]{:S(2)}) copy-start(f32[1,1,256]{2,1,0:T(1,128)} %param.11) | copy-start | bytes 3076
  49.0 51.6 %all-to-all-start = ((f32[16,4,6,1024]{3,1,2,0:T(4,128)}), f32[16,4,6,1024]{3,1,2,0:T(4,128)S(1)}, u32[]{:S(2)}, u32[]{:S(2)}) async-start(f32[16,4,6,1024]{3,1,2,0:T(4,128)} %copy.120), calls=%async_computation | async-start | bytes 3145728 | tf_op jit(solution)/shard_map/all_to_all | solution.py:138
  116.8 0.7 copy-start.3
where the time goes:
time: 189 us; the launch traced here: 187 us
  local copies, waits for them, and re-layouts  55.9 us (30%)
  blocking collectives  43.9 us (23%)
  waiting for transfers between devices  39.1 us (21%)
  starting transfers between devices  32.1 us (17%)
  matrix products  7.1 us (4%)
  other arithmetic  6.56 us (3%)
  between operations  1.95 us (1%)
    all_to_all x1, blocking collectives, local(): lax.all_to_all(increment, 'member', split_axis=1, concat_axis=0, tiled=True)  43.9 us
    all_to_all x1, waiting for transfers between devices, local(): lax.all_to_all(regions, 'member', split_axis=0, concat_axis=1, tiled=True)  37.7 us
    all_to_all x1, starting transfers between devices, local(): lax.all_to_all(regions, 'member', split_axis=0, concat_axis=1, tiled=True)  13.1 us
    ppermute x2, starting transfers between devices, with_halo(): lax.ppermute(lax.slice_in_dim(block, 0, width, axis=dim), axis, backward)  13.1 us
    transpose x1, local copies, waits for them, and re-layouts, local(): returned.transpose(2, 3, 0, 4, 1, 5)  11.4 us
    unnamed x14, local copies, waits for them, and re-layouts  7.48 us
    reshape x2, local copies, waits for them, and re-layouts, local(): regions.transpose(2, 4, 0, 1, 3, 5)  7.18 us
    ppermute x2, starting transfers between devices, with_halo(): lax.ppermute(lax.slice_in_dim(block, block.shape[dim] - width, None, axis...  5.87 us
  transfers between devices with their start and end apart: 5, of which 3 were waited for; matrix products, arithmetic and copies ran while one was open for 0% of the time, Pallas kernels for 0%

commit v1 on v0

v1 whole, which is shorter than its diff:
```python
import math

import jax
import jax.numpy as jnp
from jax import lax
from jax.experimental import pallas as pl
from jax.experimental.pallas import tpu as pltpu
from jax.sharding import PartitionSpec as P

NS_ITERS = 8
CORIOLIS = 0.1
STRATIFY = 1.5
HALO = 4
VMEM_LIMIT = 48 * 1024 * 1024


def call(kernel, out_shape, n_in, scratch=(), aliases=None, flops=1000000, nbytes=3000000):
    whole = pl.BlockSpec(memory_space=pltpu.VMEM)
    return pl.pallas_call(
        kernel,
        out_shape=out_shape,
        in_specs=[whole] * n_in,
        out_specs=jax.tree.map(lambda _: whole, out_shape),
        scratch_shapes=list(scratch),
        input_output_aliases=aliases or {},
        compiler_params=pltpu.CompilerParams(vmem_limit_bytes=VMEM_LIMIT),
        cost_estimate=pl.CostEstimate(flops=flops, bytes_accessed=nbytes, transcendentals=0),
    )


def east(field):
    rows = field.shape[0]
    return pltpu.roll(field, rows - 1, 0) - pltpu.roll(field, 1, 0)


def north(field, first, last):
    cols = field.shape[1]
    ahead = jnp.where(last, 0.0, pltpu.roll(field, cols - 1, 1))
    behind = jnp.where(first, 0.0, pltpu.roll(field, 1, 1))
    return ahead - behind


def step(state, mask, first, last):
    u1, v1, h1, u2, v2, h2 = state
    h1 = h1 - 0.125 * (east(u1) + north(v1, first, last))
    h2 = h2 - 0.0625 * (east(u2) + north(v2, first, last))
    p1 = h1 + h2
    p2 = h1 + STRATIFY * h2
    u1n = (u1 + CORIOLIS * v1 - 0.125 * east(p1)) * mask
    v1n = (v1 - CORIOLIS * u1 - 0.125 * north(p1, first, last)) * mask
    u2n = (u2 + CORIOLIS * v2 - 0.125 * east(p2)) * mask
    v2n = (v2 - CORIOLIS * u2 - 0.125 * north(p2, first, last)) * mask
    return (u1n, v1n, h1, u2n, v2n, h2)


def forecast(state, mask):
    lane = lax.broadcasted_iota(jnp.int32, mask.shape, 1)
    first = lane == 0
    last = lane == mask.shape[1] - 1
    for _ in range(2):
        state = step(state, mask, first, last)
    return state


def swap_blocks(x, low, even):
    y0 = jnp.where(low, x[0], pltpu.roll(x[2], 64, 1))
    y2 = jnp.where(low, pltpu.roll(x[0], 64, 1), x[2])
    y1 = jnp.where(low, x[1], pltpu.roll(x[3], 64, 1))
    y3 = jnp.where(low, pltpu.roll(x[1], 64, 1), x[3])
    z0 = jnp.where(even, y0, pltpu.roll(y1, 32, 1))
    z1 = jnp.where(even, pltpu.roll(y0, 96, 1), y1)
    z2 = jnp.where(even, y2, pltpu.roll(y3, 32, 1))
    z3 = jnp.where(even, pltpu.roll(y2, 96, 1), y3)
    return (z0, z1, z2, z3)


def lane_tests():
    lane = lax.broadcasted_iota(jnp.int32, (8, 128), 1)
    return lane < 64, (lane // 32) % 2 == 0, lane


def edges_kernel(state, land, low_out, high_out):
    low_out[24] = land[60:64, :].astype(jnp.float32)
    high_out[24] = land[0:4, :].astype(jnp.float32)
    for m in range(4):
        for f in range(6):
            low_out[6 * m + f] = state[m, f, 60:64, :]
            high_out[6 * m + f] = state[m, f, 0:4, :]


def interior_kernel(state, land, packed):
    low, even, _ = lane_tests()
    mask = land[...].astype(jnp.float32)

    def one(m, carry):
        fields = forecast(tuple(state[m, f] for f in range(6)), mask)
        for f in range(6):
            for qx in range(2):
                for g in range(2):
                    x = [
                        fields[f][qx * 32 + 8 * a : qx * 32 + 8 * a + 8, g * 128 : g * 128 + 128]
                        for a in range(4)
                    ]
                    z = swap_blocks(x, low, even)
                    for b in range(4):
                        packed[qx * 8 + g * 4 + b, m, f] = z[b]
        return carry

    lax.fori_loop(0, 4, one, 0)


def border_kernel(state, land, from_low, from_high, inner, packed):
    _, _, lane = lane_tests()
    pad = jnp.zeros((8 - HALO, 256), jnp.float32)
    mask_low = jnp.concatenate([pad, from_low[24], land[0:16, :].astype(jnp.float32)], axis=0)
    mask_high = jnp.concatenate([land[48:64, :].astype(jnp.float32), from_high[24], pad], axis=0)

    def one(m, carry):
        for qx in range(2):
            if qx == 0:
                begin = tuple(
                    jnp.concatenate([pad, from_low[6 * m + f], state[m, f, 0:16, :]], axis=0)
                    for f in range(6)
                )
                fields = forecast(begin, mask_low)
                mine = lane < 32
            else:
                begin = tuple(
                    jnp.concatenate([state[m, f, 48:64, :], from_high[6 * m + f], pad], axis=0)
                    for f in range(6)
                )
                fields = forecast(begin, mask_high)
                mine = lane >= 96
            for f in range(6):
                for g in range(2):
                    x = fields[f][8:16, g * 128 : g * 128 + 128]
                    for b in range(4):
                        turn = ((0 if qx == 0 else 3) - b) % 4 * 32
                        moved = pltpu.roll(x, turn, 1) if turn else x
                        q = qx * 8 + g * 4 + b
                        packed[q, m, f] = jnp.where(mine, moved, inner[q, m, f])
        return carry

    lax.fori_loop(0, 4, one, 0)


def analysis_kernel(x_ref, index, count, values, errors, out_ref, dev_ref):
    highest = lax.Precision.HIGHEST
    members = 64
    chosen = index[...]
    entry_row = ((chosen >> 10) << 3) + ((chosen >> 5) & 7)
    entry_lane = (((chosen >> 8) & 3) << 5) + (chosen & 31)
    rows_of = [jnp.broadcast_to(entry_row[:, 128 * i : 128 * i + 128], (members, 128)) for i in range(2)]
    lanes_of = [jnp.broadcast_to(entry_lane[:, 128 * i : 128 * i + 128], (members, 128)) for i in range(2)]

    def scan(r, acc):
        x = x_ref[pl.ds(r, members, stride=48), :]
        dev_ref[r] = x - jnp.sum(x, axis=0, keepdims=True) * (1.0 / members)
        return tuple(
            jnp.where(rows_of[i] == r, jnp.take_along_axis(x, lanes_of[i], axis=1), acc[i])
            for i in range(2)
        )

    zero = jnp.zeros((members, 128), jnp.float32)
    observed = jnp.concatenate(lax.fori_loop(0, 48, scan, (zero, zero)), axis=1)
    obs_mean = jnp.sum(observed, axis=0, keepdims=True) * (1.0 / members)
    spread = observed - obs_mean
    slots = lax.broadcasted_iota(jnp.int32, (1, 256), 1)
    weight = jnp.where(slots < count[0, 0], 1.0 / errors[...], 0.0)
    innovation = values[...] - obs_mean
    scaled = spread * weight
    eye = (
        lax.broadcasted_iota(jnp.int32, (members, members), 0)
        == lax.broadcasted_iota(jnp.int32, (members, members), 1)
    ).astype(jnp.float32)

    def dot(a, b):
        return jnp.dot(a, b, precision=highest, preferred_element_type=jnp.float32)

    system = (members - 1.0) * eye + lax.dot_general(
        scaled, spread, (((1,), (1,)), ((), ())), precision=highest, preferred_element_type=jnp.float32
    )
    total = jnp.sum(jnp.sum(system * system, axis=1, keepdims=True), axis=0, keepdims=True)
    norm = jnp.sqrt(total)
    root = system / norm
    inverse = eye
    for sweep in range(NS_ITERS):
        factor = 1.5 * eye - 0.5 * (root if sweep == 0 else dot(inverse, root))
        if sweep < NS_ITERS - 1:
            root = dot(root, factor)
        inverse = factor if sweep == 0 else dot(factor, inverse)
    sqrt_inv = inverse / jnp.sqrt(norm)
    moved = jnp.sum(scaled * innovation, axis=1, keepdims=True)
    half = jnp.sum(sqrt_inv * moved, axis=0, keepdims=True)
    mean_weights = jnp.sum(sqrt_inv * half, axis=1, keepdims=True)
    transform = mean_weights + math.sqrt(members - 1.0) * sqrt_inv - eye
    flipped = transform.T

    def apply(r, carry):
        out_ref[pl.ds(r, members, stride=48), :] = dot(flipped, dev_ref[r])
        return carry

    lax.fori_loop(0, 48, apply, 0)


def unpack_kernel(packed, land, out):
    low, even, _ = lane_tests()
    mask = land[...].astype(jnp.float32)

    def one(m, carry):
        for f in range(6):
            for qx in range(2):
                for g in range(2):
                    x = [packed[qx * 8 + g * 4 + b, m, f] for b in range(4)]
                    z = swap_blocks(x, low, even)
                    for a in range(4):
                        rows = slice(qx * 32 + 8 * a, qx * 32 + 8 * a + 8)
                        cols = slice(g * 128, g * 128 + 128)
                        out[m, f, rows, cols] = z[a] * mask[rows, cols]
        return carry

    lax.fori_loop(0, 4, one, 0)


def shape(*dims):
    return jax.ShapeDtypeStruct(dims, jnp.float32)


def local(initial_realizations, land_mask, obs_index, obs_count, obs_value, obs_error):
    to_high, to_low = call(edges_kernel, [shape(25, HALO, 256)] * 2, 2, nbytes=200000)(
        initial_realizations, land_mask
    )
    count = lax.axis_size("domain")
    forward = [(i, (i + 1) % count) for i in range(count)]
    backward = [(target, source) for source, target in forward]
    from_low = lax.ppermute(to_high, "domain", forward)
    from_high = lax.ppermute(to_low, "domain", backward)
    packed = call(interior_kernel, shape(16, 4, 6, 8, 128), 2)(initial_realizations, land_mask)
    packed = call(border_kernel, shape(16, 4, 6, 8, 128), 5, aliases={4: 0})(
        initial_realizations, land_mask, from_low, from_high, packed
    )
    grouped = lax.all_to_all(packed, "member", split_axis=0, concat_axis=0, tiled=True)
    whole = pl.BlockSpec(memory_space=pltpu.VMEM)
    increment = pl.pallas_call(
        analysis_kernel,
        out_shape=shape(3072, 128),
        in_specs=[whole, whole, pl.BlockSpec(memory_space=pltpu.SMEM), whole, whole],
        out_specs=whole,
        scratch_shapes=[pltpu.VMEM((48, 64, 128), jnp.float32)],
        compiler_params=pltpu.CompilerParams(vmem_limit_bytes=VMEM_LIMIT),
    )(grouped.reshape(3072, 128), obs_index[0], obs_count, obs_value[0], obs_error[0])
    returned = lax.all_to_all(
        increment.reshape(16, 4, 6, 8, 128), "member", split_axis=0, concat_axis=0, tiled=True
    )
    return call(unpack_kernel, shape(4, 6, 64, 256), 2)(returned, land_mask)


def solution(mesh):
    in_specs = (
        P("member", None, "domain", None),
        P("domain", None),
        P("domain", "member", None),
        P("domain", "member"),
        P("domain", "member", None),
        P("domain", "member", None),
    )
    out_specs = P("member", None, "domain", None)
    return jax.shard_map(local, mesh=mesh, in_specs=in_specs, out_specs=out_specs, check_vma=False)
```

time: 189 us -> 138 us (0.73); the launches traced: 187 us -> 138 us
  local copies, waits for them, and re-layouts: 55.9 us -> 2.26 us
  Pallas kernels: 0 us -> 31.4 us
  starting transfers between devices: 32.1 us -> 21.5 us
  matrix products: 7.1 us -> 0 us
  other arithmetic: 6.56 us -> 0 us
    pallas_call x0 -> x5, Pallas kernels: none -> 31.4 us  [the longest x1 16.1 us: local(): pl.pallas_call(analysis_kernel, out_shape=shape(3072, 128), in_specs=[who...]
    reshape x6 -> x0, local copies, waits for them, and re-layouts: 20 us -> none  [the longest x2 7.18 us: local(): regions.transpose(2, 4, 0, 1, 3, 5)]
    transpose x1 -> x0, local copies, waits for them, and re-layouts: 11.4 us -> none  [local(): returned.transpose(2, 3, 0, 4, 1, 5)]
    ppermute x4 -> x2, starting transfers between devices: 19 us -> 10 us  [the longest x1 6.09 us: local(): from_high = lax.ppermute(to_low, 'domain', backward)]
    dot_general x28 -> x0, matrix products: 7.1 us -> none  [the longest x1 1.56 us: apply_transform(): jnp.einsum('rjk,rjvc->rkvc', matrices, deviations, precision=lax.Precisio...]
    another operation x8 -> x0, local copies, waits for them, and re-layouts: 5.72 us -> none  [advance(): jnp.stack([zonal_top_new, merid_top_new, new_top[..., 1:-1, :], zonal_dee...]
    unnamed x14 -> x12, local copies, waits for them, and re-layouts: 7.48 us -> 2.26 us
    slice x11 -> x0, local copies, waits for them, and re-layouts: 3.48 us -> none  [the longest x7 1.65 us: diff_north(): return (padded[..., 2:] - padded[..., :-2]) * 0.5]
  transfers between devices with their start and end apart: 5 -> 3, of which waited for: 3 -> 1; matrix products, arithmetic and copies ran while one was open for 0% -> 0% of each run, Pallas kernels for 0% -> 5%
where the time goes in v1:
time: 138 us
  blocking collectives  44 us (32%)
  waiting for transfers between devices  37.8 us (27%)
  Pallas kernels  31.4 us (23%)
  starting transfers between devices  21.5 us (16%)
  local copies, waits for them, and re-layouts  2.26 us (2%)
    all_to_all x1, blocking collectives, local(): lax.all_to_all(increment.reshape(16, 4, 6, 8, 128), 'member', split_axis=...  44 us
    all_to_all x1, waiting for transfers between devices, local(): lax.all_to_all(packed, 'member', split_axis=0, concat_axis=0, tiled=True)  37.8 us
    pallas_call x1, Pallas kernels, local(): pl.pallas_call(analysis_kernel, out_shape=shape(3072, 128), in_specs=[who...  16.1 us
    all_to_all x1, starting transfers between devices, local(): lax.all_to_all(packed, 'member', split_axis=0, concat_axis=0, tiled=True)  11.4 us
    pallas_call x1, Pallas kernels, local(): call(interior_kernel, shape(16, 4, 6, 8, 128), 2)  6.43 us
    ppermute x1, starting transfers between devices, local(): from_high = lax.ppermute(to_low, 'domain', backward)  6.09 us
    pallas_call x1, Pallas kernels, local(): call(border_kernel, shape(16, 4, 6, 8, 128), 5, aliases={4: 0})  4.54 us
    pallas_call x1, Pallas kernels, local(): return call(unpack_kernel, shape(4, 6, 64, 256), 2)(returned, land_mask)  4.34 us
  transfers between devices with their start and end apart: 3, of which 1 were waited for; matrix products, arithmetic and copies ran while one was open for 0% of the time, Pallas kernels for 5%

profile of v1, /device:TPU:1, one launch (start us, length us, event | category | flops | bytes accessed | tf_op | source)
XLA Modules:
  0.0 137.6 jit_solution(17882079335902251098)
XLA Ops:
  0.0 0.0 copy-start
  0.0 1.4 %copy-done = f32[4,6,64,256]{3,2,1,0:T(8,128)S(1)} copy-done((f32[4,6,64,256]{3,2,1,0:T(8,128)S(1)}, f32[4,6,64,256]{3,2,1,0:T(8,128)}, u32[]{:S(2)}) %copy-start) | copy-done | bytes 1572888
  1.4 0.0 copy-start.1
  1.4 0.8 copy-done.1
  2.3 3.9 %collective-permute-start = (f32[25,4,256]{2,1,0:T(4,128)S(1)}, f32[25,4,256]{2,1,0:T(4,128)S(1)}, u32[]{:S(2)}, u32[]{:S(2)}) collective-permute-start(f32[25,4,256]{2,1,0:T(4,128)S(1)} %get-tuple-element.7), channel_id=1, source_target_pairs={{0,1},{1,2},{2,3},{3,4},{4,5},{5,6},{6,7},{7,8},{8,9},{9,10},{10,1... | collective-permute-start | bytes 307208 | tf_op jit(solution)/shard_map/ppermute | solution.py:236
  6.2 6.1 %collective-permute-start.1 = (f32[25,4,256]{2,1,0:T(4,128)S(1)}, f32[25,4,256]{2,1,0:T(4,128)S(1)}, u32[]{:S(2)}, u32[]{:S(2)}) collective-permute-start(f32[25,4,256]{2,1,0:T(4,128)S(1)} %get-tuple-element.8), channel_id=1, source_target_pairs={{1,0},{2,1},{3,2},{4,3},{5,4},{6,5},{7,6},{8,7},{9,8},{10,9},{11,1... | collective-permute-start | bytes 307208 | tf_op jit(solution)/shard_map/ppermute | solution.py:237
  12.3 6.4 %shard_map.65.inner = f32[16,4,6,8,128]{4,3,2,1,0:T(8,128)} custom-call(f32[4,6,64,256]{3,2,1,0:T(8,128)S(1)} %copy-done, s32[64,256]{1,0:T(8,128)S(1)} %copy-done.1), custom_call_target="tpu_custom_call" | custom-call | flops 1000000 | bytes 3000000 | tf_op jit(solution)/shard_map/pallas_call | solution.py:238
  18.8 0.0 collective-permute-done.from_low
  18.8 0.0 collective-permute-done.1.from_high
  18.8 4.5 %shard_map.66 = f32[16,4,6,8,128]{4,3,2,1,0:T(8,128)} custom-call(f32[4,6,64,256]{3,2,1,0:T(8,128)S(1)} %copy-done, s32[64,256]{1,0:T(8,128)S(1)} %copy-done.1, f32[25,4,256]{2,1,0:T(4,128)S(1)} %collective-permute-done.from_low, f32[25,4,256]{2,1,0:T(4,128)S(1)} %collective-permute-done.1.from_high, ...), custom_call_target="tpu_custom_call", output_to_operand_aliasing={{}: (4, {})} | custom-call | flops 1000000 | bytes 3000000 | tf_op jit(solution)/shard_map/pallas_call | solution.py:239
  23.3 0.0 copy-start.3
  23.3 0.0 copy-start.4
  23.3 0.0 copy-start.5
  23.3 11.4 %all-to-all-start = ((f32[16,4,6,8,128]{4,3,2,1,0:T(8,128)}), f32[16,4,6,8,128]{4,3,2,1,0:T(8,128)S(1)}, u32[]{:S(2)}, u32[]{:S(2)}) async-start(f32[16,4,6,8,128]{4,3,2,1,0:T(8,128)} %shard_map.66), calls=%async_computation | async-start | bytes 3145728 | tf_op jit(solution)/shard_map/all_to_all | solution.py:242
  35.4 37.8 %all-to-all-done = f32[16,4,6,8,128]{4,3,2,1,0:T(8,128)S(1)} async-done(((f32[16,4,6,8,128]{4,3,2,1,0:T(8,128)}), f32[16,4,6,8,128]{4,3,2,1,0:T(8,128)S(1)}, u32[]{:S(2)}, u32[]{:S(2)}) %all-to-all-start) | async-done | bytes 1572896 | tf_op jit(solution)/shard_map/all_to_all | solution.py:242
  73.2 0.0 copy-done.3
  73.2 0.0 copy-done.4
  73.2 0.0 copy-done.5
  73.2 16.1 %shard_map.67 = f32[3072,128]{1,0:T(8,128)S(1)} custom-call(f32[3072,128]{1,0:T(8,128)S(1)} %bitcast.5, s32[1,256]{1,0:T(1,128)S(1)} %bitcast.7, s32[1,1]{1,0:T(1,128)S(6)} %copy.9.count, f32[1,256]{1,0:T(1,128)S(1)} %bitcast.8, f32[1,256]{1,0:T(1,128)S(1)} %bitcast.9), custom_call_target="tpu_custom_call" | custom-call | tf_op jit(solution)/shard_map/pallas_call | solution.py:244
  89.3 0.0 copy-start.2
  89.3 44.0 %all_to_all.10.packed = f32[16,4,6,8,128]{4,3,2,1,0:T(8,128)S(1)} all-to-all(f32[16,4,6,8,128]{4,3,2,1,0:T(8,128)S(1)} %bitcast.6), channel_id=1, replica_groups=mesh['member'=16,'domain'=32] {'member'}, dimensions={0} | all-to-all | bytes 3145728 | tf_op jit(solution)/shard_map/all_to_all | solution.py:252
  133.3 0.0 copy-done.2
  133.3 4.3 %shard_map.68 = f32[4,6,64,256]{3,2,1,0:T(8,128)} custom-call(f32[16,4,6,8,128]{4,3,2,1,0:T(8,128)S(1)} %all_to_all.10.packed, s32[64,256]{1,0:T(8,128)S(1)} %copy-done.2), custom_call_target="tpu_custom_call" | custom-call | flops 1000000 | bytes 3000000 | tf_op jit(solution)/shard_map/pallas_call | solution.py:255
  (1 shorter events, 0.0 us)
Async XLA Ops:
  0.0 1.4 %copy-start = (f32[4,6,64,256]{3,2,1,0:T(8,128)S(1)}, f32[4,6,64,256]{3,2,1,0:T(8,128)}, u32[]{:S(2)}) copy-start(f32[4,6,64,256]{3,2,1,0:T(8,128)} %state.5) | copy-start | bytes 4718596
  1.4 0.8 copy-start.1
  2.3 16.5 %collective-permute-start = (f32[25,4,256]{2,1,0:T(4,128)S(1)}, f32[25,4,256]{2,1,0:T(4,128)S(1)}, u32[]{:S(2)}, u32[]{:S(2)}) collective-permute-start(f32[25,4,256]{2,1,0:T(4,128)S(1)} %get-tuple-element.7), channel_id=1, source_target_pairs={{0,1},{1,2},{2,3},{3,4},{4,5},{5,6},{6,7},{7,8},{8,9},{9,10},{10,1... | collective-permute-start | bytes 307208 | tf_op jit(solution)/shard_map/ppermute | solution.py:236
  6.2 12.5 %collective-permute-start.1 = (f32[25,4,256]{2,1,0:T(4,128)S(1)}, f32[25,4,256]{2,1,0:T(4,128)S(1)}, u32[]{:S(2)}, u32[]{:S(2)}) collective-permute-start(f32[25,4,256]{2,1,0:T(4,128)S(1)} %get-tuple-element.8), channel_id=1, source_target_pairs={{1,0},{2,1},{3,2},{4,3},{5,4},{6,5},{7,6},{8,7},{9,8},{10,9},{11,1... | collective-permute-start | bytes 307208 | tf_op jit(solution)/shard_map/ppermute | solution.py:237
  23.3 49.9 %copy-start.3 = (s32[1,1,256]{2,1,0:T(1,128)S(1)}, s32[1,1,256]{2,1,0:T(1,128)}, u32[]{:S(2)}) copy-start(s32[1,1,256]{2,1,0:T(1,128)} %param.8) | copy-start | bytes 3076
  23.3 49.9 %copy-start.4 = (f32[1,1,256]{2,1,0:T(1,128)S(1)}, f32[1,1,256]{2,1,0:T(1,128)}, u32[]{:S(2)}) copy-start(f32[1,1,256]{2,1,0:T(1,128)} %param.10) | copy-start | bytes 3076
  23.3 49.9 %copy-start.5 = (f32[1,1,256]{2,1,0:T(1,128)S(1)}, f32[1,1,256]{2,1,0:T(1,128)}, u32[]{:S(2)}) copy-start(f32[1,1,256]{2,1,0:T(1,128)} %param.11) | copy-start | bytes 3076
  23.3 49.8 %all-to-all-start = ((f32[16,4,6,8,128]{4,3,2,1,0:T(8,128)}), f32[16,4,6,8,128]{4,3,2,1,0:T(8,128)S(1)}, u32[]{:S(2)}, u32[]{:S(2)}) async-start(f32[16,4,6,8,128]{4,3,2,1,0:T(8,128)} %shard_map.66), calls=%async_computation | async-start | bytes 3145728 | tf_op jit(solution)/shard_map/all_to_all | solution.py:242
  89.3 44.0 %copy-start.2 = (s32[64,256]{1,0:T(8,128)S(1)}, s32[64,256]{1,0:T(8,128)}, u32[]{:S(2)}) copy-start(s32[64,256]{1,0:T(8,128)} %land.7) | copy-start | bytes 196612

commit v2 on v1

v2 whole, which is shorter than its diff:
```python
import math

import jax
import jax.numpy as jnp
from jax import lax
from jax.experimental import pallas as pl
from jax.experimental.pallas import tpu as pltpu
from jax.sharding import PartitionSpec as P

NS_ITERS = 8
CORIOLIS = 0.1
STRATIFY = 1.5
HALO = 4
SCAN = 8
APPLY = 8
VMEM_LIMIT = 48 * 1024 * 1024


def call(kernel, out_shape, n_in, scratch=(), aliases=None, flops=1000000, nbytes=3000000):
    whole = pl.BlockSpec(memory_space=pltpu.VMEM)
    return pl.pallas_call(
        kernel,
        out_shape=out_shape,
        in_specs=[whole] * n_in,
        out_specs=jax.tree.map(lambda _: whole, out_shape),
        scratch_shapes=list(scratch),
        input_output_aliases=aliases or {},
        compiler_params=pltpu.CompilerParams(vmem_limit_bytes=VMEM_LIMIT),
        cost_estimate=pl.CostEstimate(flops=flops, bytes_accessed=nbytes, transcendentals=0),
    )


def east(field):
    rows = field.shape[0]
    return pltpu.roll(field, rows - 1, 0) - pltpu.roll(field, 1, 0)


def north(field, first, last):
    cols = field.shape[1]
    ahead = jnp.where(last, 0.0, pltpu.roll(field, cols - 1, 1))
    behind = jnp.where(first, 0.0, pltpu.roll(field, 1, 1))
    return ahead - behind


def step(state, mask, first, last):
    u1, v1, h1, u2, v2, h2 = state
    h1 = h1 - 0.125 * (east(u1) + north(v1, first, last))
    h2 = h2 - 0.0625 * (east(u2) + north(v2, first, last))
    p1 = h1 + h2
    p2 = h1 + STRATIFY * h2
    u1n = (u1 + CORIOLIS * v1 - 0.125 * east(p1)) * mask
    v1n = (v1 - CORIOLIS * u1 - 0.125 * north(p1, first, last)) * mask
    u2n = (u2 + CORIOLIS * v2 - 0.125 * east(p2)) * mask
    v2n = (v2 - CORIOLIS * u2 - 0.125 * north(p2, first, last)) * mask
    return (u1n, v1n, h1, u2n, v2n, h2)


def forecast(state, mask):
    lane = lax.broadcasted_iota(jnp.int32, mask.shape, 1)
    first = lane == 0
    last = lane == mask.shape[1] - 1
    for _ in range(2):
        state = step(state, mask, first, last)
    return state


def swap_blocks(groups):
    lane = lax.broadcasted_iota(jnp.int32, (8, 128), 1)
    low = lane < 64
    even = (lane & 32) == 0
    half = [
        (
            jnp.where(low, x[0], pltpu.roll(x[2], 64, 1)),
            jnp.where(low, x[1], pltpu.roll(x[3], 64, 1)),
            jnp.where(low, pltpu.roll(x[0], 64, 1), x[2]),
            jnp.where(low, pltpu.roll(x[1], 64, 1), x[3]),
        )
        for x in groups
    ]
    return [
        (
            jnp.where(even, y[0], pltpu.roll(y[1], 32, 1)),
            jnp.where(even, pltpu.roll(y[0], 96, 1), y[1]),
            jnp.where(even, y[2], pltpu.roll(y[3], 32, 1)),
            jnp.where(even, pltpu.roll(y[2], 96, 1), y[3]),
        )
        for y in half
    ]


BLOCKS = [(f, qx, g) for f in range(6) for qx in range(2) for g in range(2)]


def tile_at(qx, g, a):
    row = qx * 32 + 8 * a
    return slice(row, row + 8), slice(g * 128, g * 128 + 128)


def edges_kernel(top, bottom, land_top, land_bottom, low_out, high_out):
    low_out[24] = land_bottom[8 - HALO :, :].astype(jnp.float32)
    high_out[24] = land_top[:HALO, :].astype(jnp.float32)
    for m in range(4):
        for f in range(6):
            low_out[6 * m + f] = bottom[m, f, 8 - HALO :, :]
            high_out[6 * m + f] = top[m, f, :HALO, :]


def forecast_kernel(state, land, from_low, from_high, packed):
    mask = jnp.concatenate([land[...].astype(jnp.float32), from_high[24], from_low[24]], axis=0)

    def one(m, carry):
        begin = tuple(
            jnp.concatenate([state[m, f], from_high[6 * m + f], from_low[6 * m + f]], axis=0)
            for f in range(6)
        )
        fields = forecast(begin, mask)
        for i in range(0, len(BLOCKS), 12):
            todo = BLOCKS[i : i + 12]
            tiles = swap_blocks([[fields[f][tile_at(qx, g, a)] for a in range(4)] for f, qx, g in todo])
            for (f, qx, g), z in zip(todo, tiles):
                for b in range(4):
                    packed[qx * 8 + g * 4 + b, m, f] = z[b]
        return carry

    lax.fori_loop(0, 4, one, 0)


def analysis_kernel(x_ref, index, count, values, errors, out_ref, dev_ref):
    highest = lax.Precision.HIGHEST
    members = 64
    chosen = index[...]
    entry_row = ((chosen >> 10) << 3) + ((chosen >> 5) & 7)
    entry_lane = (((chosen >> 8) & 3) << 5) + (chosen & 31)
    rows_of = [jnp.broadcast_to(entry_row[:, 128 * i : 128 * i + 128], (members, 128)) for i in range(2)]
    lanes_of = [jnp.broadcast_to(entry_lane[:, 128 * i : 128 * i + 128], (members, 128)) for i in range(2)]

    def scan(block, acc):
        tiles = [x_ref[pl.ds(block * SCAN + i, members, stride=48), :] for i in range(SCAN)]
        for i in range(SCAN):
            acc = tuple(
                jnp.where(
                    rows_of[half] == block * SCAN + i,
                    jnp.take_along_axis(tiles[i], lanes_of[half], axis=1),
                    acc[half],
                )
                for half in range(2)
            )
        return acc

    def split(rows):
        tiles = [x_ref[pl.ds(r, members, stride=48), :] for r in rows]
        for r, x in zip(rows, tiles):
            dev = x - jnp.sum(x, axis=0, keepdims=True) * (1.0 / members)
            high = dev.astype(jnp.bfloat16)
            dev_ref[r, 0:members, :] = high
            dev_ref[r, members:, :] = (dev - high.astype(jnp.float32)).astype(jnp.bfloat16)

    zero = jnp.zeros((members, 128), jnp.float32)
    observed = jnp.concatenate(lax.fori_loop(0, 48 // SCAN, scan, (zero, zero)), axis=1)
    obs_mean = jnp.sum(observed, axis=0, keepdims=True) * (1.0 / members)
    spread = observed - obs_mean
    slots = lax.broadcasted_iota(jnp.int32, (1, 256), 1)
    weight = jnp.where(slots < count[0, 0], 1.0 / errors[...], 0.0)
    innovation = values[...] - obs_mean
    scaled = spread * weight
    eye = (
        lax.broadcasted_iota(jnp.int32, (members, members), 0)
        == lax.broadcasted_iota(jnp.int32, (members, members), 1)
    ).astype(jnp.float32)

    def dot(a, b):
        return jnp.dot(a, b, precision=highest, preferred_element_type=jnp.float32)

    system = (members - 1.0) * eye + lax.dot_general(
        scaled, spread, (((1,), (1,)), ((), ())), precision=highest, preferred_element_type=jnp.float32
    )
    total = jnp.sum(jnp.sum(system * system, axis=1, keepdims=True), axis=0, keepdims=True)
    norm = jnp.sqrt(total)
    root = system / norm
    inverse = eye
    for sweep in range(NS_ITERS):
        split(range(6 * sweep, 6 * sweep + 6))
        factor = 1.5 * eye - 0.5 * (root if sweep == 0 else dot(inverse, root))
        if sweep < NS_ITERS - 1:
            root = dot(root, factor)
        inverse = factor if sweep == 0 else dot(factor, inverse)
    sqrt_inv = inverse / jnp.sqrt(norm)
    moved = jnp.sum(scaled * innovation, axis=1, keepdims=True)
    half = jnp.sum(sqrt_inv * moved, axis=0, keepdims=True)
    mean_weights = jnp.sum(sqrt_inv * half, axis=1, keepdims=True)
    transform = mean_weights + math.sqrt(members - 1.0) * sqrt_inv - eye
    flipped = transform.T
    high = flipped.astype(jnp.bfloat16)
    low = (flipped - high.astype(jnp.float32)).astype(jnp.bfloat16)
    left = jnp.concatenate([high, high, low, low], axis=1)

    def apply(block, carry):
        first = block * (2 * APPLY)
        results = []
        for i in range(APPLY):
            pair = jnp.concatenate([dev_ref[first + 2 * i], dev_ref[first + 2 * i + 1]], axis=1)
            right = jnp.concatenate([pair, pair], axis=0)
            results.append(jnp.dot(left, right, preferred_element_type=jnp.float32))
        for i in range(APPLY):
            for j in range(2):
                out_ref[pl.ds(first + 2 * i + j, members, stride=48), :] = results[i][:, 128 * j : 128 * j + 128]
        return carry

    lax.fori_loop(0, 24 // APPLY, apply, 0)


def unpack_kernel(packed, land, out):
    mask = land[...].astype(jnp.float32)

    def one(m, carry):
        for i in range(0, len(BLOCKS), 12):
            todo = BLOCKS[i : i + 12]
            tiles = swap_blocks([[packed[qx * 8 + g * 4 + b, m, f] for b in range(4)] for f, qx, g in todo])
            for (f, qx, g), z in zip(todo, tiles):
                for a in range(4):
                    rows, cols = tile_at(qx, g, a)
                    out[m, f, rows, cols] = z[a] * mask[rows, cols]
        return carry

    lax.fori_loop(0, 4, one, 0)


def shape(*dims):
    return jax.ShapeDtypeStruct(dims, jnp.float32)


def local(initial_realizations, land_mask, obs_index, obs_count, obs_value, obs_error):
    payload = pl.BlockSpec((25, HALO, 256), lambda i: (0, 0, 0))
    to_high, to_low = pl.pallas_call(
        edges_kernel,
        grid=(1,),
        out_shape=[shape(25, HALO, 256)] * 2,
        in_specs=[
            pl.BlockSpec((4, 6, 8, 256), lambda i: (0, 0, 0, 0)),
            pl.BlockSpec((4, 6, 8, 256), lambda i: (0, 0, 7, 0)),
            pl.BlockSpec((8, 256), lambda i: (0, 0)),
            pl.BlockSpec((8, 256), lambda i: (7, 0)),
        ],
        out_specs=[payload, payload],
        cost_estimate=pl.CostEstimate(flops=100000, bytes_accessed=800000, transcendentals=0),
    )(initial_realizations, initial_realizations, land_mask, land_mask)
    count = lax.axis_size("domain")
    forward = [(i, (i + 1) % count) for i in range(count)]
    backward = [(target, source) for source, target in forward]
    from_low = lax.ppermute(to_high, "domain", forward)
    from_high = lax.ppermute(to_low, "domain", backward)
    packed = call(forecast_kernel, shape(16, 4, 6, 8, 128), 4)(
        initial_realizations, land_mask, from_low, from_high
    )
    grouped = lax.all_to_all(packed, "member", split_axis=0, concat_axis=0, tiled=True)
    whole = pl.BlockSpec(memory_space=pltpu.VMEM)
    increment = pl.pallas_call(
        analysis_kernel,
        out_shape=shape(3072, 128),
        in_specs=[whole, whole, pl.BlockSpec(memory_space=pltpu.SMEM), whole, whole],
        out_specs=whole,
        scratch_shapes=[pltpu.VMEM((48, 128, 128), jnp.bfloat16)],
        compiler_params=pltpu.CompilerParams(vmem_limit_bytes=VMEM_LIMIT),
    )(grouped.reshape(3072, 128), obs_index[0], obs_count, obs_value[0], obs_error[0])
    returned = lax.all_to_all(
        increment.reshape(16, 4, 6, 8, 128), "member", split_axis=0, concat_axis=0, tiled=True
    )
    return call(unpack_kernel, shape(4, 6, 64, 256), 2)(returned, land_mask)


def solution(mesh):
    in_specs = (
        P("member", None, "domain", None),
        P("domain", None),
        P("domain", "member", None),
        P("domain", "member"),
        P("domain", "member", None),
        P("domain", "member", None),
    )
    out_specs = P("member", None, "domain", None)
    return jax.shard_map(local, mesh=mesh, in_specs=in_specs, out_specs=out_specs, check_vma=False)
```

time: 138 us -> 123 us (0.89); the launches traced: 138 us -> 121 us
  Pallas kernels: 31.4 us -> 14.7 us
  local copies, waits for them, and re-layouts: 2.26 us -> 0.02 us
  waiting for transfers between devices: 37.8 us -> 39.8 us
    pallas_call x1, Pallas kernels: 16.1 us -> 6.11 us  [local(): pl.pallas_call(analysis_kernel, out_shape=shape(3072, 128), in_specs=[who...]
    pallas_call x3 -> x2, Pallas kernels: 11 us -> 6.18 us  [the longest x1 4.34 us: local(): call(forecast_kernel, shape(16, 4, 6, 8, 128), 4)]
    unnamed x12 -> x10, local copies, waits for them, and re-layouts: 2.26 us -> 0.02 us
    pallas_call x1, Pallas kernels: 4.34 us -> 2.38 us  [local(): return call(unpack_kernel, shape(4, 6, 64, 256), 2)(returned, land_mask)]
    ppermute x1, waiting for transfers between devices: 0.01 us -> 1.65 us  [local(): from_high = lax.ppermute(to_low, 'domain', backward)]
  transfers between devices with their start and end apart: 3 -> 3, of which waited for: 1 -> 3; matrix products, arithmetic and copies ran while one was open for 0% -> 0% of each run, Pallas kernels for 5% -> 0%
where the time goes in v2:
time: 123 us; the launch traced here: 121 us
  blocking collectives  43.8 us (36%)
  waiting for transfers between devices  39.8 us (32%)
  starting transfers between devices  22 us (18%)
  Pallas kernels  14.7 us (12%)
    all_to_all x1, blocking collectives, local(): lax.all_to_all(increment.reshape(16, 4, 6, 8, 128), 'member', split_axis=...  43.8 us
    all_to_all x1, waiting for transfers between devices, local(): lax.all_to_all(packed, 'member', split_axis=0, concat_axis=0, tiled=True)  37.8 us
    all_to_all x1, starting transfers between devices, local(): lax.all_to_all(packed, 'member', split_axis=0, concat_axis=0, tiled=True)  12 us
    pallas_call x1, Pallas kernels, local(): pl.pallas_call(analysis_kernel, out_shape=shape(3072, 128), in_specs=[who...  6.11 us
    ppermute x1, starting transfers between devices, local(): from_high = lax.ppermute(to_low, 'domain', backward)  6.09 us
    pallas_call x1, Pallas kernels, local(): call(forecast_kernel, shape(16, 4, 6, 8, 128), 4)  4.34 us
    ppermute x1, starting transfers between devices, local(): from_low = lax.ppermute(to_high, 'domain', forward)  3.94 us
  transfers between devices with their start and end apart: 3, of which 3 were waited for; matrix products, arithmetic and copies ran while one was open for 0% of the time, Pallas kernels for 0%

profile of v2, /device:TPU:1, one launch (start us, length us, event | category | flops | bytes accessed | tf_op | source)
XLA Modules:
  0.0 121.0 jit_solution(168837949534522826)
XLA Ops:
  0.0 0.0 copy-start
  0.0 0.0 copy-start.1
  0.0 1.8 %shard_map.64 = (f32[25,4,256]{2,1,0:T(4,128)}, f32[25,4,256]{2,1,0:T(4,128)}) custom-call(f32[4,6,64,256]{3,2,1,0:T(8,128)} %state.1, f32[4,6,64,256]{3,2,1,0:T(8,128)} %state.1, s32[64,256]{1,0:T(8,128)} %land.3, s32[64,256]{1,0:T(8,128)} %land.3), custom_call_target="tpu_custom_call" | custom-call | flops 100000 | bytes 800000 | tf_op jit(solution)/shard_map/pallas_call | solution.py:234
  1.8 3.9 %collective-permute-start = (f32[25,4,256]{2,1,0:T(4,128)}, f32[25,4,256]{2,1,0:T(4,128)S(1)}, u32[]{:S(2)}, u32[]{:S(2)}) collective-permute-start(f32[25,4,256]{2,1,0:T(4,128)} %get-tuple-element.7), channel_id=1, source_target_pairs={{0,1},{1,2},{2,3},{3,4},{4,5},{5,6},{6,7},{7,8},{8,9},{9,10},{10,1... | collective-permute-start | bytes 307208 | tf_op jit(solution)/shard_map/ppermute | solution.py:250
  5.8 6.1 %collective-permute-start.1 = (f32[25,4,256]{2,1,0:T(4,128)}, f32[25,4,256]{2,1,0:T(4,128)S(1)}, u32[]{:S(2)}, u32[]{:S(2)}) collective-permute-start(f32[25,4,256]{2,1,0:T(4,128)} %get-tuple-element.8), channel_id=1, source_target_pairs={{1,0},{2,1},{3,2},{4,3},{5,4},{6,5},{7,6},{8,7},{9,8},{10,9},{11,1... | collective-permute-start | bytes 307208 | tf_op jit(solution)/shard_map/ppermute | solution.py:251
  11.9 0.3 collective-permute-done.from_low
  12.2 1.7 %collective-permute-done.1.from_high = f32[25,4,256]{2,1,0:T(4,128)S(1)} collective-permute-done((f32[25,4,256]{2,1,0:T(4,128)}, f32[25,4,256]{2,1,0:T(4,128)S(1)}, u32[]{:S(2)}, u32[]{:S(2)}) %collective-permute-start.1) | collective-permute-done | bytes 102432 | tf_op jit(solution)/shard_map/ppermute | solution.py:251
  13.9 0.0 copy-done
  13.9 0.0 copy-done.1
  13.9 4.3 %shard_map.65 = f32[16,4,6,8,128]{4,3,2,1,0:T(8,128)} custom-call(f32[4,6,64,256]{3,2,1,0:T(8,128)S(1)} %copy-done, s32[64,256]{1,0:T(8,128)S(1)} %copy-done.1, f32[25,4,256]{2,1,0:T(4,128)S(1)} %collective-permute-done.from_low, f32[25,4,256]{2,1,0:T(4,128)S(1)} %collective-permute-done.1.from_high), custom_call_target="tpu_custom_call" | custom-call | flops 1000000 | bytes 3000000 | tf_op jit(solution)/shard_map/pallas_call | solution.py:252
  18.2 0.0 copy-start.2
  18.2 0.0 copy-start.3
  18.2 0.0 copy-start.4
  18.2 12.0 %all-to-all-start = ((f32[16,4,6,8,128]{4,3,2,1,0:T(8,128)}), f32[16,4,6,8,128]{4,3,2,1,0:T(8,128)S(1)}, u32[]{:S(2)}, u32[]{:S(2)}) async-start(f32[16,4,6,8,128]{4,3,2,1,0:T(8,128)} %shard_map.65), calls=%async_computation | async-start | bytes 3145728 | tf_op jit(solution)/shard_map/all_to_all | solution.py:255
  30.8 37.8 %all-to-all-done = f32[16,4,6,8,128]{4,3,2,1,0:T(8,128)S(1)} async-done(((f32[16,4,6,8,128]{4,3,2,1,0:T(8,128)}), f32[16,4,6,8,128]{4,3,2,1,0:T(8,128)S(1)}, u32[]{:S(2)}, u32[]{:S(2)}) %all-to-all-start) | async-done | bytes 1572896 | tf_op jit(solution)/shard_map/all_to_all | solution.py:255
  68.6 0.0 copy-done.2
  68.6 0.0 copy-done.3
  68.6 0.0 copy-done.4
  68.6 6.1 %shard_map.66 = f32[3072,128]{1,0:T(8,128)S(1)} custom-call(f32[3072,128]{1,0:T(8,128)S(1)} %bitcast.5, s32[1,256]{1,0:T(1,128)S(1)} %bitcast.7, s32[1,1]{1,0:T(1,128)S(6)} %copy.7.count, f32[1,256]{1,0:T(1,128)S(1)} %bitcast.8, f32[1,256]{1,0:T(1,128)S(1)} %bitcast.9), custom_call_target="tpu_custom_call" | custom-call | tf_op jit(solution)/shard_map/pallas_call | solution.py:257
  74.8 43.8 %all_to_all.10.packed = f32[16,4,6,8,128]{4,3,2,1,0:T(8,128)S(1)} all-to-all(f32[16,4,6,8,128]{4,3,2,1,0:T(8,128)S(1)} %bitcast.6), channel_id=1, replica_groups=mesh['member'=16,'domain'=32] {'member'}, dimensions={0} | all-to-all | bytes 3145728 | tf_op jit(solution)/shard_map/all_to_all | solution.py:265
  118.6 2.4 %shard_map.67 = f32[4,6,64,256]{3,2,1,0:T(8,128)} custom-call(f32[16,4,6,8,128]{4,3,2,1,0:T(8,128)S(1)} %all_to_all.10.packed, s32[64,256]{1,0:T(8,128)S(1)} %copy-done.1), custom_call_target="tpu_custom_call" | custom-call | flops 1000000 | bytes 3000000 | tf_op jit(solution)/shard_map/pallas_call | solution.py:268
Async XLA Ops:
  0.0 13.9 %copy-start = (f32[4,6,64,256]{3,2,1,0:T(8,128)S(1)}, f32[4,6,64,256]{3,2,1,0:T(8,128)}, u32[]{:S(2)}) copy-start(f32[4,6,64,256]{3,2,1,0:T(8,128)} %state.1) | copy-start | bytes 4718596
  0.0 13.9 %copy-start.1 = (s32[64,256]{1,0:T(8,128)S(1)}, s32[64,256]{1,0:T(8,128)}, u32[]{:S(2)}) copy-start(s32[64,256]{1,0:T(8,128)} %land.3) | copy-start | bytes 196612
  1.8 10.4 %collective-permute-start = (f32[25,4,256]{2,1,0:T(4,128)}, f32[25,4,256]{2,1,0:T(4,128)S(1)}, u32[]{:S(2)}, u32[]{:S(2)}) collective-permute-start(f32[25,4,256]{2,1,0:T(4,128)} %get-tuple-element.7), channel_id=1, source_target_pairs={{0,1},{1,2},{2,3},{3,4},{4,5},{5,6},{6,7},{7,8},{8,9},{9,10},{10,1... | collective-permute-start | bytes 307208 | tf_op jit(solution)/shard_map/ppermute | solution.py:250
  5.8 8.1 %collective-permute-start.1 = (f32[25,4,256]{2,1,0:T(4,128)}, f32[25,4,256]{2,1,0:T(4,128)S(1)}, u32[]{:S(2)}, u32[]{:S(2)}) collective-permute-start(f32[25,4,256]{2,1,0:T(4,128)} %get-tuple-element.8), channel_id=1, source_target_pairs={{1,0},{2,1},{3,2},{4,3},{5,4},{6,5},{7,6},{8,7},{9,8},{10,9},{11,1... | collective-permute-start | bytes 307208 | tf_op jit(solution)/shard_map/ppermute | solution.py:251
  18.2 50.4 %copy-start.2 = (s32[1,1,256]{2,1,0:T(1,128)S(1)}, s32[1,1,256]{2,1,0:T(1,128)}, u32[]{:S(2)}) copy-start(s32[1,1,256]{2,1,0:T(1,128)} %param.8) | copy-start | bytes 3076
  18.2 50.4 %copy-start.3 = (f32[1,1,256]{2,1,0:T(1,128)S(1)}, f32[1,1,256]{2,1,0:T(1,128)}, u32[]{:S(2)}) copy-start(f32[1,1,256]{2,1,0:T(1,128)} %param.10) | copy-start | bytes 3076
  18.2 50.4 %copy-start.4 = (f32[1,1,256]{2,1,0:T(1,128)S(1)}, f32[1,1,256]{2,1,0:T(1,128)}, u32[]{:S(2)}) copy-start(f32[1,1,256]{2,1,0:T(1,128)} %param.11) | copy-start | bytes 3076
  18.2 50.4 %all-to-all-start = ((f32[16,4,6,8,128]{4,3,2,1,0:T(8,128)}), f32[16,4,6,8,128]{4,3,2,1,0:T(8,128)S(1)}, u32[]{:S(2)}, u32[]{:S(2)}) async-start(f32[16,4,6,8,128]{4,3,2,1,0:T(8,128)} %shard_map.65), calls=%async_computation | async-start | bytes 3145728 | tf_op jit(solution)/shard_map/all_to_all | solution.py:255

commit v3 on v2

v3 whole, which is shorter than its diff:
```python
import math

import jax
import jax.numpy as jnp
from jax import lax
from jax.experimental import pallas as pl
from jax.experimental.pallas import tpu as pltpu
from jax.sharding import PartitionSpec as P

NS_ITERS = 8
CORIOLIS = 0.1
STRATIFY = 1.5
HALO = 4
SCAN = 14
VMEM_LIMIT = 48 * 1024 * 1024
WHOLE_VMEM = 62 * 1024 * 1024


def east(field):
    rows = field.shape[0]
    return pltpu.roll(field, rows - 1, 0) - pltpu.roll(field, 1, 0)


def north(field, first, last):
    cols = field.shape[1]
    ahead = jnp.where(last, 0.0, pltpu.roll(field, cols - 1, 1))
    behind = jnp.where(first, 0.0, pltpu.roll(field, 1, 1))
    return ahead - behind


def step(state, mask, first, last):
    u1, v1, h1, u2, v2, h2 = state
    h1 = h1 - 0.125 * (east(u1) + north(v1, first, last))
    h2 = h2 - 0.0625 * (east(u2) + north(v2, first, last))
    p1 = h1 + h2
    p2 = h1 + STRATIFY * h2
    u1n = (u1 + CORIOLIS * v1 - 0.125 * east(p1)) * mask
    v1n = (v1 - CORIOLIS * u1 - 0.125 * north(p1, first, last)) * mask
    u2n = (u2 + CORIOLIS * v2 - 0.125 * east(p2)) * mask
    v2n = (v2 - CORIOLIS * u2 - 0.125 * north(p2, first, last)) * mask
    return (u1n, v1n, h1, u2n, v2n, h2)


def forecast(state, mask):
    lane = lax.broadcasted_iota(jnp.int32, mask.shape, 1)
    first = lane == 0
    last = lane == mask.shape[1] - 1
    for _ in range(2):
        state = step(state, mask, first, last)
    return state


def swap_blocks(groups):
    lane = lax.broadcasted_iota(jnp.int32, (8, 128), 1)
    low = lane < 64
    even = (lane & 32) == 0
    half = [
        (
            jnp.where(low, x[0], pltpu.roll(x[2], 64, 1)),
            jnp.where(low, x[1], pltpu.roll(x[3], 64, 1)),
            jnp.where(low, pltpu.roll(x[0], 64, 1), x[2]),
            jnp.where(low, pltpu.roll(x[1], 64, 1), x[3]),
        )
        for x in groups
    ]
    return [
        (
            jnp.where(even, y[0], pltpu.roll(y[1], 32, 1)),
            jnp.where(even, pltpu.roll(y[0], 96, 1), y[1]),
            jnp.where(even, y[2], pltpu.roll(y[3], 32, 1)),
            jnp.where(even, pltpu.roll(y[2], 96, 1), y[3]),
        )
        for y in half
    ]


BLOCKS = [(f, qx, g) for f in range(6) for qx in range(2) for g in range(2)]
INNER = 7
INNER_ROWS = 6 * INNER


def edges_kernel(state, land, low_out, high_out, top, bottom, land_top, land_bottom, sems):
    copies = [
        pltpu.make_async_copy(state.at[:, :, 0:8, :], top, sems.at[0]),
        pltpu.make_async_copy(state.at[:, :, 56:64, :], bottom, sems.at[1]),
        pltpu.make_async_copy(land.at[0:8, :], land_top, sems.at[2]),
        pltpu.make_async_copy(land.at[56:64, :], land_bottom, sems.at[3]),
    ]
    for copy in copies:
        copy.start()
    for copy in copies:
        copy.wait()
    low_out[24] = land_bottom[8 - HALO :, :].astype(jnp.float32)
    high_out[24] = land_top[:HALO, :].astype(jnp.float32)
    for m in range(4):
        for f in range(6):
            low_out[6 * m + f] = bottom[m, f, 8 - HALO :, :]
            high_out[6 * m + f] = top[m, f, :HALO, :]


CUTS = (0, 40, 80, 120, 168)


def inner_kernel(state, land, out, begin, land_ref, packed, fields_ref, sems):
    arrive = [pltpu.make_async_copy(land, land_ref, sems.at[0])]
    arrive += [pltpu.make_async_copy(state.at[m], begin.at[m], sems.at[1 + m]) for m in range(4)]
    leave = [
        pltpu.make_async_copy(
            packed.at[:, pl.ds(CUTS[m], CUTS[m + 1] - CUTS[m]), :],
            out.at[:, pl.ds(CUTS[m], CUTS[m + 1] - CUTS[m]), :],
            sems.at[5 + m],
        )
        for m in range(4)
    ]
    for copy in arrive:
        copy.start()
    arrive[0].wait()
    mask = land_ref[...].astype(jnp.float32)
    for m in range(4):
        arrive[1 + m].wait()
        fields = forecast(tuple(begin[m, f] for f in range(6)), mask)
        for f in range(6):
            for g in range(2):
                fields_ref[m % 2, f, g] = fields[f][:, 128 * g : 128 * g + 128]
        for i in range(0, len(BLOCKS), 12):
            todo = BLOCKS[i : i + 12]
            tiles = swap_blocks(
                [
                    [fields_ref[m % 2, f, g, pl.ds((4, 32)[qx] + a, 8, stride=4), :] for a in range(4)]
                    for f, qx, g in todo
                ]
            )
            for (f, qx, g), z in zip(todo, tiles):
                row = m * INNER_ROWS + f * INNER
                for b in range(4):
                    packed[qx * 8 + g * 4 + b, row : row + INNER, :] = z[b][0:INNER]
        leave[m].start()
    for copy in leave:
        copy.wait()


def outer_kernel(state, land, from_low, from_high, packed, fields_ref):
    mask = jnp.concatenate(
        [
            land[0:16, :].astype(jnp.float32),
            land[48:64, :].astype(jnp.float32),
            from_high[24],
            from_low[24],
        ],
        axis=0,
    )

    def one(m, carry):
        begin = tuple(
            jnp.concatenate(
                [state[m, f, 0:16, :], state[m, f, 48:64, :], from_high[6 * m + f], from_low[6 * m + f]],
                axis=0,
            )
            for f in range(6)
        )
        fields = forecast(begin, mask)
        for f in range(6):
            for g in range(2):
                cols = slice(128 * g, 128 * g + 128)
                sides = jnp.concatenate([fields[f][0:4, cols], fields[f][28:32, cols]], axis=0)
                fields_ref[g, pl.ds(pl.multiple_of((6 * m + f) * 8, 8), 8), :] = sides
        return carry

    lax.fori_loop(0, 4, one, 0)
    todo = [(i, qx, g) for i in range(3) for qx in range(2) for g in range(2)]
    tiles = swap_blocks(
        [
            [fields_ref[g, pl.ds(64 * i + 4 * qx + a, 8, stride=8), :] for a in range(4)]
            for i, qx, g in todo
        ]
    )
    for (i, qx, g), z in zip(todo, tiles):
        for b in range(4):
            packed[qx * 8 + g * 4 + b, 8 * i : 8 * i + 8, :] = z[b]


def places(index, members):
    chosen = index[...]
    side = lax.axis_index("member") // 8
    field = chosen >> 10
    group = ((chosen >> 7) + side) & 7
    row = jnp.where(group == 0, INNER_ROWS + field, field * INNER + group - 1)
    lane = chosen & 127
    halves = [slice(0, 128), slice(128, 256)]
    return (
        [jnp.broadcast_to(row[:, half], (members, 128)) for half in halves],
        [jnp.broadcast_to(lane[:, half], (members, 128)) for half in halves],
    )


def pick(tile, r, rows_of, lanes_of, acc):
    return tuple(
        jnp.where(rows_of[half] == r, jnp.take_along_axis(tile, lanes_of[half], axis=1), acc[half])
        for half in range(2)
    )


def split(x):
    members = x.shape[0]
    dev = x - jnp.sum(x, axis=0, keepdims=True) * (1.0 / members)
    high = dev.astype(jnp.bfloat16)
    return high, (dev - high.astype(jnp.float32)).astype(jnp.bfloat16)


def gather_kernel(x_ref, index, observed, dev_ref):
    members = 64
    rows_of, lanes_of = places(index, members)

    def scan(block, acc):
        rows = [block * SCAN + i for i in range(SCAN)]
        tiles = [x_ref[pl.ds(r, members, stride=INNER_ROWS), :] for r in rows]
        for r, tile in zip(rows, tiles):
            acc = pick(tile, r, rows_of, lanes_of, acc)
        for r, tile in zip(rows, tiles):
            high, low = split(tile)
            dev_ref[r, 0:members, :] = high
            dev_ref[r, members:, :] = low
        return acc

    zero = jnp.zeros((members, 128), jnp.float32)
    acc = lax.fori_loop(0, INNER_ROWS // SCAN, scan, (zero, zero))
    observed[:, 0:128] = acc[0]
    observed[:, 128:256] = acc[1]


def analysis_kernel(
    x_ref, picked, dev_ref, index, count, values, errors, out, out_ref, outer_ref, sems
):
    highest = lax.Precision.HIGHEST
    members = 64
    rows_of, lanes_of = places(index, members)
    acc = (picked[:, 0:128], picked[:, 128:256])
    for f in range(6):
        tile = x_ref[pl.ds(f, members, stride=6), :]
        acc = pick(tile, INNER_ROWS + f, rows_of, lanes_of, acc)
        high, low = split(tile)
        outer_ref[f, 0:members, :] = high
        outer_ref[f, members:, :] = low
    observed = jnp.concatenate(acc, axis=1)
    obs_mean = jnp.sum(observed, axis=0, keepdims=True) * (1.0 / members)
    spread = observed - obs_mean
    slots = lax.broadcasted_iota(jnp.int32, (1, 256), 1)
    weight = jnp.where(slots < count[...], 1.0 / errors[...], 0.0)
    innovation = values[...] - obs_mean
    scaled = spread * weight
    eye = (
        lax.broadcasted_iota(jnp.int32, (members, members), 0)
        == lax.broadcasted_iota(jnp.int32, (members, members), 1)
    ).astype(jnp.float32)

    def parts(a):
        high = a.astype(jnp.bfloat16)
        return high, (a - high.astype(jnp.float32)).astype(jnp.bfloat16)

    def times(a, b):
        left = jnp.concatenate(a, axis=1)
        right = jnp.concatenate(b + b, axis=0)
        return jnp.dot(left, right, preferred_element_type=jnp.float32)

    gram = lax.dot_general(
        scaled, spread, (((1,), (1,)), ((), ())), precision=highest, preferred_element_type=jnp.float32
    )
    system = (members - 1.0) * eye + gram
    total = jnp.sum(jnp.sum(system * system, axis=1, keepdims=True), axis=0, keepdims=True)
    norm = jnp.sqrt(total)
    twice = jnp.concatenate([eye, eye], axis=1)
    root = jnp.concatenate([system, system], axis=1) / norm
    inverse = twice
    for sweep in range(NS_ITERS):
        root_parts, inverse_parts = parts(root), parts(inverse)
        factor = 1.5 * twice - 0.5 * (root if sweep == 0 else times(inverse_parts, root_parts))
        factor_parts = parts(factor)
        if sweep < NS_ITERS - 1:
            root = times(root_parts, factor_parts)
        inverse = factor if sweep == 0 else times(factor_parts, inverse_parts)
    sqrt_inv = inverse[:, 0:members] / jnp.sqrt(norm)
    moved = jnp.sum(scaled * innovation, axis=1, keepdims=True)
    half = jnp.sum(sqrt_inv * moved, axis=0, keepdims=True)
    mean_weights = jnp.sum(sqrt_inv * half, axis=1, keepdims=True)
    transform = mean_weights + math.sqrt(members - 1.0) * sqrt_inv - eye
    flipped = transform.T
    high = flipped.astype(jnp.bfloat16)
    low = (flipped - high.astype(jnp.float32)).astype(jnp.bfloat16)
    left = jnp.concatenate([high, high, low, low], axis=1)

    rows_out = out_ref.reshape(members, 48, 128)
    leave = [
        pltpu.make_async_copy(
            rows_out.at[:, pl.ds(16 * i, 16), :], out.at[:, pl.ds(16 * i, 16), :], sems.at[i]
        )
        for i in range(3)
    ]

    def apply(pair_of, places_of):
        results = []
        for pair in pair_of:
            right = jnp.concatenate([pair, pair], axis=0)
            results.append(jnp.dot(left, right, preferred_element_type=jnp.float32))
        for result, rows in zip(results, places_of):
            for j in range(2):
                out_ref[pl.ds(rows[j], members, stride=48), :] = result[:, 128 * j : 128 * j + 128]

    for i in range(3):
        first = 2 * INNER * i
        pairs = [
            jnp.concatenate([dev_ref[first + 2 * k], dev_ref[first + 2 * k + 1]], axis=1)
            for k in range(INNER)
        ]
        pairs.append(jnp.concatenate([outer_ref[2 * i], outer_ref[2 * i + 1]], axis=1))
        spots = [[r + r // INNER + 1 for r in (first + 2 * k, first + 2 * k + 1)] for k in range(INNER)]
        spots.append([16 * i, 16 * i + 8])
        apply(pairs, spots)
        leave[i].start()
    for copy in leave:
        copy.wait()


def unpack_kernel(packed, land, out, field, sems):
    copies = [
        pltpu.make_async_copy(field.at[m, :, g], out.at[m, :, :, pl.ds(128 * g, 128)], sems.at[m, g])
        for m in range(4)
        for g in range(2)
    ]
    masks = {}
    for qx in range(2):
        for g in range(2):
            for a in range(4):
                rows = land[g, pl.ds(32 * qx + a, 8, stride=4), :]
                masks[qx, g, a] = rows
    for m in range(4):
        for i in range(0, len(BLOCKS), 12):
            todo = BLOCKS[i : i + 12]
            tiles = swap_blocks(
                [
                    [
                        packed[qx * 8 + g * 4 + b, 48 * m + 8 * f : 48 * m + 8 * f + 8, :]
                        for b in range(4)
                    ]
                    for f, qx, g in todo
                ]
            )
            for (f, qx, g), z in zip(todo, tiles):
                for a in range(4):
                    tile = pltpu.roll(z[a], 7, 0) if qx else z[a]
                    field[m, f, g, pl.ds(32 * qx + a, 8, stride=4), :] = tile * masks[qx, g, a]
        for g in range(2):
            copies[2 * m + g].start()
    for copy in copies:
        copy.wait()


def shape(*dims):
    return jax.ShapeDtypeStruct(dims, jnp.float32)


def local(initial_realizations, land_mask, obs_index, obs_count, obs_value, obs_error):
    whole = pl.BlockSpec(memory_space=pltpu.VMEM)
    far = pl.BlockSpec(memory_space=pltpu.HBM)
    to_high, to_low = pl.pallas_call(
        edges_kernel,
        out_shape=[shape(25, HALO, 256)] * 2,
        in_specs=[far, far],
        out_specs=[whole, whole],
        scratch_shapes=[
            pltpu.VMEM((4, 6, 8, 256), jnp.float32),
            pltpu.VMEM((4, 6, 8, 256), jnp.float32),
            pltpu.VMEM((8, 256), jnp.int32),
            pltpu.VMEM((8, 256), jnp.int32),
            pltpu.SemaphoreType.DMA((4,)),
        ],
        cost_estimate=pl.CostEstimate(flops=100000, bytes_accessed=800000, transcendentals=0),
    )(initial_realizations, land_mask)
    count = lax.axis_size("domain")
    forward = [(i, (i + 1) % count) for i in range(count)]
    backward = [(target, source) for source, target in forward]
    from_low = lax.ppermute(to_high, "domain", forward)
    from_high = lax.ppermute(to_low, "domain", backward)
    inner = pl.pallas_call(
        inner_kernel,
        out_shape=shape(16, 4 * INNER_ROWS, 128),
        in_specs=[far, far],
        out_specs=far,
        scratch_shapes=[
            pltpu.VMEM((4, 6, 64, 256), jnp.float32),
            pltpu.VMEM((64, 256), jnp.int32),
            pltpu.VMEM((16, 4 * INNER_ROWS, 128), jnp.float32),
            pltpu.VMEM((2, 6, 2, 64, 128), jnp.float32),
            pltpu.SemaphoreType.DMA((9,)),
        ],
        compiler_params=pltpu.CompilerParams(vmem_limit_bytes=WHOLE_VMEM),
        cost_estimate=pl.CostEstimate(flops=20000000, bytes_accessed=3000000, transcendentals=0),
    )(initial_realizations, land_mask)
    outer = pl.pallas_call(
        outer_kernel,
        out_shape=shape(16, 24, 128),
        in_specs=[whole] * 4,
        out_specs=whole,
        scratch_shapes=[pltpu.VMEM((2, 192, 128), jnp.float32)],
        compiler_params=pltpu.CompilerParams(vmem_limit_bytes=VMEM_LIMIT),
        cost_estimate=pl.CostEstimate(flops=10000000, bytes_accessed=3000000, transcendentals=0),
    )(initial_realizations, land_mask, from_low, from_high)
    inner = lax.all_to_all(inner, "member", split_axis=0, concat_axis=0, tiled=True)
    outer = lax.all_to_all(outer, "member", split_axis=0, concat_axis=0, tiled=True)
    observed, deviations = pl.pallas_call(
        gather_kernel,
        out_shape=[shape(64, 256), jax.ShapeDtypeStruct((INNER_ROWS, 128, 128), jnp.bfloat16)],
        in_specs=[whole] * 2,
        out_specs=[whole] * 2,
        compiler_params=pltpu.CompilerParams(vmem_limit_bytes=VMEM_LIMIT),
        cost_estimate=pl.CostEstimate(flops=10000000, bytes_accessed=3000000, transcendentals=0),
    )(inner.reshape(64 * INNER_ROWS, 128), obs_index[0])
    increment = pl.pallas_call(
        analysis_kernel,
        out_shape=shape(64, 48, 128),
        in_specs=[whole] * 7,
        out_specs=far,
        scratch_shapes=[
            pltpu.VMEM((3072, 128), jnp.float32),
            pltpu.VMEM((6, 128, 128), jnp.bfloat16),
            pltpu.SemaphoreType.DMA((3,)),
        ],
        compiler_params=pltpu.CompilerParams(vmem_limit_bytes=VMEM_LIMIT),
        cost_estimate=pl.CostEstimate(flops=60000000, bytes_accessed=3000000, transcendentals=0),
    )(
        outer.reshape(384, 128),
        observed,
        deviations,
        obs_index[0],
        obs_count,
        obs_value[0],
        obs_error[0],
    )
    returned = lax.all_to_all(
        increment.reshape(16, 192, 128), "member", split_axis=0, concat_axis=0, tiled=True
    )
    ocean = land_mask.astype(jnp.float32).reshape(64, 2, 128).transpose(1, 0, 2)
    return pl.pallas_call(
        unpack_kernel,
        out_shape=shape(4, 6, 64, 256),
        in_specs=[whole, whole],
        out_specs=far,
        scratch_shapes=[pltpu.VMEM((4, 6, 2, 64, 128), jnp.float32), pltpu.SemaphoreType.DMA((4, 2))],
        compiler_params=pltpu.CompilerParams(vmem_limit_bytes=VMEM_LIMIT),
    )(returned, ocean)


def solution(mesh):
    in_specs = (
        P("member", None, "domain", None),
        P("domain", None),
        P("domain", "member", None),
        P("domain", "member"),
        P("domain", "member", None),
        P("domain", "member", None),
    )
    out_specs = P("member", None, "domain", None)
    return jax.shard_map(local, mesh=mesh, in_specs=in_specs, out_specs=out_specs, check_vma=False)
```

time: 123 us -> 114 us (0.927); the launches traced: 121 us -> 114 us
  blocking collectives: 43.8 us -> 0 us
  waiting for transfers between devices: 39.8 us -> 67.5 us
  starting transfers between devices: 22 us -> 28.8 us
  Pallas kernels: 14.7 us -> 16.9 us
    all_to_all x1 -> x0, blocking collectives: 43.8 us -> none  [local(): lax.all_to_all(increment.reshape(16, 4, 6, 8, 128), 'member', split_axis=...]
    all_to_all x1 -> x3, waiting for transfers between devices: 37.8 us -> 64.9 us  [the longest x1 37.9 us: local(): lax.all_to_all(increment.reshape(16, 192, 128), 'member', split_axis=0, c...]
    all_to_all x1 -> x3, starting transfers between devices: 12 us -> 19.6 us  [the longest x1 12 us: local(): lax.all_to_all(inner, 'member', split_axis=0, concat_axis=0, tiled=True)]
    pallas_call x4 -> x6, Pallas kernels: 14.7 us -> 16.9 us  [the longest x1 5.07 us: local(): pl.pallas_call(inner_kernel, out_shape=shape(16, 4 * INNER_ROWS, 128), in...]
  transfers between devices with their start and end apart: 3 -> 5, of which waited for: 3 -> 5; matrix products, arithmetic and copies ran while one was open for 0% -> 0% of each run, Pallas kernels for 0% -> 5%
where the time goes in v3:
time: 114 us
  waiting for transfers between devices  67.5 us (59%)
  starting transfers between devices  28.8 us (25%)
  Pallas kernels  16.9 us (15%)
    all_to_all x1, waiting for transfers between devices, local(): lax.all_to_all(increment.reshape(16, 192, 128), 'member', split_axis=0, c...  37.9 us
    all_to_all x1, waiting for transfers between devices, local(): lax.all_to_all(inner, 'member', split_axis=0, concat_axis=0, tiled=True)  18.6 us
    all_to_all x1, starting transfers between devices, local(): lax.all_to_all(inner, 'member', split_axis=0, concat_axis=0, tiled=True)  12 us
    all_to_all x1, waiting for transfers between devices, local(): lax.all_to_all(outer, 'member', split_axis=0, concat_axis=0, tiled=True)  8.46 us
    ppermute x1, starting transfers between devices, local(): from_high = lax.ppermute(to_low, 'domain', backward)  6.09 us
    pallas_call x1, Pallas kernels, local(): pl.pallas_call(inner_kernel, out_shape=shape(16, 4 * INNER_ROWS, 128), in...  5.07 us
    pallas_call x1, Pallas kernels, local(): pl.pallas_call(analysis_kernel, out_shape=shape(64, 48, 128), in_specs=[w...  4.51 us
    all_to_all x1, starting transfers between devices, local(): lax.all_to_all(outer, 'member', split_axis=0, concat_axis=0, tiled=True)  3.98 us
  transfers between devices with their start and end apart: 5, of which 5 were waited for; matrix products, arithmetic and copies ran while one was open for 0% of the time, Pallas kernels for 5%

profile of v3, /device:TPU:1, one launch (start us, length us, event | category | flops | bytes accessed | tf_op | source)
XLA Modules:
  0.0 114.0 jit_solution(16654595673797104004)
XLA Ops:
  0.0 5.1 %shard_map.66 = f32[16,168,128]{2,1,0:T(8,128)} custom-call(f32[4,6,64,256]{3,2,1,0:T(8,128)} %state.5, s32[64,256]{1,0:T(8,128)} %land.5), custom_call_target="tpu_custom_call" | custom-call | flops 20000000 | bytes 3000000 | tf_op jit(solution)/shard_map/pallas_call | solution.py:383
  5.1 0.0 copy-start
  5.1 0.0 copy-start.1
  5.1 12.0 %all-to-all-start.1 = ((f32[16,168,128]{2,1,0:T(8,128)}), f32[16,168,128]{2,1,0:T(8,128)S(1)}, u32[]{:S(2)}, u32[]{:S(2)}) async-start(f32[16,168,128]{2,1,0:T(8,128)} %shard_map.66), calls=%async_computation.1 | async-start | bytes 2752512 | tf_op jit(solution)/shard_map/all_to_all | solution.py:407
  17.1 1.8 %shard_map.64 = (f32[25,4,256]{2,1,0:T(4,128)}, f32[25,4,256]{2,1,0:T(4,128)}) custom-call(f32[4,6,64,256]{3,2,1,0:T(8,128)} %state.5, s32[64,256]{1,0:T(8,128)} %land.5), custom_call_target="tpu_custom_call" | custom-call | flops 100000 | bytes 800000 | tf_op jit(solution)/shard_map/pallas_call | solution.py:364
  18.8 0.0 copy-start.2
  18.9 3.1 %collective-permute-start = (f32[25,4,256]{2,1,0:T(4,128)}, f32[25,4,256]{2,1,0:T(4,128)S(1)}, u32[]{:S(2)}, u32[]{:S(2)}) collective-permute-start(f32[25,4,256]{2,1,0:T(4,128)} %get-tuple-element.9), channel_id=1, source_target_pairs={{0,1},{1,2},{2,3},{3,4},{4,5},{5,6},{6,7},{7,8},{8,9},{9,10},{10,1... | collective-permute-start | bytes 307208 | tf_op jit(solution)/shard_map/ppermute | solution.py:381
  22.0 0.0 copy-start.3
  22.0 0.0 copy-start.4
  22.0 6.1 %collective-permute-start.1 = (f32[25,4,256]{2,1,0:T(4,128)}, f32[25,4,256]{2,1,0:T(4,128)S(1)}, u32[]{:S(2)}, u32[]{:S(2)}) collective-permute-start(f32[25,4,256]{2,1,0:T(4,128)} %get-tuple-element.10), channel_id=1, source_target_pairs={{1,0},{2,1},{3,2},{4,3},{5,4},{6,5},{7,6},{8,7},{9,8},{10,9},{11,1... | collective-permute-start | bytes 307208 | tf_op jit(solution)/shard_map/ppermute | solution.py:382
  28.1 1.4 %collective-permute-done.from_low = f32[25,4,256]{2,1,0:T(4,128)S(1)} collective-permute-done((f32[25,4,256]{2,1,0:T(4,128)}, f32[25,4,256]{2,1,0:T(4,128)S(1)}, u32[]{:S(2)}, u32[]{:S(2)}) %collective-permute-start) | collective-permute-done | bytes 102432 | tf_op jit(solution)/shard_map/ppermute | solution.py:381
  29.5 1.1 %collective-permute-done.1.from_high = f32[25,4,256]{2,1,0:T(4,128)S(1)} collective-permute-done((f32[25,4,256]{2,1,0:T(4,128)}, f32[25,4,256]{2,1,0:T(4,128)S(1)}, u32[]{:S(2)}, u32[]{:S(2)}) %collective-permute-start.1) | collective-permute-done | bytes 102432 | tf_op jit(solution)/shard_map/ppermute | solution.py:382
  30.7 0.0 copy-done
  30.7 0.0 copy-done.1
  30.7 2.4 %shard_map.65 = f32[16,24,128]{2,1,0:T(8,128)} custom-call(f32[4,6,64,256]{3,2,1,0:T(8,128)S(1)} %copy-done, s32[64,256]{1,0:T(8,128)S(1)} %copy-done.1, f32[25,4,256]{2,1,0:T(4,128)S(1)} %collective-permute-done.from_low, f32[25,4,256]{2,1,0:T(4,128)S(1)} %collective-permute-done.1.from_high), custom_call_target="tpu_custom_call" | custom-call | flops 10000000 | bytes 3000000 | tf_op jit(solution)/shard_map/pallas_call | solution.py:398
  33.0 18.6 %all-to-all-done.1 = f32[16,168,128]{2,1,0:T(8,128)S(1)} async-done(((f32[16,168,128]{2,1,0:T(8,128)}), f32[16,168,128]{2,1,0:T(8,128)S(1)}, u32[]{:S(2)}, u32[]{:S(2)}) %all-to-all-start.1) | async-done | bytes 1376288 | tf_op jit(solution)/shard_map/all_to_all | solution.py:407
  51.6 4.0 %all-to-all-start = ((f32[16,24,128]{2,1,0:T(8,128)}), f32[16,24,128]{2,1,0:T(8,128)S(1)}, u32[]{:S(2)}, u32[]{:S(2)}) async-start(f32[16,24,128]{2,1,0:T(8,128)} %shard_map.65), calls=%async_computation | async-start | bytes 393216 | tf_op jit(solution)/shard_map/all_to_all | solution.py:408
  56.2 0.0 copy-done.2
  56.2 1.2 %shard_map.67 = (f32[64,256]{1,0:T(8,128)S(1)}, bf16[42,128,128]{2,1,0:T(8,128)(2,1)S(1)}) custom-call(f32[2688,128]{1,0:T(8,128)S(1)} %bitcast.13, s32[1,256]{1,0:T(1,128)S(1)} %bitcast.15), custom_call_target="tpu_custom_call" | custom-call | flops 10000000 | bytes 3000000 | tf_op jit(solution)/shard_map/pallas_call | solution.py:409
  57.4 8.5 %all-to-all-done = f32[16,24,128]{2,1,0:T(8,128)S(1)} async-done(((f32[16,24,128]{2,1,0:T(8,128)}), f32[16,24,128]{2,1,0:T(8,128)S(1)}, u32[]{:S(2)}, u32[]{:S(2)}) %all-to-all-start) | async-done | bytes 196640 | tf_op jit(solution)/shard_map/all_to_all | solution.py:408
  65.9 0.0 copy-done.3
  65.9 0.0 copy-done.4
  65.9 4.5 %shard_map.68 = f32[64,48,128]{2,1,0:T(8,128)} custom-call(f32[384,128]{1,0:T(8,128)S(1)} %bitcast.14, f32[64,256]{1,0:T(8,128)S(1)} %get-tuple-element.11.picked, bf16[42,128,128]{2,1,0:T(8,128)(2,1)S(1)} %get-tuple-element.12.dev_ref, s32[1,256]{1,0:T(1,128)S(1)} %bitcast.16, s32[1,1]{1,0:T(1,128)S(6)} %copy.10.count, f32[1,256]{1,0:T(1,128)S(1)} %bitcast.17, ...), custom_call_target="tpu_custom_call" | custom-call | flops 60000000 | bytes 3000000 | tf_op jit(solution)/shard_map/pallas_call | solution.py:417
  70.4 3.6 %all-to-all-start.2 = ((f32[16,192,128]{2,1,0:T(8,128)}), f32[16,192,128]{2,1,0:T(8,128)S(1)}, u32[]{:S(2)}, u32[]{:S(2)}) async-start(f32[16,192,128]{2,1,0:T(8,128)} %bitcast.5), calls=%async_computation.2 | async-start | bytes 3145728 | tf_op jit(solution)/shard_map/all_to_all | solution.py:438
  74.0 37.9 %all-to-all-done.2.packed = f32[16,192,128]{2,1,0:T(8,128)S(1)} async-done(((f32[16,192,128]{2,1,0:T(8,128)}), f32[16,192,128]{2,1,0:T(8,128)S(1)}, u32[]{:S(2)}, u32[]{:S(2)}) %all-to-all-start.2) | async-done | bytes 1572896 | tf_op jit(solution)/shard_map/all_to_all | solution.py:438
  112.0 2.0 %shard_map.69 = f32[4,6,64,256]{3,2,1,0:T(8,128)} custom-call(f32[16,192,128]{2,1,0:T(8,128)S(1)} %all-to-all-done.2.packed, f32[2,64,128]{2,1,0:T(8,128)S(1)} %bitcast_bitcast_fusion.land), custom_call_target="tpu_custom_call" | custom-call | tf_op jit(solution)/shard_map/pallas_call | solution.py:442
  (1 shorter events, 0.0 us)
Async XLA Ops:
  5.1 25.6 %copy-start = (f32[4,6,64,256]{3,2,1,0:T(8,128)S(1)}, f32[4,6,64,256]{3,2,1,0:T(8,128)}, u32[]{:S(2)}) copy-start(f32[4,6,64,256]{3,2,1,0:T(8,128)} %state.5) | copy-start | bytes 4718596
  5.1 25.6 %copy-start.1 = (s32[64,256]{1,0:T(8,128)S(1)}, s32[64,256]{1,0:T(8,128)}, u32[]{:S(2)}) copy-start(s32[64,256]{1,0:T(8,128)} %land.5) | copy-start | bytes 196612
  5.1 46.5 %all-to-all-start.1 = ((f32[16,168,128]{2,1,0:T(8,128)}), f32[16,168,128]{2,1,0:T(8,128)S(1)}, u32[]{:S(2)}, u32[]{:S(2)}) async-start(f32[16,168,128]{2,1,0:T(8,128)} %shard_map.66), calls=%async_computation.1 | async-start | bytes 2752512 | tf_op jit(solution)/shard_map/all_to_all | solution.py:407
  18.8 37.4 %copy-start.2 = (s32[1,1,256]{2,1,0:T(1,128)S(1)}, s32[1,1,256]{2,1,0:T(1,128)}, u32[]{:S(2)}) copy-start(s32[1,1,256]{2,1,0:T(1,128)} %param.8) | copy-start | bytes 3076
  18.9 10.7 %collective-permute-start = (f32[25,4,256]{2,1,0:T(4,128)}, f32[25,4,256]{2,1,0:T(4,128)S(1)}, u32[]{:S(2)}, u32[]{:S(2)}) collective-permute-start(f32[25,4,256]{2,1,0:T(4,128)} %get-tuple-element.9), channel_id=1, source_target_pairs={{0,1},{1,2},{2,3},{3,4},{4,5},{5,6},{6,7},{7,8},{8,9},{9,10},{10,1... | collective-permute-start | bytes 307208 | tf_op jit(solution)/shard_map/ppermute | solution.py:381
  22.0 43.9 %copy-start.3 = (f32[1,1,256]{2,1,0:T(1,128)S(1)}, f32[1,1,256]{2,1,0:T(1,128)}, u32[]{:S(2)}) copy-start(f32[1,1,256]{2,1,0:T(1,128)} %param.10) | copy-start | bytes 3076
  22.0 43.9 %copy-start.4 = (f32[1,1,256]{2,1,0:T(1,128)S(1)}, f32[1,1,256]{2,1,0:T(1,128)}, u32[]{:S(2)}) copy-start(f32[1,1,256]{2,1,0:T(1,128)} %param.11) | copy-start | bytes 3076
  22.0 8.6 %collective-permute-start.1 = (f32[25,4,256]{2,1,0:T(4,128)}, f32[25,4,256]{2,1,0:T(4,128)S(1)}, u32[]{:S(2)}, u32[]{:S(2)}) collective-permute-start(f32[25,4,256]{2,1,0:T(4,128)} %get-tuple-element.10), channel_id=1, source_target_pairs={{1,0},{2,1},{3,2},{4,3},{5,4},{6,5},{7,6},{8,7},{9,8},{10,9},{11,1... | collective-permute-start | bytes 307208 | tf_op jit(solution)/shard_map/ppermute | solution.py:382
  51.6 14.3 %all-to-all-start = ((f32[16,24,128]{2,1,0:T(8,128)}), f32[16,24,128]{2,1,0:T(8,128)S(1)}, u32[]{:S(2)}, u32[]{:S(2)}) async-start(f32[16,24,128]{2,1,0:T(8,128)} %shard_map.65), calls=%async_computation | async-start | bytes 393216 | tf_op jit(solution)/shard_map/all_to_all | solution.py:408
  70.4 41.6 %all-to-all-start.2 = ((f32[16,192,128]{2,1,0:T(8,128)}), f32[16,192,128]{2,1,0:T(8,128)S(1)}, u32[]{:S(2)}, u32[]{:S(2)}) async-start(f32[16,192,128]{2,1,0:T(8,128)} %bitcast.5), calls=%async_computation.2 | async-start | bytes 3145728 | tf_op jit(solution)/shard_map/all_to_all | solution.py:438

commit v4 on v3

--- a/solution.py
+++ b/solution.py
@@ -17,61 +17,67 @@
 
 
 def east(field):
-    rows = field.shape[0]
-    return pltpu.roll(field, rows - 1, 0) - pltpu.roll(field, 1, 0)
+    return tuple(pltpu.roll(x, x.shape[0] - 1, 0) - pltpu.roll(x, 1, 0) for x in field)
 
 
 def north(field, first, last):
-    cols = field.shape[1]
-    ahead = jnp.where(last, 0.0, pltpu.roll(field, cols - 1, 1))
-    behind = jnp.where(first, 0.0, pltpu.roll(field, 1, 1))
-    return ahead - behind
+    west, rest = field
+    west_up, rest_up = pltpu.roll(west, 1, 1), pltpu.roll(rest, 1, 1)
+    west_down, rest_down = pltpu.roll(west, 127, 1), pltpu.roll(rest, 127, 1)
+    return (
+        jnp.where(last, rest_down, west_down) - jnp.where(first, 0.0, west_up),
+        jnp.where(last, 0.0, rest_down) - jnp.where(first, west_up, rest_up),
+    )
 
 
 def step(state, mask, first, last):
     u1, v1, h1, u2, v2, h2 = state
-    h1 = h1 - 0.125 * (east(u1) + north(v1, first, last))
-    h2 = h2 - 0.0625 * (east(u2) + north(v2, first, last))
-    p1 = h1 + h2
-    p2 = h1 + STRATIFY * h2
-    u1n = (u1 + CORIOLIS * v1 - 0.125 * east(p1)) * mask
-    v1n = (v1 - CORIOLIS * u1 - 0.125 * north(p1, first, last)) * mask
-    u2n = (u2 + CORIOLIS * v2 - 0.125 * east(p2)) * mask
-    v2n = (v2 - CORIOLIS * u2 - 0.125 * north(p2, first, last)) * mask
-    return (u1n, v1n, h1, u2n, v2n, h2)
+    halves = range(2)
+    du, dv = east(u1), north(v1, first, last)
+    h1 = tuple(h1[i] - 0.125 * (du[i] + dv[i]) for i in halves)
+    du, dv = east(u2), north(v2, first, last)
+    h2 = tuple(h2[i] - 0.0625 * (du[i] + dv[i]) for i in halves)
+
+    def turn(u, v, p):
+        px, py = east(p), north(p, first, last)
+        return (
+            tuple((u[i] + CORIOLIS * v[i] - 0.125 * px[i]) * mask[i] for i in halves),
+            tuple((v[i] - CORIOLIS * u[i] - 0.125 * py[i]) * mask[i] for i in halves),
+        )
+
+    u1, v1 = turn(u1, v1, tuple(h1[i] + h2[i] for i in halves))
+    u2, v2 = turn(u2, v2, tuple(h1[i] + STRATIFY * h2[i] for i in halves))
+    return (u1, v1, h1, u2, v2, h2)
+
+
+def halves_of(x):
+    return (x[..., 0:128], x[..., 128:256])
 
 
 def forecast(state, mask):
-    lane = lax.broadcasted_iota(jnp.int32, mask.shape, 1)
+    lane = lax.broadcasted_iota(jnp.int32, mask.shape[:1] + (128,), 1)
     first = lane == 0
-    last = lane == mask.shape[1] - 1
+    last = lane == 127
+    state = tuple(halves_of(x) for x in state)
+    mask = halves_of(mask)
     for _ in range(2):
         state = step(state, mask, first, last)
     return state
 
 
+def skew(x, odd, high):
+    once = [jnp.where(odd, x[(i + 1) % 4], x[i]) for i in range(4)]
+    return [jnp.where(high, once[(i + 2) % 4], once[i]) for i in range(4)]
+
+
 def swap_blocks(groups):
     lane = lax.broadcasted_iota(jnp.int32, (8, 128), 1)
-    low = lane < 64
-    even = (lane & 32) == 0
-    half = [
-        (
-            jnp.where(low, x[0], pltpu.roll(x[2], 64, 1)),
-            jnp.where(low, x[1], pltpu.roll(x[3], 64, 1)),
-            jnp.where(low, pltpu.roll(x[0], 64, 1), x[2]),
-            jnp.where(low, pltpu.roll(x[1], 64, 1), x[3]),
-        )
-        for x in groups
-    ]
-    return [
-        (
-            jnp.where(even, y[0], pltpu.roll(y[1], 32, 1)),
-            jnp.where(even, pltpu.roll(y[0], 96, 1), y[1]),
-            jnp.where(even, y[2], pltpu.roll(y[3], 32, 1)),
-            jnp.where(even, pltpu.roll(y[2], 96, 1), y[3]),
-        )
-        for y in half
-    ]
+    odd = (lane & 32) != 0
+    high = lane >= 64
+    skewed = [skew(x, odd, high) for x in groups]
+    turned = [[w[0]] + [pltpu.roll(w[d], 32 * d, 1) for d in range(1, 4)] for w in skewed]
+    back = [skew(w, odd, high) for w in turned]
+    return [(w[0], w[3], w[2], w[1]) for w in back]
 
 
 BLOCKS = [(f, qx, g) for f in range(6) for qx in range(2) for g in range(2)]
@@ -121,7 +127,7 @@
         fields = forecast(tuple(begin[m, f] for f in range(6)), mask)
         for f in range(6):
             for g in range(2):
-                fields_ref[m % 2, f, g] = fields[f][:, 128 * g : 128 * g + 128]
+                fields_ref[m % 2, f, g] = fields[f][g]
         for i in range(0, len(BLOCKS), 12):
             todo = BLOCKS[i : i + 12]
             tiles = swap_blocks(
@@ -161,8 +167,7 @@
         fields = forecast(begin, mask)
         for f in range(6):
             for g in range(2):
-                cols = slice(128 * g, 128 * g + 128)
-                sides = jnp.concatenate([fields[f][0:4, cols], fields[f][28:32, cols]], axis=0)
+                sides = jnp.concatenate([fields[f][g][0:4], fields[f][g][28:32]], axis=0)
                 fields_ref[g, pl.ds(pl.multiple_of((6 * m + f) * 8, 8), 8), :] = sides
         return carry
 
@@ -231,7 +236,6 @@
 def analysis_kernel(
     x_ref, picked, dev_ref, index, count, values, errors, out, out_ref, outer_ref, sems
 ):
-    highest = lax.Precision.HIGHEST
     members = 64
     rows_of, lanes_of = places(index, members)
     acc = (picked[:, 0:128], picked[:, 128:256])
@@ -262,9 +266,16 @@
         right = jnp.concatenate(b + b, axis=0)
         return jnp.dot(left, right, preferred_element_type=jnp.float32)
 
-    gram = lax.dot_general(
-        scaled, spread, (((1,), (1,)), ((), ())), precision=highest, preferred_element_type=jnp.float32
-    )
+    scaled_high, scaled_low = parts(scaled)
+    spread_high, spread_low = parts(spread)
+
+    def over_slots(a, b):
+        return lax.dot_general(a, b, (((1,), (1,)), ((), ())), preferred_element_type=jnp.float32)
+
+    gram = over_slots(scaled_high, spread_high) + (
+        over_slots(scaled_high, spread_low) + over_slots(scaled_low, spread_high)
+    )
+    moved = jnp.sum(eye * jnp.sum(scaled * innovation, axis=1, keepdims=True), axis=0, keepdims=True)
     system = (members - 1.0) * eye + gram
     total = jnp.sum(jnp.sum(system * system, axis=1, keepdims=True), axis=0, keepdims=True)
     norm = jnp.sqrt(total)
@@ -279,11 +290,9 @@
             root = times(root_parts, factor_parts)
         inverse = factor if sweep == 0 else times(factor_parts, inverse_parts)
     sqrt_inv = inverse[:, 0:members] / jnp.sqrt(norm)
-    moved = jnp.sum(scaled * innovation, axis=1, keepdims=True)
-    half = jnp.sum(sqrt_inv * moved, axis=0, keepdims=True)
-    mean_weights = jnp.sum(sqrt_inv * half, axis=1, keepdims=True)
-    transform = mean_weights + math.sqrt(members - 1.0) * sqrt_inv - eye
-    flipped = transform.T
+    half = jnp.sum(sqrt_inv * moved, axis=1, keepdims=True)
+    mean_weights = jnp.sum(sqrt_inv * half, axis=0, keepdims=True)
+    flipped = mean_weights + math.sqrt(members - 1.0) * sqrt_inv - eye
     high = flipped.astype(jnp.bfloat16)
     low = (flipped - high.astype(jnp.float32)).astype(jnp.bfloat16)
     left = jnp.concatenate([high, high, low, low], axis=1)

time: 114 us -> 113 us (level)
  Pallas kernels: 16.9 us -> 15.4 us
where the time goes in v4:
time: 113 us
  waiting for transfers between devices  67.6 us (60%)
  starting transfers between devices  28.8 us (25%)
  Pallas kernels  15.4 us (14%)
    all_to_all x1, waiting for transfers between devices, local(): lax.all_to_all(increment.reshape(16, 192, 128), 'member', split_axis=0, c...  38 us
    all_to_all x1, waiting for transfers between devices, local(): lax.all_to_all(inner, 'member', split_axis=0, concat_axis=0, tiled=True)  18.7 us
    all_to_all x1, starting transfers between devices, local(): lax.all_to_all(inner, 'member', split_axis=0, concat_axis=0, tiled=True)  12 us
    all_to_all x1, waiting for transfers between devices, local(): lax.all_to_all(outer, 'member', split_axis=0, concat_axis=0, tiled=True)  8.46 us
    ppermute x1, starting transfers between devices, local(): from_high = lax.ppermute(to_low, 'domain', backward)  6.09 us
    pallas_call x1, Pallas kernels, local(): pl.pallas_call(inner_kernel, out_shape=shape(16, 4 * INNER_ROWS, 128), in...  4.41 us
    pallas_call x1, Pallas kernels, local(): pl.pallas_call(analysis_kernel, out_shape=shape(64, 48, 128), in_specs=[w...  4.39 us
    all_to_all x1, starting transfers between devices, local(): lax.all_to_all(outer, 'member', split_axis=0, concat_axis=0, tiled=True)  3.98 us
  transfers between devices with their start and end apart: 5, of which 5 were waited for; matrix products, arithmetic and copies ran while one was open for 0% of the time, Pallas kernels for 5%

profile of v4, /device:TPU:1, one launch (start us, length us, event | category | flops | bytes accessed | tf_op | source)
XLA Modules:
  0.0 112.7 jit_solution(8332891065025350395)
XLA Ops:
  0.0 4.4 %shard_map.66 = f32[16,168,128]{2,1,0:T(8,128)} custom-call(f32[4,6,64,256]{3,2,1,0:T(8,128)} %state.5, s32[64,256]{1,0:T(8,128)} %land.5), custom_call_target="tpu_custom_call" | custom-call | flops 20000000 | bytes 3000000 | tf_op jit(solution)/shard_map/pallas_call | solution.py:392
  4.4 0.0 copy-start
  4.4 0.0 copy-start.1
  4.4 12.0 %all-to-all-start.1 = ((f32[16,168,128]{2,1,0:T(8,128)}), f32[16,168,128]{2,1,0:T(8,128)S(1)}, u32[]{:S(2)}, u32[]{:S(2)}) async-start(f32[16,168,128]{2,1,0:T(8,128)} %shard_map.66), calls=%async_computation.1 | async-start | bytes 2752512 | tf_op jit(solution)/shard_map/all_to_all | solution.py:416
  16.4 1.8 %shard_map.64 = (f32[25,4,256]{2,1,0:T(4,128)}, f32[25,4,256]{2,1,0:T(4,128)}) custom-call(f32[4,6,64,256]{3,2,1,0:T(8,128)} %state.5, s32[64,256]{1,0:T(8,128)} %land.5), custom_call_target="tpu_custom_call" | custom-call | flops 100000 | bytes 800000 | tf_op jit(solution)/shard_map/pallas_call | solution.py:373
  18.2 0.0 copy-start.2
  18.2 3.1 %collective-permute-start = (f32[25,4,256]{2,1,0:T(4,128)}, f32[25,4,256]{2,1,0:T(4,128)S(1)}, u32[]{:S(2)}, u32[]{:S(2)}) collective-permute-start(f32[25,4,256]{2,1,0:T(4,128)} %get-tuple-element.9), channel_id=1, source_target_pairs={{0,1},{1,2},{2,3},{3,4},{4,5},{5,6},{6,7},{7,8},{8,9},{9,10},{10,1... | collective-permute-start | bytes 307208 | tf_op jit(solution)/shard_map/ppermute | solution.py:390
  21.3 0.0 copy-start.3
  21.4 0.0 copy-start.4
  21.4 6.1 %collective-permute-start.1 = (f32[25,4,256]{2,1,0:T(4,128)}, f32[25,4,256]{2,1,0:T(4,128)S(1)}, u32[]{:S(2)}, u32[]{:S(2)}) collective-permute-start(f32[25,4,256]{2,1,0:T(4,128)} %get-tuple-element.10), channel_id=1, source_target_pairs={{1,0},{2,1},{3,2},{4,3},{5,4},{6,5},{7,6},{8,7},{9,8},{10,9},{11,1... | collective-permute-start | bytes 307208 | tf_op jit(solution)/shard_map/ppermute | solution.py:391
  27.5 1.4 %collective-permute-done.from_low = f32[25,4,256]{2,1,0:T(4,128)S(1)} collective-permute-done((f32[25,4,256]{2,1,0:T(4,128)}, f32[25,4,256]{2,1,0:T(4,128)S(1)}, u32[]{:S(2)}, u32[]{:S(2)}) %collective-permute-start) | collective-permute-done | bytes 102432 | tf_op jit(solution)/shard_map/ppermute | solution.py:390
  28.8 1.1 %collective-permute-done.1.from_high = f32[25,4,256]{2,1,0:T(4,128)S(1)} collective-permute-done((f32[25,4,256]{2,1,0:T(4,128)}, f32[25,4,256]{2,1,0:T(4,128)S(1)}, u32[]{:S(2)}, u32[]{:S(2)}) %collective-permute-start.1) | collective-permute-done | bytes 102432 | tf_op jit(solution)/shard_map/ppermute | solution.py:391
  30.0 0.0 copy-done
  30.0 0.0 copy-done.1
  30.0 2.3 %shard_map.65 = f32[16,24,128]{2,1,0:T(8,128)} custom-call(f32[4,6,64,256]{3,2,1,0:T(8,128)S(1)} %copy-done, s32[64,256]{1,0:T(8,128)S(1)} %copy-done.1, f32[25,4,256]{2,1,0:T(4,128)S(1)} %collective-permute-done.from_low, f32[25,4,256]{2,1,0:T(4,128)S(1)} %collective-permute-done.1.from_high), custom_call_target="tpu_custom_call" | custom-call | flops 10000000 | bytes 3000000 | tf_op jit(solution)/shard_map/pallas_call | solution.py:407
  32.3 18.7 %all-to-all-done.1 = f32[16,168,128]{2,1,0:T(8,128)S(1)} async-done(((f32[16,168,128]{2,1,0:T(8,128)}), f32[16,168,128]{2,1,0:T(8,128)S(1)}, u32[]{:S(2)}, u32[]{:S(2)}) %all-to-all-start.1) | async-done | bytes 1376288 | tf_op jit(solution)/shard_map/all_to_all | solution.py:416
  50.9 4.0 %all-to-all-start = ((f32[16,24,128]{2,1,0:T(8,128)}), f32[16,24,128]{2,1,0:T(8,128)S(1)}, u32[]{:S(2)}, u32[]{:S(2)}) async-start(f32[16,24,128]{2,1,0:T(8,128)} %shard_map.65), calls=%async_computation | async-start | bytes 393216 | tf_op jit(solution)/shard_map/all_to_all | solution.py:417
  55.5 0.0 copy-done.2
  55.6 1.2 %shard_map.67 = (f32[64,256]{1,0:T(8,128)S(1)}, bf16[42,128,128]{2,1,0:T(8,128)(2,1)S(1)}) custom-call(f32[2688,128]{1,0:T(8,128)S(1)} %bitcast.13, s32[1,256]{1,0:T(1,128)S(1)} %bitcast.15), custom_call_target="tpu_custom_call" | custom-call | flops 10000000 | bytes 3000000 | tf_op jit(solution)/shard_map/pallas_call | solution.py:418
  56.8 8.5 %all-to-all-done = f32[16,24,128]{2,1,0:T(8,128)S(1)} async-done(((f32[16,24,128]{2,1,0:T(8,128)}), f32[16,24,128]{2,1,0:T(8,128)S(1)}, u32[]{:S(2)}, u32[]{:S(2)}) %all-to-all-start) | async-done | bytes 196640 | tf_op jit(solution)/shard_map/all_to_all | solution.py:417
  65.2 0.0 copy-done.3
  65.2 0.0 copy-done.4
  65.2 4.4 %shard_map.68 = f32[64,48,128]{2,1,0:T(8,128)} custom-call(f32[384,128]{1,0:T(8,128)S(1)} %bitcast.14, f32[64,256]{1,0:T(8,128)S(1)} %get-tuple-element.11.picked, bf16[42,128,128]{2,1,0:T(8,128)(2,1)S(1)} %get-tuple-element.12.dev_ref, s32[1,256]{1,0:T(1,128)S(1)} %bitcast.16, s32[1,1]{1,0:T(1,128)S(6)} %copy.10.count, f32[1,256]{1,0:T(1,128)S(1)} %bitcast.17, ...), custom_call_target="tpu_custom_call" | custom-call | flops 60000000 | bytes 3000000 | tf_op jit(solution)/shard_map/pallas_call | solution.py:426
  69.6 3.6 %all-to-all-start.2 = ((f32[16,192,128]{2,1,0:T(8,128)}), f32[16,192,128]{2,1,0:T(8,128)S(1)}, u32[]{:S(2)}, u32[]{:S(2)}) async-start(f32[16,192,128]{2,1,0:T(8,128)} %bitcast.5), calls=%async_computation.2 | async-start | bytes 3145728 | tf_op jit(solution)/shard_map/all_to_all | solution.py:447
  73.3 38.0 %all-to-all-done.2.packed = f32[16,192,128]{2,1,0:T(8,128)S(1)} async-done(((f32[16,192,128]{2,1,0:T(8,128)}), f32[16,192,128]{2,1,0:T(8,128)S(1)}, u32[]{:S(2)}, u32[]{:S(2)}) %all-to-all-start.2) | async-done | bytes 1572896 | tf_op jit(solution)/shard_map/all_to_all | solution.py:447
  111.3 1.4 %shard_map.69 = f32[4,6,64,256]{3,2,1,0:T(8,128)} custom-call(f32[16,192,128]{2,1,0:T(8,128)S(1)} %all-to-all-done.2.packed, f32[2,64,128]{2,1,0:T(8,128)S(1)} %bitcast_bitcast_fusion.land), custom_call_target="tpu_custom_call" | custom-call | tf_op jit(solution)/shard_map/pallas_call | solution.py:451
  (1 shorter events, 0.0 us)
Async XLA Ops:
  4.4 25.6 %copy-start = (f32[4,6,64,256]{3,2,1,0:T(8,128)S(1)}, f32[4,6,64,256]{3,2,1,0:T(8,128)}, u32[]{:S(2)}) copy-start(f32[4,6,64,256]{3,2,1,0:T(8,128)} %state.5) | copy-start | bytes 4718596
  4.4 25.6 %copy-start.1 = (s32[64,256]{1,0:T(8,128)S(1)}, s32[64,256]{1,0:T(8,128)}, u32[]{:S(2)}) copy-start(s32[64,256]{1,0:T(8,128)} %land.5) | copy-start | bytes 196612
  4.4 46.5 %all-to-all-start.1 = ((f32[16,168,128]{2,1,0:T(8,128)}), f32[16,168,128]{2,1,0:T(8,128)S(1)}, u32[]{:S(2)}, u32[]{:S(2)}) async-start(f32[16,168,128]{2,1,0:T(8,128)} %shard_map.66), calls=%async_computation.1 | async-start | bytes 2752512 | tf_op jit(solution)/shard_map/all_to_all | solution.py:416
  18.2 37.4 %copy-start.2 = (s32[1,1,256]{2,1,0:T(1,128)S(1)}, s32[1,1,256]{2,1,0:T(1,128)}, u32[]{:S(2)}) copy-start(s32[1,1,256]{2,1,0:T(1,128)} %param.8) | copy-start | bytes 3076
  18.2 10.7 %collective-permute-start = (f32[25,4,256]{2,1,0:T(4,128)}, f32[25,4,256]{2,1,0:T(4,128)S(1)}, u32[]{:S(2)}, u32[]{:S(2)}) collective-permute-start(f32[25,4,256]{2,1,0:T(4,128)} %get-tuple-element.9), channel_id=1, source_target_pairs={{0,1},{1,2},{2,3},{3,4},{4,5},{5,6},{6,7},{7,8},{8,9},{9,10},{10,1... | collective-permute-start | bytes 307208 | tf_op jit(solution)/shard_map/ppermute | solution.py:390
  21.3 43.9 %copy-start.3 = (f32[1,1,256]{2,1,0:T(1,128)S(1)}, f32[1,1,256]{2,1,0:T(1,128)}, u32[]{:S(2)}) copy-start(f32[1,1,256]{2,1,0:T(1,128)} %param.10) | copy-start | bytes 3076
  21.4 43.9 %copy-start.4 = (f32[1,1,256]{2,1,0:T(1,128)S(1)}, f32[1,1,256]{2,1,0:T(1,128)}, u32[]{:S(2)}) copy-start(f32[1,1,256]{2,1,0:T(1,128)} %param.11) | copy-start | bytes 3076
  21.4 8.6 %collective-permute-start.1 = (f32[25,4,256]{2,1,0:T(4,128)}, f32[25,4,256]{2,1,0:T(4,128)S(1)}, u32[]{:S(2)}, u32[]{:S(2)}) collective-permute-start(f32[25,4,256]{2,1,0:T(4,128)} %get-tuple-element.10), channel_id=1, source_target_pairs={{1,0},{2,1},{3,2},{4,3},{5,4},{6,5},{7,6},{8,7},{9,8},{10,9},{11,1... | collective-permute-start | bytes 307208 | tf_op jit(solution)/shard_map/ppermute | solution.py:391
  50.9 14.3 %all-to-all-start = ((f32[16,24,128]{2,1,0:T(8,128)}), f32[16,24,128]{2,1,0:T(8,128)S(1)}, u32[]{:S(2)}, u32[]{:S(2)}) async-start(f32[16,24,128]{2,1,0:T(8,128)} %shard_map.65), calls=%async_computation | async-start | bytes 393216 | tf_op jit(solution)/shard_map/all_to_all | solution.py:417
  69.6 41.6 %all-to-all-start.2 = ((f32[16,192,128]{2,1,0:T(8,128)}), f32[16,192,128]{2,1,0:T(8,128)S(1)}, u32[]{:S(2)}, u32[]{:S(2)}) async-start(f32[16,192,128]{2,1,0:T(8,128)} %bitcast.5), calls=%async_computation.2 | async-start | bytes 3145728 | tf_op jit(solution)/shard_map/all_to_all | solution.py:447

commit v5 on v4

--- a/solution.py
+++ b/solution.py
@@ -122,25 +122,35 @@
         copy.start()
     arrive[0].wait()
     mask = land_ref[...].astype(jnp.float32)
-    for m in range(4):
-        arrive[1 + m].wait()
-        fields = forecast(tuple(begin[m, f] for f in range(6)), mask)
-        for f in range(6):
-            for g in range(2):
-                fields_ref[m % 2, f, g] = fields[f][g]
-        for i in range(0, len(BLOCKS), 12):
-            todo = BLOCKS[i : i + 12]
-            tiles = swap_blocks(
-                [
-                    [fields_ref[m % 2, f, g, pl.ds((4, 32)[qx] + a, 8, stride=4), :] for a in range(4)]
-                    for f, qx, g in todo
-                ]
-            )
-            for (f, qx, g), z in zip(todo, tiles):
-                row = m * INNER_ROWS + f * INNER
-                for b in range(4):
-                    packed[qx * 8 + g * 4 + b, row : row + INNER, :] = z[b][0:INNER]
-        leave[m].start()
+    mask = jnp.concatenate([mask, mask], axis=0)
+    for pair in range(2):
+        members = (2 * pair, 2 * pair + 1)
+        for m in members:
+            arrive[1 + m].wait()
+        fields = forecast(
+            tuple(jnp.concatenate([begin[m, f] for m in members], axis=0) for f in range(6)), mask
+        )
+        for m in members:
+            for f in range(6):
+                for g in range(2):
+                    fields_ref[m % 2, f, g] = fields[f][g][64 * (m % 2) : 64 * (m % 2) + 64]
+        for m in members:
+            for i in range(0, len(BLOCKS), 12):
+                todo = BLOCKS[i : i + 12]
+                tiles = swap_blocks(
+                    [
+                        [
+                            fields_ref[m % 2, f, g, pl.ds((4, 32)[qx] + a, 8, stride=4), :]
+                            for a in range(4)
+                        ]
+                        for f, qx, g in todo
+                    ]
+                )
+                for (f, qx, g), z in zip(todo, tiles):
+                    row = m * INNER_ROWS + f * INNER
+                    for b in range(4):
+                        packed[qx * 8 + g * 4 + b, row : row + INNER, :] = z[b][0:INNER]
+            leave[m].start()
     for copy in leave:
         copy.wait()
 
@@ -252,50 +262,73 @@
     weight = jnp.where(slots < count[...], 1.0 / errors[...], 0.0)
     innovation = values[...] - obs_mean
     scaled = spread * weight
-    eye = (
-        lax.broadcasted_iota(jnp.int32, (members, members), 0)
-        == lax.broadcasted_iota(jnp.int32, (members, members), 1)
-    ).astype(jnp.float32)
-
-    def parts(a):
-        high = a.astype(jnp.bfloat16)
-        return high, (a - high.astype(jnp.float32)).astype(jnp.bfloat16)
+    column = lax.broadcasted_iota(jnp.int32, (members, 2 * members), 1)
+    line = lax.broadcasted_iota(jnp.int32, (members, 2 * members), 0)
+    twice = (line == (column & (members - 1))).astype(jnp.float32)
+    once = (line == column).astype(jnp.float32)
+
+    def parts(a, count=3):
+        found = []
+        for _ in range(count):
+            found.append(a.astype(jnp.bfloat16))
+            a = a - found[-1].astype(jnp.float32)
+        return found
+
+    nothing = jnp.zeros((members, 2 * members), jnp.bfloat16)
 
     def times(a, b):
-        left = jnp.concatenate(a, axis=1)
-        right = jnp.concatenate(b + b, axis=0)
-        return jnp.dot(left, right, preferred_element_type=jnp.float32)
-
-    scaled_high, scaled_low = parts(scaled)
-    spread_high, spread_low = parts(spread)
+        (ah, am, al), (bh, bm, bl) = a, b
+        coarse = jnp.dot(
+            jnp.concatenate([ah, am], axis=1),
+            jnp.concatenate([bh, bm, bh, bm], axis=0),
+            preferred_element_type=jnp.float32,
+        )
+        fine = jnp.dot(
+            jnp.concatenate([al, ah], axis=1),
+            jnp.concatenate([bh, bm, bl, nothing], axis=0),
+            preferred_element_type=jnp.float32,
+        )
+        return coarse + fine
 
     def over_slots(a, b):
-        return lax.dot_general(a, b, (((1,), (1,)), ((), ())), preferred_element_type=jnp.float32)
-
-    gram = over_slots(scaled_high, spread_high) + (
-        over_slots(scaled_high, spread_low) + over_slots(scaled_low, spread_high)
-    )
-    moved = jnp.sum(eye * jnp.sum(scaled * innovation, axis=1, keepdims=True), axis=0, keepdims=True)
-    system = (members - 1.0) * eye + gram
-    total = jnp.sum(jnp.sum(system * system, axis=1, keepdims=True), axis=0, keepdims=True)
-    norm = jnp.sqrt(total)
-    twice = jnp.concatenate([eye, eye], axis=1)
-    root = jnp.concatenate([system, system], axis=1) / norm
-    inverse = twice
-    for sweep in range(NS_ITERS):
+        return lax.dot_general(
+            a,
+            jnp.concatenate([b, b], axis=0),
+            (((1,), (1,)), ((), ())),
+            preferred_element_type=jnp.float32,
+        )
+
+    (ah, am, al), (bh, bm, bl) = parts(scaled), parts(spread)
+    gram = over_slots(ah, bh) + (
+        (over_slots(ah, bm) + over_slots(am, bh))
+        + (over_slots(am, bm) + over_slots(ah, bl) + over_slots(al, bh))
+    )
+    moved = jnp.sum(once * jnp.sum(scaled * innovation, axis=1, keepdims=True), axis=0, keepdims=True)
+    system = (members - 1.0) * twice + gram
+    system_parts = parts(system)
+    square = times(system_parts, system_parts)
+    total = 0.5 * jnp.sum(jnp.sum(system * system, axis=0, keepdims=True), axis=1, keepdims=True)
+    norm_inv = lax.rsqrt(total)
+    norm_inv_root = jnp.sqrt(norm_inv)
+    root = system * norm_inv
+    inverse = 1.5 * twice - 0.5 * root
+    root = 1.5 * root - 0.5 * (square * norm_inv * norm_inv)
+    for sweep in range(1, NS_ITERS):
         root_parts, inverse_parts = parts(root), parts(inverse)
-        factor = 1.5 * twice - 0.5 * (root if sweep == 0 else times(inverse_parts, root_parts))
+        factor = 1.5 * twice - 0.5 * times(inverse_parts, root_parts)
         factor_parts = parts(factor)
         if sweep < NS_ITERS - 1:
             root = times(root_parts, factor_parts)
-        inverse = factor if sweep == 0 else times(factor_parts, inverse_parts)
-    sqrt_inv = inverse[:, 0:members] / jnp.sqrt(norm)
-    half = jnp.sum(sqrt_inv * moved, axis=1, keepdims=True)
-    mean_weights = jnp.sum(sqrt_inv * half, axis=0, keepdims=True)
-    flipped = mean_weights + math.sqrt(members - 1.0) * sqrt_inv - eye
-    high = flipped.astype(jnp.bfloat16)
-    low = (flipped - high.astype(jnp.float32)).astype(jnp.bfloat16)
-    left = jnp.concatenate([high, high, low, low], axis=1)
+            inverse = times(factor_parts, inverse_parts)
+    left_half = (column[0:1] < members).astype(jnp.float32)
+    weights = moved
+    for _ in range(2):
+        step_one = jnp.sum(inverse * weights, axis=1, keepdims=True)
+        weights = jnp.sum(factor * step_one, axis=0, keepdims=True) * left_half
+    weights = weights + pltpu.roll(weights, members, 1)
+    sqrt_inv = times(factor_parts, inverse_parts) * norm_inv_root
+    flipped = weights * norm_inv + math.sqrt(members - 1.0) * sqrt_inv - twice
+    left = jnp.concatenate(parts(flipped, 2), axis=1)
 
     rows_out = out_ref.reshape(members, 48, 128)
     leave = [

time: 113 us -> 113 us (level)
  no operation moved by 1% of the time
where the time goes in v5:
time: 113 us; the launch traced here: 112 us
  waiting for transfers between devices  67.6 us (60%)
  starting transfers between devices  28.8 us (25%)
  Pallas kernels  15.2 us (13%)
    all_to_all x1, waiting for transfers between devices, local(): lax.all_to_all(increment.reshape(16, 192, 128), 'member', split_axis=0, c...  38 us
    all_to_all x1, waiting for transfers between devices, local(): lax.all_to_all(inner, 'member', split_axis=0, concat_axis=0, tiled=True)  18.7 us
    all_to_all x1, starting transfers between devices, local(): lax.all_to_all(inner, 'member', split_axis=0, concat_axis=0, tiled=True)  12 us
    all_to_all x1, waiting for transfers between devices, local(): lax.all_to_all(outer, 'member', split_axis=0, concat_axis=0, tiled=True)  8.46 us
    ppermute x1, starting transfers between devices, local(): from_high = lax.ppermute(to_low, 'domain', backward)  6.09 us
    pallas_call x1, Pallas kernels, local(): pl.pallas_call(analysis_kernel, out_shape=shape(64, 48, 128), in_specs=[w...  4.52 us
    pallas_call x1, Pallas kernels, local(): pl.pallas_call(inner_kernel, out_shape=shape(16, 4 * INNER_ROWS, 128), in...  4.02 us
    all_to_all x1, starting transfers between devices, local(): lax.all_to_all(outer, 'member', split_axis=0, concat_axis=0, tiled=True)  3.98 us
  transfers between devices with their start and end apart: 5, of which 5 were waited for; matrix products, arithmetic and copies ran while one was open for 0% of the time, Pallas kernels for 5%

profile of v5, /device:TPU:1, one launch (start us, length us, event | category | flops | bytes accessed | tf_op | source)
XLA Modules:
  0.0 112.4 jit_solution(7007084541756221256)
XLA Ops:
  0.0 4.0 %shard_map.66 = f32[16,168,128]{2,1,0:T(8,128)} custom-call(f32[4,6,64,256]{3,2,1,0:T(8,128)} %state.5, s32[64,256]{1,0:T(8,128)} %land.5), custom_call_target="tpu_custom_call" | custom-call | flops 20000000 | bytes 3000000 | tf_op jit(solution)/shard_map/pallas_call | solution.py:425
  4.0 0.0 copy-start
  4.0 0.0 copy-start.1
  4.1 12.0 %all-to-all-start.1 = ((f32[16,168,128]{2,1,0:T(8,128)}), f32[16,168,128]{2,1,0:T(8,128)S(1)}, u32[]{:S(2)}, u32[]{:S(2)}) async-start(f32[16,168,128]{2,1,0:T(8,128)} %shard_map.66), calls=%async_computation.1 | async-start | bytes 2752512 | tf_op jit(solution)/shard_map/all_to_all | solution.py:449
  16.0 1.8 %shard_map.64 = (f32[25,4,256]{2,1,0:T(4,128)}, f32[25,4,256]{2,1,0:T(4,128)}) custom-call(f32[4,6,64,256]{3,2,1,0:T(8,128)} %state.5, s32[64,256]{1,0:T(8,128)} %land.5), custom_call_target="tpu_custom_call" | custom-call | flops 100000 | bytes 800000 | tf_op jit(solution)/shard_map/pallas_call | solution.py:406
  17.8 0.0 copy-start.2
  17.8 3.1 %collective-permute-start = (f32[25,4,256]{2,1,0:T(4,128)}, f32[25,4,256]{2,1,0:T(4,128)S(1)}, u32[]{:S(2)}, u32[]{:S(2)}) collective-permute-start(f32[25,4,256]{2,1,0:T(4,128)} %get-tuple-element.9), channel_id=1, source_target_pairs={{0,1},{1,2},{2,3},{3,4},{4,5},{5,6},{6,7},{7,8},{8,9},{9,10},{10,1... | collective-permute-start | bytes 307208 | tf_op jit(solution)/shard_map/ppermute | solution.py:423
  21.0 0.0 copy-start.3
  21.0 0.0 copy-start.4
  21.0 6.1 %collective-permute-start.1 = (f32[25,4,256]{2,1,0:T(4,128)}, f32[25,4,256]{2,1,0:T(4,128)S(1)}, u32[]{:S(2)}, u32[]{:S(2)}) collective-permute-start(f32[25,4,256]{2,1,0:T(4,128)} %get-tuple-element.10), channel_id=1, source_target_pairs={{1,0},{2,1},{3,2},{4,3},{5,4},{6,5},{7,6},{8,7},{9,8},{10,9},{11,1... | collective-permute-start | bytes 307208 | tf_op jit(solution)/shard_map/ppermute | solution.py:424
  27.1 1.4 %collective-permute-done.from_low = f32[25,4,256]{2,1,0:T(4,128)S(1)} collective-permute-done((f32[25,4,256]{2,1,0:T(4,128)}, f32[25,4,256]{2,1,0:T(4,128)S(1)}, u32[]{:S(2)}, u32[]{:S(2)}) %collective-permute-start) | collective-permute-done | bytes 102432 | tf_op jit(solution)/shard_map/ppermute | solution.py:423
  28.5 1.1 %collective-permute-done.1.from_high = f32[25,4,256]{2,1,0:T(4,128)S(1)} collective-permute-done((f32[25,4,256]{2,1,0:T(4,128)}, f32[25,4,256]{2,1,0:T(4,128)S(1)}, u32[]{:S(2)}, u32[]{:S(2)}) %collective-permute-start.1) | collective-permute-done | bytes 102432 | tf_op jit(solution)/shard_map/ppermute | solution.py:424
  29.6 0.0 copy-done
  29.6 0.0 copy-done.1
  29.6 2.3 %shard_map.65 = f32[16,24,128]{2,1,0:T(8,128)} custom-call(f32[4,6,64,256]{3,2,1,0:T(8,128)S(1)} %copy-done, s32[64,256]{1,0:T(8,128)S(1)} %copy-done.1, f32[25,4,256]{2,1,0:T(4,128)S(1)} %collective-permute-done.from_low, f32[25,4,256]{2,1,0:T(4,128)S(1)} %collective-permute-done.1.from_high), custom_call_target="tpu_custom_call" | custom-call | flops 10000000 | bytes 3000000 | tf_op jit(solution)/shard_map/pallas_call | solution.py:440
  31.9 18.7 %all-to-all-done.1 = f32[16,168,128]{2,1,0:T(8,128)S(1)} async-done(((f32[16,168,128]{2,1,0:T(8,128)}), f32[16,168,128]{2,1,0:T(8,128)S(1)}, u32[]{:S(2)}, u32[]{:S(2)}) %all-to-all-start.1) | async-done | bytes 1376288 | tf_op jit(solution)/shard_map/all_to_all | solution.py:449
  50.5 4.0 %all-to-all-start = ((f32[16,24,128]{2,1,0:T(8,128)}), f32[16,24,128]{2,1,0:T(8,128)S(1)}, u32[]{:S(2)}, u32[]{:S(2)}) async-start(f32[16,24,128]{2,1,0:T(8,128)} %shard_map.65), calls=%async_computation | async-start | bytes 393216 | tf_op jit(solution)/shard_map/all_to_all | solution.py:450
  55.2 0.0 copy-done.2
  55.2 1.2 %shard_map.67 = (f32[64,256]{1,0:T(8,128)S(1)}, bf16[42,128,128]{2,1,0:T(8,128)(2,1)S(1)}) custom-call(f32[2688,128]{1,0:T(8,128)S(1)} %bitcast.13, s32[1,256]{1,0:T(1,128)S(1)} %bitcast.15), custom_call_target="tpu_custom_call" | custom-call | flops 10000000 | bytes 3000000 | tf_op jit(solution)/shard_map/pallas_call | solution.py:451
  56.4 8.5 %all-to-all-done = f32[16,24,128]{2,1,0:T(8,128)S(1)} async-done(((f32[16,24,128]{2,1,0:T(8,128)}), f32[16,24,128]{2,1,0:T(8,128)S(1)}, u32[]{:S(2)}, u32[]{:S(2)}) %all-to-all-start) | async-done | bytes 196640 | tf_op jit(solution)/shard_map/all_to_all | solution.py:450
  64.8 0.0 copy-done.3
  64.8 0.0 copy-done.4
  64.8 4.5 %shard_map.68 = f32[64,48,128]{2,1,0:T(8,128)} custom-call(f32[384,128]{1,0:T(8,128)S(1)} %bitcast.14, f32[64,256]{1,0:T(8,128)S(1)} %get-tuple-element.11.picked, bf16[42,128,128]{2,1,0:T(8,128)(2,1)S(1)} %get-tuple-element.12.dev_ref, s32[1,256]{1,0:T(1,128)S(1)} %bitcast.16, s32[1,1]{1,0:T(1,128)S(6)} %copy.10.count, f32[1,256]{1,0:T(1,128)S(1)} %bitcast.17, ...), custom_call_target="tpu_custom_call" | custom-call | flops 60000000 | bytes 3000000 | tf_op jit(solution)/shard_map/pallas_call | solution.py:459
  69.4 3.6 %all-to-all-start.2 = ((f32[16,192,128]{2,1,0:T(8,128)}), f32[16,192,128]{2,1,0:T(8,128)S(1)}, u32[]{:S(2)}, u32[]{:S(2)}) async-start(f32[16,192,128]{2,1,0:T(8,128)} %bitcast.5), calls=%async_computation.2 | async-start | bytes 3145728 | tf_op jit(solution)/shard_map/all_to_all | solution.py:480
  73.0 38.0 %all-to-all-done.2.packed = f32[16,192,128]{2,1,0:T(8,128)S(1)} async-done(((f32[16,192,128]{2,1,0:T(8,128)}), f32[16,192,128]{2,1,0:T(8,128)S(1)}, u32[]{:S(2)}, u32[]{:S(2)}) %all-to-all-start.2) | async-done | bytes 1572896 | tf_op jit(solution)/shard_map/all_to_all | solution.py:480
  111.0 1.4 %shard_map.69 = f32[4,6,64,256]{3,2,1,0:T(8,128)} custom-call(f32[16,192,128]{2,1,0:T(8,128)S(1)} %all-to-all-done.2.packed, f32[2,64,128]{2,1,0:T(8,128)S(1)} %bitcast_bitcast_fusion.land), custom_call_target="tpu_custom_call" | custom-call | tf_op jit(solution)/shard_map/pallas_call | solution.py:484
  (1 shorter events, 0.0 us)
Async XLA Ops:
  4.0 25.6 %copy-start = (f32[4,6,64,256]{3,2,1,0:T(8,128)S(1)}, f32[4,6,64,256]{3,2,1,0:T(8,128)}, u32[]{:S(2)}) copy-start(f32[4,6,64,256]{3,2,1,0:T(8,128)} %state.5) | copy-start | bytes 4718596
  4.0 25.6 %copy-start.1 = (s32[64,256]{1,0:T(8,128)S(1)}, s32[64,256]{1,0:T(8,128)}, u32[]{:S(2)}) copy-start(s32[64,256]{1,0:T(8,128)} %land.5) | copy-start | bytes 196612
  4.1 46.5 %all-to-all-start.1 = ((f32[16,168,128]{2,1,0:T(8,128)}), f32[16,168,128]{2,1,0:T(8,128)S(1)}, u32[]{:S(2)}, u32[]{:S(2)}) async-start(f32[16,168,128]{2,1,0:T(8,128)} %shard_map.66), calls=%async_computation.1 | async-start | bytes 2752512 | tf_op jit(solution)/shard_map/all_to_all | solution.py:449
  17.8 37.4 %copy-start.2 = (s32[1,1,256]{2,1,0:T(1,128)S(1)}, s32[1,1,256]{2,1,0:T(1,128)}, u32[]{:S(2)}) copy-start(s32[1,1,256]{2,1,0:T(1,128)} %param.8) | copy-start | bytes 3076
  17.8 10.7 %collective-permute-start = (f32[25,4,256]{2,1,0:T(4,128)}, f32[25,4,256]{2,1,0:T(4,128)S(1)}, u32[]{:S(2)}, u32[]{:S(2)}) collective-permute-start(f32[25,4,256]{2,1,0:T(4,128)} %get-tuple-element.9), channel_id=1, source_target_pairs={{0,1},{1,2},{2,3},{3,4},{4,5},{5,6},{6,7},{7,8},{8,9},{9,10},{10,1... | collective-permute-start | bytes 307208 | tf_op jit(solution)/shard_map/ppermute | solution.py:423
  21.0 43.9 %copy-start.3 = (f32[1,1,256]{2,1,0:T(1,128)S(1)}, f32[1,1,256]{2,1,0:T(1,128)}, u32[]{:S(2)}) copy-start(f32[1,1,256]{2,1,0:T(1,128)} %param.10) | copy-start | bytes 3076
  21.0 43.9 %copy-start.4 = (f32[1,1,256]{2,1,0:T(1,128)S(1)}, f32[1,1,256]{2,1,0:T(1,128)}, u32[]{:S(2)}) copy-start(f32[1,1,256]{2,1,0:T(1,128)} %param.11) | copy-start | bytes 3076
  21.0 8.6 %collective-permute-start.1 = (f32[25,4,256]{2,1,0:T(4,128)}, f32[25,4,256]{2,1,0:T(4,128)S(1)}, u32[]{:S(2)}, u32[]{:S(2)}) collective-permute-start(f32[25,4,256]{2,1,0:T(4,128)} %get-tuple-element.10), channel_id=1, source_target_pairs={{1,0},{2,1},{3,2},{4,3},{5,4},{6,5},{7,6},{8,7},{9,8},{10,9},{11,1... | collective-permute-start | bytes 307208 | tf_op jit(solution)/shard_map/ppermute | solution.py:424
  50.5 14.3 %all-to-all-start = ((f32[16,24,128]{2,1,0:T(8,128)}), f32[16,24,128]{2,1,0:T(8,128)S(1)}, u32[]{:S(2)}, u32[]{:S(2)}) async-start(f32[16,24,128]{2,1,0:T(8,128)} %shard_map.65), calls=%async_computation | async-start | bytes 393216 | tf_op jit(solution)/shard_map/all_to_all | solution.py:450
  69.4 41.6 %all-to-all-start.2 = ((f32[16,192,128]{2,1,0:T(8,128)}), f32[16,192,128]{2,1,0:T(8,128)S(1)}, u32[]{:S(2)}, u32[]{:S(2)}) async-start(f32[16,192,128]{2,1,0:T(8,128)} %bitcast.5), calls=%async_computation.2 | async-start | bytes 3145728 | tf_op jit(solution)/shard_map/all_to_all | solution.py:480

commit v6 on v5

--- a/solution.py
+++ b/solution.py
@@ -155,7 +155,7 @@
         copy.wait()
 
 
-def outer_kernel(state, land, from_low, from_high, packed, fields_ref):
+def outer_kernel(state, land, from_low, from_high, packed, ocean, fields_ref):
     mask = jnp.concatenate(
         [
             land[0:16, :].astype(jnp.float32),
@@ -182,6 +182,8 @@
         return carry
 
     lax.fori_loop(0, 4, one, 0)
+    for g in range(2):
+        ocean[g] = land[:, 128 * g : 128 * g + 128].astype(jnp.float32)
     todo = [(i, qx, g) for i in range(3) for qx in range(2) for g in range(2)]
     tiles = swap_blocks(
         [
@@ -244,7 +246,7 @@
 
 
 def analysis_kernel(
-    x_ref, picked, dev_ref, index, count, values, errors, out, out_ref, outer_ref, sems
+    x_ref, picked, dev_ref, index, count, values, errors, out_ref, outer_ref
 ):
     members = 64
     rows_of, lanes_of = places(index, members)
@@ -330,14 +332,6 @@
     flipped = weights * norm_inv + math.sqrt(members - 1.0) * sqrt_inv - twice
     left = jnp.concatenate(parts(flipped, 2), axis=1)
 
-    rows_out = out_ref.reshape(members, 48, 128)
-    leave = [
-        pltpu.make_async_copy(
-            rows_out.at[:, pl.ds(16 * i, 16), :], out.at[:, pl.ds(16 * i, 16), :], sems.at[i]
-        )
-        for i in range(3)
-    ]
-
     def apply(pair_of, places_of):
         results = []
         for pair in pair_of:
@@ -357,9 +351,6 @@
         spots = [[r + r // INNER + 1 for r in (first + 2 * k, first + 2 * k + 1)] for k in range(INNER)]
         spots.append([16 * i, 16 * i + 8])
         apply(pairs, spots)
-        leave[i].start()
-    for copy in leave:
-        copy.wait()
 
 
 def unpack_kernel(packed, land, out, field, sems):
@@ -437,11 +428,11 @@
         compiler_params=pltpu.CompilerParams(vmem_limit_bytes=WHOLE_VMEM),
         cost_estimate=pl.CostEstimate(flops=20000000, bytes_accessed=3000000, transcendentals=0),
     )(initial_realizations, land_mask)
-    outer = pl.pallas_call(
+    outer, ocean = pl.pallas_call(
         outer_kernel,
-        out_shape=shape(16, 24, 128),
+        out_shape=[shape(16, 24, 128), shape(2, 64, 128)],
         in_specs=[whole] * 4,
-        out_specs=whole,
+        out_specs=[whole] * 2,
         scratch_shapes=[pltpu.VMEM((2, 192, 128), jnp.float32)],
         compiler_params=pltpu.CompilerParams(vmem_limit_bytes=VMEM_LIMIT),
         cost_estimate=pl.CostEstimate(flops=10000000, bytes_accessed=3000000, transcendentals=0),
@@ -458,14 +449,10 @@
     )(inner.reshape(64 * INNER_ROWS, 128), obs_index[0])
     increment = pl.pallas_call(
         analysis_kernel,
-        out_shape=shape(64, 48, 128),
+        out_shape=shape(3072, 128),
         in_specs=[whole] * 7,
-        out_specs=far,
-        scratch_shapes=[
-            pltpu.VMEM((3072, 128), jnp.float32),
-            pltpu.VMEM((6, 128, 128), jnp.bfloat16),
-            pltpu.SemaphoreType.DMA((3,)),
-        ],
+        out_specs=whole,
+        scratch_shapes=[pltpu.VMEM((6, 128, 128), jnp.bfloat16)],
         compiler_params=pltpu.CompilerParams(vmem_limit_bytes=VMEM_LIMIT),
         cost_estimate=pl.CostEstimate(flops=60000000, bytes_accessed=3000000, transcendentals=0),
     )(
@@ -480,7 +467,6 @@
     returned = lax.all_to_all(
         increment.reshape(16, 192, 128), "member", split_axis=0, concat_axis=0, tiled=True
     )
-    ocean = land_mask.astype(jnp.float32).reshape(64, 2, 128).transpose(1, 0, 2)
     return pl.pallas_call(
         unpack_kernel,
         out_shape=shape(4, 6, 64, 256),

time: 113 us -> 113 us (level)
  blocking collectives: 0 us -> 42.5 us
  waiting for transfers between devices: 67.6 us -> 29.7 us
  starting transfers between devices: 28.8 us -> 25.2 us
    all_to_all x0 -> x1, blocking collectives: none -> 42.5 us  [local(): lax.all_to_all(increment.reshape(16, 192, 128), 'member', split_axis=0, c...]
    all_to_all x1 -> x0, waiting for transfers between devices: 38 us -> none  [local(): lax.all_to_all(increment.reshape(16, 192, 128), 'member', split_axis=0, c...]
    all_to_all x1 -> x0, starting transfers between devices: 3.62 us -> none  [local(): lax.all_to_all(increment.reshape(16, 192, 128), 'member', split_axis=0, c...]
  transfers between devices with their start and end apart: 5 -> 4, of which waited for: 5 -> 4; matrix products, arithmetic and copies ran while one was open for 0% -> 0% of each run, Pallas kernels for 5% -> 5%
where the time goes in v6:
time: 113 us; the launch traced here: 112 us
  blocking collectives  42.5 us (38%)
  waiting for transfers between devices  29.7 us (26%)
  starting transfers between devices  25.2 us (22%)
  Pallas kernels  14.3 us (13%)
    all_to_all x1, blocking collectives, local(): lax.all_to_all(increment.reshape(16, 192, 128), 'member', split_axis=0, c...  42.5 us
    all_to_all x1, waiting for transfers between devices, local(): lax.all_to_all(inner, 'member', split_axis=0, concat_axis=0, tiled=True)  18.7 us
    all_to_all x1, starting transfers between devices, local(): lax.all_to_all(inner, 'member', split_axis=0, concat_axis=0, tiled=True)  12 us
    all_to_all x1, waiting for transfers between devices, local(): lax.all_to_all(outer, 'member', split_axis=0, concat_axis=0, tiled=True)  8.46 us
    ppermute x1, starting transfers between devices, local(): from_high = lax.ppermute(to_low, 'domain', backward)  6.09 us
    pallas_call x1, Pallas kernels, local(): pl.pallas_call(inner_kernel, out_shape=shape(16, 4 * INNER_ROWS, 128), in...  4.02 us
    all_to_all x1, starting transfers between devices, local(): lax.all_to_all(outer, 'member', split_axis=0, concat_axis=0, tiled=True)  3.98 us
    pallas_call x1, Pallas kernels, local(): pl.pallas_call(analysis_kernel, out_shape=shape(3072, 128), in_specs=[who...  3.7 us
  transfers between devices with their start and end apart: 4, of which 4 were waited for; matrix products, arithmetic and copies ran while one was open for 0% of the time, Pallas kernels for 5%

profile of v6, /device:TPU:1, one launch (start us, length us, event | category | flops | bytes accessed | tf_op | source)
XLA Modules:
  0.0 112.4 jit_solution(14121551034861290092)
XLA Ops:
  0.0 4.0 %shard_map.66 = f32[16,168,128]{2,1,0:T(8,128)} custom-call(f32[4,6,64,256]{3,2,1,0:T(8,128)} %state.5, s32[64,256]{1,0:T(8,128)} %land.5), custom_call_target="tpu_custom_call" | custom-call | flops 20000000 | bytes 3000000 | tf_op jit(solution)/shard_map/pallas_call | solution.py:416
  4.0 0.0 copy-start
  4.0 0.0 copy-start.1
  4.1 12.0 %all-to-all-start.1 = ((f32[16,168,128]{2,1,0:T(8,128)}), f32[16,168,128]{2,1,0:T(8,128)S(1)}, u32[]{:S(2)}, u32[]{:S(2)}) async-start(f32[16,168,128]{2,1,0:T(8,128)} %shard_map.66), calls=%async_computation.1 | async-start | bytes 2752512 | tf_op jit(solution)/shard_map/all_to_all | solution.py:440
  16.0 0.0 copy-start.2
  16.0 1.8 %shard_map.64 = (f32[25,4,256]{2,1,0:T(4,128)}, f32[25,4,256]{2,1,0:T(4,128)}) custom-call(f32[4,6,64,256]{3,2,1,0:T(8,128)} %state.5, s32[64,256]{1,0:T(8,128)} %land.5), custom_call_target="tpu_custom_call" | custom-call | flops 100000 | bytes 800000 | tf_op jit(solution)/shard_map/pallas_call | solution.py:397
  17.8 3.1 %collective-permute-start = (f32[25,4,256]{2,1,0:T(4,128)}, f32[25,4,256]{2,1,0:T(4,128)S(1)}, u32[]{:S(2)}, u32[]{:S(2)}) collective-permute-start(f32[25,4,256]{2,1,0:T(4,128)} %get-tuple-element.11), channel_id=1, source_target_pairs={{0,1},{1,2},{2,3},{3,4},{4,5},{5,6},{6,7},{7,8},{8,9},{9,10},{10,1... | collective-permute-start | bytes 307208 | tf_op jit(solution)/shard_map/ppermute | solution.py:414
  21.0 0.0 copy-start.3
  21.0 0.0 copy-start.4
  21.0 6.1 %collective-permute-start.1 = (f32[25,4,256]{2,1,0:T(4,128)}, f32[25,4,256]{2,1,0:T(4,128)S(1)}, u32[]{:S(2)}, u32[]{:S(2)}) collective-permute-start(f32[25,4,256]{2,1,0:T(4,128)} %get-tuple-element.12), channel_id=1, source_target_pairs={{1,0},{2,1},{3,2},{4,3},{5,4},{6,5},{7,6},{8,7},{9,8},{10,9},{11,1... | collective-permute-start | bytes 307208 | tf_op jit(solution)/shard_map/ppermute | solution.py:415
  27.1 1.4 %collective-permute-done.from_low = f32[25,4,256]{2,1,0:T(4,128)S(1)} collective-permute-done((f32[25,4,256]{2,1,0:T(4,128)}, f32[25,4,256]{2,1,0:T(4,128)S(1)}, u32[]{:S(2)}, u32[]{:S(2)}) %collective-permute-start) | collective-permute-done | bytes 102432 | tf_op jit(solution)/shard_map/ppermute | solution.py:414
  28.5 1.1 %collective-permute-done.1.from_high = f32[25,4,256]{2,1,0:T(4,128)S(1)} collective-permute-done((f32[25,4,256]{2,1,0:T(4,128)}, f32[25,4,256]{2,1,0:T(4,128)S(1)}, u32[]{:S(2)}, u32[]{:S(2)}) %collective-permute-start.1) | collective-permute-done | bytes 102432 | tf_op jit(solution)/shard_map/ppermute | solution.py:415
  29.6 0.0 copy-done
  29.6 0.0 copy-done.1
  29.6 2.3 %shard_map.65 = (f32[16,24,128]{2,1,0:T(8,128)}, f32[2,64,128]{2,1,0:T(8,128)S(1)}) custom-call(f32[4,6,64,256]{3,2,1,0:T(8,128)S(1)} %copy-done, s32[64,256]{1,0:T(8,128)S(1)} %copy-done.1, f32[25,4,256]{2,1,0:T(4,128)S(1)} %collective-permute-done.from_low, f32[25,4,256]{2,1,0:T(4,128)S(1)} %collective-permute-done.1.from_high), custom_call_target="tpu_custom_call" | custom-call | flops 10000000 | bytes 3000000 | tf_op jit(solution)/shard_map/pallas_call | solution.py:431
  31.9 18.7 %all-to-all-done.1 = f32[16,168,128]{2,1,0:T(8,128)S(1)} async-done(((f32[16,168,128]{2,1,0:T(8,128)}), f32[16,168,128]{2,1,0:T(8,128)S(1)}, u32[]{:S(2)}, u32[]{:S(2)}) %all-to-all-start.1) | async-done | bytes 1376288 | tf_op jit(solution)/shard_map/all_to_all | solution.py:440
  50.5 4.0 %all-to-all-start = ((f32[16,24,128]{2,1,0:T(8,128)}), f32[16,24,128]{2,1,0:T(8,128)S(1)}, u32[]{:S(2)}, u32[]{:S(2)}) async-start(f32[16,24,128]{2,1,0:T(8,128)} %get-tuple-element.13), calls=%async_computation | async-start | bytes 393216 | tf_op jit(solution)/shard_map/all_to_all | solution.py:441
  55.2 0.0 copy-done.2
  55.2 1.2 %shard_map.67 = (f32[64,256]{1,0:T(8,128)S(1)}, bf16[42,128,128]{2,1,0:T(8,128)(2,1)S(1)}) custom-call(f32[2688,128]{1,0:T(8,128)S(1)} %bitcast.7, s32[1,256]{1,0:T(1,128)S(1)} %bitcast.9), custom_call_target="tpu_custom_call" | custom-call | flops 10000000 | bytes 3000000 | tf_op jit(solution)/shard_map/pallas_call | solution.py:442
  56.4 8.5 %all-to-all-done = f32[16,24,128]{2,1,0:T(8,128)S(1)} async-done(((f32[16,24,128]{2,1,0:T(8,128)}), f32[16,24,128]{2,1,0:T(8,128)S(1)}, u32[]{:S(2)}, u32[]{:S(2)}) %all-to-all-start) | async-done | bytes 196640 | tf_op jit(solution)/shard_map/all_to_all | solution.py:441
  64.8 0.0 copy-done.3
  64.8 0.0 copy-done.4
  64.8 3.7 %shard_map.68 = f32[3072,128]{1,0:T(8,128)S(1)} custom-call(f32[384,128]{1,0:T(8,128)S(1)} %bitcast.8, f32[64,256]{1,0:T(8,128)S(1)} %get-tuple-element.14.picked, bf16[42,128,128]{2,1,0:T(8,128)(2,1)S(1)} %get-tuple-element.15.dev_ref, s32[1,256]{1,0:T(1,128)S(1)} %bitcast.10, s32[1,1]{1,0:T(1,128)S(6)} %copy.7.count, f32[1,256]{1,0:T(1,128)S(1)} %bitcast.11, ...), custom_call_target="tpu_custom_call" | custom-call | flops 60000000 | bytes 3000000 | tf_op jit(solution)/shard_map/pallas_call | solution.py:450
  68.6 42.5 %all_to_all.15.packed = f32[16,192,128]{2,1,0:T(8,128)S(1)} all-to-all(f32[16,192,128]{2,1,0:T(8,128)S(1)} %bitcast.6), channel_id=1, replica_groups=mesh['member'=16,'domain'=32] {'member'}, dimensions={0} | all-to-all | bytes 3145728 | tf_op jit(solution)/shard_map/all_to_all | solution.py:467
  111.0 1.4 %shard_map.69 = f32[4,6,64,256]{3,2,1,0:T(8,128)} custom-call(f32[16,192,128]{2,1,0:T(8,128)S(1)} %all_to_all.15.packed, f32[2,64,128]{2,1,0:T(8,128)S(1)} %get-tuple-element.16.land), custom_call_target="tpu_custom_call" | custom-call | tf_op jit(solution)/shard_map/pallas_call | solution.py:470
Async XLA Ops:
  4.0 25.6 %copy-start = (f32[4,6,64,256]{3,2,1,0:T(8,128)S(1)}, f32[4,6,64,256]{3,2,1,0:T(8,128)}, u32[]{:S(2)}) copy-start(f32[4,6,64,256]{3,2,1,0:T(8,128)} %state.5) | copy-start | bytes 4718596
  4.0 25.6 %copy-start.1 = (s32[64,256]{1,0:T(8,128)S(1)}, s32[64,256]{1,0:T(8,128)}, u32[]{:S(2)}) copy-start(s32[64,256]{1,0:T(8,128)} %land.5) | copy-start | bytes 196612
  4.1 46.5 %all-to-all-start.1 = ((f32[16,168,128]{2,1,0:T(8,128)}), f32[16,168,128]{2,1,0:T(8,128)S(1)}, u32[]{:S(2)}, u32[]{:S(2)}) async-start(f32[16,168,128]{2,1,0:T(8,128)} %shard_map.66), calls=%async_computation.1 | async-start | bytes 2752512 | tf_op jit(solution)/shard_map/all_to_all | solution.py:440
  16.0 39.1 %copy-start.2 = (s32[1,1,256]{2,1,0:T(1,128)S(1)}, s32[1,1,256]{2,1,0:T(1,128)}, u32[]{:S(2)}) copy-start(s32[1,1,256]{2,1,0:T(1,128)} %param.8) | copy-start | bytes 3076
  17.8 10.7 %collective-permute-start = (f32[25,4,256]{2,1,0:T(4,128)}, f32[25,4,256]{2,1,0:T(4,128)S(1)}, u32[]{:S(2)}, u32[]{:S(2)}) collective-permute-start(f32[25,4,256]{2,1,0:T(4,128)} %get-tuple-element.11), channel_id=1, source_target_pairs={{0,1},{1,2},{2,3},{3,4},{4,5},{5,6},{6,7},{7,8},{8,9},{9,10},{10,1... | collective-permute-start | bytes 307208 | tf_op jit(solution)/shard_map/ppermute | solution.py:414
  21.0 43.9 %copy-start.3 = (f32[1,1,256]{2,1,0:T(1,128)S(1)}, f32[1,1,256]{2,1,0:T(1,128)}, u32[]{:S(2)}) copy-start(f32[1,1,256]{2,1,0:T(1,128)} %param.10) | copy-start | bytes 3076
  21.0 43.9 %copy-start.4 = (f32[1,1,256]{2,1,0:T(1,128)S(1)}, f32[1,1,256]{2,1,0:T(1,128)}, u32[]{:S(2)}) copy-start(f32[1,1,256]{2,1,0:T(1,128)} %param.11) | copy-start | bytes 3076
  21.0 8.6 %collective-permute-start.1 = (f32[25,4,256]{2,1,0:T(4,128)}, f32[25,4,256]{2,1,0:T(4,128)S(1)}, u32[]{:S(2)}, u32[]{:S(2)}) collective-permute-start(f32[25,4,256]{2,1,0:T(4,128)} %get-tuple-element.12), channel_id=1, source_target_pairs={{1,0},{2,1},{3,2},{4,3},{5,4},{6,5},{7,6},{8,7},{9,8},{10,9},{11,1... | collective-permute-start | bytes 307208 | tf_op jit(solution)/shard_map/ppermute | solution.py:415
  50.5 14.3 %all-to-all-start = ((f32[16,24,128]{2,1,0:T(8,128)}), f32[16,24,128]{2,1,0:T(8,128)S(1)}, u32[]{:S(2)}, u32[]{:S(2)}) async-start(f32[16,24,128]{2,1,0:T(8,128)} %get-tuple-element.13), calls=%async_computation | async-start | bytes 393216 | tf_op jit(solution)/shard_map/all_to_all | solution.py:441

commit v7 on v6

--- a/solution.py
+++ b/solution.py
@@ -330,13 +330,13 @@
     weights = weights + pltpu.roll(weights, members, 1)
     sqrt_inv = times(factor_parts, inverse_parts) * norm_inv_root
     flipped = weights * norm_inv + math.sqrt(members - 1.0) * sqrt_inv - twice
-    left = jnp.concatenate(parts(flipped, 2), axis=1)
+    left = jnp.concatenate(parts(flipped, 2), axis=0)
 
     def apply(pair_of, places_of):
         results = []
         for pair in pair_of:
-            right = jnp.concatenate([pair, pair], axis=0)
-            results.append(jnp.dot(left, right, preferred_element_type=jnp.float32))
+            both = jnp.dot(left, pair, preferred_element_type=jnp.float32)
+            results.append(both[0:members] + both[members:])
         for result, rows in zip(results, places_of):
             for j in range(2):
                 out_ref[pl.ds(rows[j], members, stride=48), :] = result[:, 128 * j : 128 * j + 128]

time: 113 us -> 113 us (level)
  no operation moved by 1% of the time
where the time goes in v7:
time: 113 us; the launch traced here: 112 us
  blocking collectives  42.5 us (38%)
  waiting for transfers between devices  29.7 us (26%)
  starting transfers between devices  25.2 us (22%)
  Pallas kernels  14.3 us (13%)
    all_to_all x1, blocking collectives, local(): lax.all_to_all(increment.reshape(16, 192, 128), 'member', split_axis=0, c...  42.5 us
    all_to_all x1, waiting for transfers between devices, local(): lax.all_to_all(inner, 'member', split_axis=0, concat_axis=0, tiled=True)  18.7 us
    all_to_all x1, starting transfers between devices, local(): lax.all_to_all(inner, 'member', split_axis=0, concat_axis=0, tiled=True)  12 us
    all_to_all x1, waiting for transfers between devices, local(): lax.all_to_all(outer, 'member', split_axis=0, concat_axis=0, tiled=True)  8.46 us
    ppermute x1, starting transfers between devices, local(): from_high = lax.ppermute(to_low, 'domain', backward)  6.09 us
    pallas_call x1, Pallas kernels, local(): pl.pallas_call(inner_kernel, out_shape=shape(16, 4 * INNER_ROWS, 128), in...  4.02 us
    all_to_all x1, starting transfers between devices, local(): lax.all_to_all(outer, 'member', split_axis=0, concat_axis=0, tiled=True)  3.98 us
    pallas_call x1, Pallas kernels, local(): pl.pallas_call(analysis_kernel, out_shape=shape(3072, 128), in_specs=[who...  3.62 us
  transfers between devices with their start and end apart: 4, of which 4 were waited for; matrix products, arithmetic and copies ran while one was open for 0% of the time, Pallas kernels for 5%

profile of v7, /device:TPU:1, one launch (start us, length us, event | category | flops | bytes accessed | tf_op | source)
XLA Modules:
  0.0 112.3 jit_solution(15194268516686879540)
XLA Ops:
  0.0 4.0 %shard_map.66 = f32[16,168,128]{2,1,0:T(8,128)} custom-call(f32[4,6,64,256]{3,2,1,0:T(8,128)} %state.5, s32[64,256]{1,0:T(8,128)} %land.5), custom_call_target="tpu_custom_call" | custom-call | flops 20000000 | bytes 3000000 | tf_op jit(solution)/shard_map/pallas_call | solution.py:416
  4.0 0.0 copy-start
  4.0 0.0 copy-start.1
  4.1 12.0 %all-to-all-start.1 = ((f32[16,168,128]{2,1,0:T(8,128)}), f32[16,168,128]{2,1,0:T(8,128)S(1)}, u32[]{:S(2)}, u32[]{:S(2)}) async-start(f32[16,168,128]{2,1,0:T(8,128)} %shard_map.66), calls=%async_computation.1 | async-start | bytes 2752512 | tf_op jit(solution)/shard_map/all_to_all | solution.py:440
  16.0 0.0 copy-start.2
  16.0 1.8 %shard_map.64 = (f32[25,4,256]{2,1,0:T(4,128)}, f32[25,4,256]{2,1,0:T(4,128)}) custom-call(f32[4,6,64,256]{3,2,1,0:T(8,128)} %state.5, s32[64,256]{1,0:T(8,128)} %land.5), custom_call_target="tpu_custom_call" | custom-call | flops 100000 | bytes 800000 | tf_op jit(solution)/shard_map/pallas_call | solution.py:397
  17.8 3.1 %collective-permute-start = (f32[25,4,256]{2,1,0:T(4,128)}, f32[25,4,256]{2,1,0:T(4,128)S(1)}, u32[]{:S(2)}, u32[]{:S(2)}) collective-permute-start(f32[25,4,256]{2,1,0:T(4,128)} %get-tuple-element.11), channel_id=1, source_target_pairs={{0,1},{1,2},{2,3},{3,4},{4,5},{5,6},{6,7},{7,8},{8,9},{9,10},{10,1... | collective-permute-start | bytes 307208 | tf_op jit(solution)/shard_map/ppermute | solution.py:414
  21.0 0.0 copy-start.3
  21.0 0.0 copy-start.4
  21.0 6.1 %collective-permute-start.1 = (f32[25,4,256]{2,1,0:T(4,128)}, f32[25,4,256]{2,1,0:T(4,128)S(1)}, u32[]{:S(2)}, u32[]{:S(2)}) collective-permute-start(f32[25,4,256]{2,1,0:T(4,128)} %get-tuple-element.12), channel_id=1, source_target_pairs={{1,0},{2,1},{3,2},{4,3},{5,4},{6,5},{7,6},{8,7},{9,8},{10,9},{11,1... | collective-permute-start | bytes 307208 | tf_op jit(solution)/shard_map/ppermute | solution.py:415
  27.1 1.4 %collective-permute-done.from_low = f32[25,4,256]{2,1,0:T(4,128)S(1)} collective-permute-done((f32[25,4,256]{2,1,0:T(4,128)}, f32[25,4,256]{2,1,0:T(4,128)S(1)}, u32[]{:S(2)}, u32[]{:S(2)}) %collective-permute-start) | collective-permute-done | bytes 102432 | tf_op jit(solution)/shard_map/ppermute | solution.py:414
  28.5 1.1 %collective-permute-done.1.from_high = f32[25,4,256]{2,1,0:T(4,128)S(1)} collective-permute-done((f32[25,4,256]{2,1,0:T(4,128)}, f32[25,4,256]{2,1,0:T(4,128)S(1)}, u32[]{:S(2)}, u32[]{:S(2)}) %collective-permute-start.1) | collective-permute-done | bytes 102432 | tf_op jit(solution)/shard_map/ppermute | solution.py:415
  29.6 0.0 copy-done
  29.6 0.0 copy-done.1
  29.6 2.3 %shard_map.65 = (f32[16,24,128]{2,1,0:T(8,128)}, f32[2,64,128]{2,1,0:T(8,128)S(1)}) custom-call(f32[4,6,64,256]{3,2,1,0:T(8,128)S(1)} %copy-done, s32[64,256]{1,0:T(8,128)S(1)} %copy-done.1, f32[25,4,256]{2,1,0:T(4,128)S(1)} %collective-permute-done.from_low, f32[25,4,256]{2,1,0:T(4,128)S(1)} %collective-permute-done.1.from_high), custom_call_target="tpu_custom_call" | custom-call | flops 10000000 | bytes 3000000 | tf_op jit(solution)/shard_map/pallas_call | solution.py:431
  31.9 18.7 %all-to-all-done.1 = f32[16,168,128]{2,1,0:T(8,128)S(1)} async-done(((f32[16,168,128]{2,1,0:T(8,128)}), f32[16,168,128]{2,1,0:T(8,128)S(1)}, u32[]{:S(2)}, u32[]{:S(2)}) %all-to-all-start.1) | async-done | bytes 1376288 | tf_op jit(solution)/shard_map/all_to_all | solution.py:440
  50.5 4.0 %all-to-all-start = ((f32[16,24,128]{2,1,0:T(8,128)}), f32[16,24,128]{2,1,0:T(8,128)S(1)}, u32[]{:S(2)}, u32[]{:S(2)}) async-start(f32[16,24,128]{2,1,0:T(8,128)} %get-tuple-element.13), calls=%async_computation | async-start | bytes 393216 | tf_op jit(solution)/shard_map/all_to_all | solution.py:441
  55.2 0.0 copy-done.2
  55.2 1.2 %shard_map.67 = (f32[64,256]{1,0:T(8,128)S(1)}, bf16[42,128,128]{2,1,0:T(8,128)(2,1)S(1)}) custom-call(f32[2688,128]{1,0:T(8,128)S(1)} %bitcast.7, s32[1,256]{1,0:T(1,128)S(1)} %bitcast.9), custom_call_target="tpu_custom_call" | custom-call | flops 10000000 | bytes 3000000 | tf_op jit(solution)/shard_map/pallas_call | solution.py:442
  56.4 8.5 %all-to-all-done = f32[16,24,128]{2,1,0:T(8,128)S(1)} async-done(((f32[16,24,128]{2,1,0:T(8,128)}), f32[16,24,128]{2,1,0:T(8,128)S(1)}, u32[]{:S(2)}, u32[]{:S(2)}) %all-to-all-start) | async-done | bytes 196640 | tf_op jit(solution)/shard_map/all_to_all | solution.py:441
  64.8 0.0 copy-done.3
  64.8 0.0 copy-done.4
  64.8 3.6 %shard_map.68 = f32[3072,128]{1,0:T(8,128)S(1)} custom-call(f32[384,128]{1,0:T(8,128)S(1)} %bitcast.8, f32[64,256]{1,0:T(8,128)S(1)} %get-tuple-element.14.picked, bf16[42,128,128]{2,1,0:T(8,128)(2,1)S(1)} %get-tuple-element.15.dev_ref, s32[1,256]{1,0:T(1,128)S(1)} %bitcast.10, s32[1,1]{1,0:T(1,128)S(6)} %copy.7.count, f32[1,256]{1,0:T(1,128)S(1)} %bitcast.11, ...), custom_call_target="tpu_custom_call" | custom-call | flops 60000000 | bytes 3000000 | tf_op jit(solution)/shard_map/pallas_call | solution.py:450
  68.5 42.5 %all_to_all.15.packed = f32[16,192,128]{2,1,0:T(8,128)S(1)} all-to-all(f32[16,192,128]{2,1,0:T(8,128)S(1)} %bitcast.6), channel_id=1, replica_groups=mesh['member'=16,'domain'=32] {'member'}, dimensions={0} | all-to-all | bytes 3145728 | tf_op jit(solution)/shard_map/all_to_all | solution.py:467
  110.9 1.4 %shard_map.69 = f32[4,6,64,256]{3,2,1,0:T(8,128)} custom-call(f32[16,192,128]{2,1,0:T(8,128)S(1)} %all_to_all.15.packed, f32[2,64,128]{2,1,0:T(8,128)S(1)} %get-tuple-element.16.land), custom_call_target="tpu_custom_call" | custom-call | tf_op jit(solution)/shard_map/pallas_call | solution.py:470
Async XLA Ops:
  4.0 25.6 %copy-start = (f32[4,6,64,256]{3,2,1,0:T(8,128)S(1)}, f32[4,6,64,256]{3,2,1,0:T(8,128)}, u32[]{:S(2)}) copy-start(f32[4,6,64,256]{3,2,1,0:T(8,128)} %state.5) | copy-start | bytes 4718596
  4.0 25.6 %copy-start.1 = (s32[64,256]{1,0:T(8,128)S(1)}, s32[64,256]{1,0:T(8,128)}, u32[]{:S(2)}) copy-start(s32[64,256]{1,0:T(8,128)} %land.5) | copy-start | bytes 196612
  4.1 46.5 %all-to-all-start.1 = ((f32[16,168,128]{2,1,0:T(8,128)}), f32[16,168,128]{2,1,0:T(8,128)S(1)}, u32[]{:S(2)}, u32[]{:S(2)}) async-start(f32[16,168,128]{2,1,0:T(8,128)} %shard_map.66), calls=%async_computation.1 | async-start | bytes 2752512 | tf_op jit(solution)/shard_map/all_to_all | solution.py:440
  16.0 39.1 %copy-start.2 = (s32[1,1,256]{2,1,0:T(1,128)S(1)}, s32[1,1,256]{2,1,0:T(1,128)}, u32[]{:S(2)}) copy-start(s32[1,1,256]{2,1,0:T(1,128)} %param.8) | copy-start | bytes 3076
  17.8 10.7 %collective-permute-start = (f32[25,4,256]{2,1,0:T(4,128)}, f32[25,4,256]{2,1,0:T(4,128)S(1)}, u32[]{:S(2)}, u32[]{:S(2)}) collective-permute-start(f32[25,4,256]{2,1,0:T(4,128)} %get-tuple-element.11), channel_id=1, source_target_pairs={{0,1},{1,2},{2,3},{3,4},{4,5},{5,6},{6,7},{7,8},{8,9},{9,10},{10,1... | collective-permute-start | bytes 307208 | tf_op jit(solution)/shard_map/ppermute | solution.py:414
  21.0 43.9 %copy-start.3 = (f32[1,1,256]{2,1,0:T(1,128)S(1)}, f32[1,1,256]{2,1,0:T(1,128)}, u32[]{:S(2)}) copy-start(f32[1,1,256]{2,1,0:T(1,128)} %param.10) | copy-start | bytes 3076
  21.0 43.9 %copy-start.4 = (f32[1,1,256]{2,1,0:T(1,128)S(1)}, f32[1,1,256]{2,1,0:T(1,128)}, u32[]{:S(2)}) copy-start(f32[1,1,256]{2,1,0:T(1,128)} %param.11) | copy-start | bytes 3076
  21.0 8.6 %collective-permute-start.1 = (f32[25,4,256]{2,1,0:T(4,128)}, f32[25,4,256]{2,1,0:T(4,128)S(1)}, u32[]{:S(2)}, u32[]{:S(2)}) collective-permute-start(f32[25,4,256]{2,1,0:T(4,128)} %get-tuple-element.12), channel_id=1, source_target_pairs={{1,0},{2,1},{3,2},{4,3},{5,4},{6,5},{7,6},{8,7},{9,8},{10,9},{11,1... | collective-permute-start | bytes 307208 | tf_op jit(solution)/shard_map/ppermute | solution.py:415
  50.5 14.3 %all-to-all-start = ((f32[16,24,128]{2,1,0:T(8,128)}), f32[16,24,128]{2,1,0:T(8,128)S(1)}, u32[]{:S(2)}, u32[]{:S(2)}) async-start(f32[16,24,128]{2,1,0:T(8,128)} %get-tuple-element.13), calls=%async_computation | async-start | bytes 393216 | tf_op jit(solution)/shard_map/all_to_all | solution.py:441

commit v8 on v7

--- a/solution.py
+++ b/solution.py
@@ -123,34 +123,43 @@
     arrive[0].wait()
     mask = land_ref[...].astype(jnp.float32)
     mask = jnp.concatenate([mask, mask], axis=0)
-    for pair in range(2):
-        members = (2 * pair, 2 * pair + 1)
-        for m in members:
-            arrive[1 + m].wait()
+
+    def cast(members):
         fields = forecast(
             tuple(jnp.concatenate([begin[m, f] for m in members], axis=0) for f in range(6)), mask
         )
         for m in members:
             for f in range(6):
                 for g in range(2):
-                    fields_ref[m % 2, f, g] = fields[f][g][64 * (m % 2) : 64 * (m % 2) + 64]
-        for m in members:
-            for i in range(0, len(BLOCKS), 12):
-                todo = BLOCKS[i : i + 12]
-                tiles = swap_blocks(
-                    [
-                        [
-                            fields_ref[m % 2, f, g, pl.ds((4, 32)[qx] + a, 8, stride=4), :]
-                            for a in range(4)
-                        ]
-                        for f, qx, g in todo
-                    ]
-                )
-                for (f, qx, g), z in zip(todo, tiles):
-                    row = m * INNER_ROWS + f * INNER
-                    for b in range(4):
-                        packed[qx * 8 + g * 4 + b, row : row + INNER, :] = z[b][0:INNER]
-            leave[m].start()
+                    fields_ref[m, f, g] = fields[f][g][64 * (m % 2) : 64 * (m % 2) + 64]
+
+    def pack(m):
+        for i in range(0, len(BLOCKS), 12):
+            todo = BLOCKS[i : i + 12]
+            tiles = swap_blocks(
+                [
+                    [fields_ref[m, f, g, pl.ds((4, 32)[qx] + a, 8, stride=4), :] for a in range(4)]
+                    for f, qx, g in todo
+                ]
+            )
+            for (f, qx, g), z in zip(todo, tiles):
+                row = m * INNER_ROWS + f * INNER
+                for b in range(4):
+                    packed[qx * 8 + g * 4 + b, row : row + INNER, :] = z[b][0:INNER]
+
+    for m in (0, 1):
+        arrive[1 + m].wait()
+    cast((0, 1))
+    for m in (2, 3):
+        arrive[1 + m].wait()
+    pack(0)
+    pack(1)
+    cast((2, 3))
+    leave[0].start()
+    leave[1].start()
+    for m in (2, 3):
+        pack(m)
+        leave[m].start()
     for copy in leave:
         copy.wait()
 
@@ -422,7 +431,7 @@
             pltpu.VMEM((4, 6, 64, 256), jnp.float32),
             pltpu.VMEM((64, 256), jnp.int32),
             pltpu.VMEM((16, 4 * INNER_ROWS, 128), jnp.float32),
-            pltpu.VMEM((2, 6, 2, 64, 128), jnp.float32),
+            pltpu.VMEM((4, 6, 2, 64, 128), jnp.float32),
             pltpu.SemaphoreType.DMA((9,)),
         ],
         compiler_params=pltpu.CompilerParams(vmem_limit_bytes=WHOLE_VMEM),

time: 113 us -> 113 us (level)
  no operation moved by 1% of the time
where the time goes in v8:
time: 113 us; the launch traced here: 112 us
  blocking collectives  42.5 us (38%)
  waiting for transfers between devices  29.7 us (26%)
  starting transfers between devices  25.2 us (22%)
  Pallas kernels  14.2 us (13%)
    all_to_all x1, blocking collectives, local(): lax.all_to_all(increment.reshape(16, 192, 128), 'member', split_axis=0, c...  42.5 us
    all_to_all x1, waiting for transfers between devices, local(): lax.all_to_all(inner, 'member', split_axis=0, concat_axis=0, tiled=True)  18.7 us
    all_to_all x1, starting transfers between devices, local(): lax.all_to_all(inner, 'member', split_axis=0, concat_axis=0, tiled=True)  12 us
    all_to_all x1, waiting for transfers between devices, local(): lax.all_to_all(outer, 'member', split_axis=0, concat_axis=0, tiled=True)  8.46 us
    ppermute x1, starting transfers between devices, local(): from_high = lax.ppermute(to_low, 'domain', backward)  6.09 us
    pallas_call x1, Pallas kernels, local(): pl.pallas_call(inner_kernel, out_shape=shape(16, 4 * INNER_ROWS, 128), in...  3.99 us
    all_to_all x1, starting transfers between devices, local(): lax.all_to_all(outer, 'member', split_axis=0, concat_axis=0, tiled=True)  3.98 us
    pallas_call x1, Pallas kernels, local(): pl.pallas_call(analysis_kernel, out_shape=shape(3072, 128), in_specs=[who...  3.62 us
  transfers between devices with their start and end apart: 4, of which 4 were waited for; matrix products, arithmetic and copies ran while one was open for 0% of the time, Pallas kernels for 5%

profile of v8, /device:TPU:1, one launch (start us, length us, event | category | flops | bytes accessed | tf_op | source)
XLA Modules:
  0.0 112.3 jit_solution(9639769148227685775)
XLA Ops:
  0.0 4.0 %shard_map.66 = f32[16,168,128]{2,1,0:T(8,128)} custom-call(f32[4,6,64,256]{3,2,1,0:T(8,128)} %state.5, s32[64,256]{1,0:T(8,128)} %land.5), custom_call_target="tpu_custom_call" | custom-call | flops 20000000 | bytes 3000000 | tf_op jit(solution)/shard_map/pallas_call | solution.py:425
  4.0 0.0 copy-start
  4.0 0.0 copy-start.1
  4.0 12.0 %all-to-all-start.1 = ((f32[16,168,128]{2,1,0:T(8,128)}), f32[16,168,128]{2,1,0:T(8,128)S(1)}, u32[]{:S(2)}, u32[]{:S(2)}) async-start(f32[16,168,128]{2,1,0:T(8,128)} %shard_map.66), calls=%async_computation.1 | async-start | bytes 2752512 | tf_op jit(solution)/shard_map/all_to_all | solution.py:449
  16.0 0.0 copy-start.2
  16.0 1.8 %shard_map.64 = (f32[25,4,256]{2,1,0:T(4,128)}, f32[25,4,256]{2,1,0:T(4,128)}) custom-call(f32[4,6,64,256]{3,2,1,0:T(8,128)} %state.5, s32[64,256]{1,0:T(8,128)} %land.5), custom_call_target="tpu_custom_call" | custom-call | flops 100000 | bytes 800000 | tf_op jit(solution)/shard_map/pallas_call | solution.py:406
  17.8 3.1 %collective-permute-start = (f32[25,4,256]{2,1,0:T(4,128)}, f32[25,4,256]{2,1,0:T(4,128)S(1)}, u32[]{:S(2)}, u32[]{:S(2)}) collective-permute-start(f32[25,4,256]{2,1,0:T(4,128)} %get-tuple-element.11), channel_id=1, source_target_pairs={{0,1},{1,2},{2,3},{3,4},{4,5},{5,6},{6,7},{7,8},{8,9},{9,10},{10,1... | collective-permute-start | bytes 307208 | tf_op jit(solution)/shard_map/ppermute | solution.py:423
  20.9 0.0 copy-start.3
  20.9 0.0 copy-start.4
  20.9 6.1 %collective-permute-start.1 = (f32[25,4,256]{2,1,0:T(4,128)}, f32[25,4,256]{2,1,0:T(4,128)S(1)}, u32[]{:S(2)}, u32[]{:S(2)}) collective-permute-start(f32[25,4,256]{2,1,0:T(4,128)} %get-tuple-element.12), channel_id=1, source_target_pairs={{1,0},{2,1},{3,2},{4,3},{5,4},{6,5},{7,6},{8,7},{9,8},{10,9},{11,1... | collective-permute-start | bytes 307208 | tf_op jit(solution)/shard_map/ppermute | solution.py:424
  27.0 1.4 %collective-permute-done.from_low = f32[25,4,256]{2,1,0:T(4,128)S(1)} collective-permute-done((f32[25,4,256]{2,1,0:T(4,128)}, f32[25,4,256]{2,1,0:T(4,128)S(1)}, u32[]{:S(2)}, u32[]{:S(2)}) %collective-permute-start) | collective-permute-done | bytes 102432 | tf_op jit(solution)/shard_map/ppermute | solution.py:423
  28.4 1.1 %collective-permute-done.1.from_high = f32[25,4,256]{2,1,0:T(4,128)S(1)} collective-permute-done((f32[25,4,256]{2,1,0:T(4,128)}, f32[25,4,256]{2,1,0:T(4,128)S(1)}, u32[]{:S(2)}, u32[]{:S(2)}) %collective-permute-start.1) | collective-permute-done | bytes 102432 | tf_op jit(solution)/shard_map/ppermute | solution.py:424
  29.6 0.0 copy-done
  29.6 0.0 copy-done.1
  29.6 2.3 %shard_map.65 = (f32[16,24,128]{2,1,0:T(8,128)}, f32[2,64,128]{2,1,0:T(8,128)S(1)}) custom-call(f32[4,6,64,256]{3,2,1,0:T(8,128)S(1)} %copy-done, s32[64,256]{1,0:T(8,128)S(1)} %copy-done.1, f32[25,4,256]{2,1,0:T(4,128)S(1)} %collective-permute-done.from_low, f32[25,4,256]{2,1,0:T(4,128)S(1)} %collective-permute-done.1.from_high), custom_call_target="tpu_custom_call" | custom-call | flops 10000000 | bytes 3000000 | tf_op jit(solution)/shard_map/pallas_call | solution.py:440
  31.8 18.7 %all-to-all-done.1 = f32[16,168,128]{2,1,0:T(8,128)S(1)} async-done(((f32[16,168,128]{2,1,0:T(8,128)}), f32[16,168,128]{2,1,0:T(8,128)S(1)}, u32[]{:S(2)}, u32[]{:S(2)}) %all-to-all-start.1) | async-done | bytes 1376288 | tf_op jit(solution)/shard_map/all_to_all | solution.py:449
  50.5 4.0 %all-to-all-start = ((f32[16,24,128]{2,1,0:T(8,128)}), f32[16,24,128]{2,1,0:T(8,128)S(1)}, u32[]{:S(2)}, u32[]{:S(2)}) async-start(f32[16,24,128]{2,1,0:T(8,128)} %get-tuple-element.13), calls=%async_computation | async-start | bytes 393216 | tf_op jit(solution)/shard_map/all_to_all | solution.py:450
  55.1 0.0 copy-done.2
  55.1 1.2 %shard_map.67 = (f32[64,256]{1,0:T(8,128)S(1)}, bf16[42,128,128]{2,1,0:T(8,128)(2,1)S(1)}) custom-call(f32[2688,128]{1,0:T(8,128)S(1)} %bitcast.7, s32[1,256]{1,0:T(1,128)S(1)} %bitcast.9), custom_call_target="tpu_custom_call" | custom-call | flops 10000000 | bytes 3000000 | tf_op jit(solution)/shard_map/pallas_call | solution.py:451
  56.3 8.5 %all-to-all-done = f32[16,24,128]{2,1,0:T(8,128)S(1)} async-done(((f32[16,24,128]{2,1,0:T(8,128)}), f32[16,24,128]{2,1,0:T(8,128)S(1)}, u32[]{:S(2)}, u32[]{:S(2)}) %all-to-all-start) | async-done | bytes 196640 | tf_op jit(solution)/shard_map/all_to_all | solution.py:450
  64.8 0.0 copy-done.3
  64.8 0.0 copy-done.4
  64.8 3.6 %shard_map.68 = f32[3072,128]{1,0:T(8,128)S(1)} custom-call(f32[384,128]{1,0:T(8,128)S(1)} %bitcast.8, f32[64,256]{1,0:T(8,128)S(1)} %get-tuple-element.14.picked, bf16[42,128,128]{2,1,0:T(8,128)(2,1)S(1)} %get-tuple-element.15.dev_ref, s32[1,256]{1,0:T(1,128)S(1)} %bitcast.10, s32[1,1]{1,0:T(1,128)S(6)} %copy.7.count, f32[1,256]{1,0:T(1,128)S(1)} %bitcast.11, ...), custom_call_target="tpu_custom_call" | custom-call | flops 60000000 | bytes 3000000 | tf_op jit(solution)/shard_map/pallas_call | solution.py:459
  68.4 42.5 %all_to_all.15.packed = f32[16,192,128]{2,1,0:T(8,128)S(1)} all-to-all(f32[16,192,128]{2,1,0:T(8,128)S(1)} %bitcast.6), channel_id=1, replica_groups=mesh['member'=16,'domain'=32] {'member'}, dimensions={0} | all-to-all | bytes 3145728 | tf_op jit(solution)/shard_map/all_to_all | solution.py:476
  110.9 1.4 %shard_map.69 = f32[4,6,64,256]{3,2,1,0:T(8,128)} custom-call(f32[16,192,128]{2,1,0:T(8,128)S(1)} %all_to_all.15.packed, f32[2,64,128]{2,1,0:T(8,128)S(1)} %get-tuple-element.16.land), custom_call_target="tpu_custom_call" | custom-call | tf_op jit(solution)/shard_map/pallas_call | solution.py:479
Async XLA Ops:
  4.0 25.6 %copy-start = (f32[4,6,64,256]{3,2,1,0:T(8,128)S(1)}, f32[4,6,64,256]{3,2,1,0:T(8,128)}, u32[]{:S(2)}) copy-start(f32[4,6,64,256]{3,2,1,0:T(8,128)} %state.5) | copy-start | bytes 4718596
  4.0 25.6 %copy-start.1 = (s32[64,256]{1,0:T(8,128)S(1)}, s32[64,256]{1,0:T(8,128)}, u32[]{:S(2)}) copy-start(s32[64,256]{1,0:T(8,128)} %land.5) | copy-start | bytes 196612
  4.0 46.5 %all-to-all-start.1 = ((f32[16,168,128]{2,1,0:T(8,128)}), f32[16,168,128]{2,1,0:T(8,128)S(1)}, u32[]{:S(2)}, u32[]{:S(2)}) async-start(f32[16,168,128]{2,1,0:T(8,128)} %shard_map.66), calls=%async_computation.1 | async-start | bytes 2752512 | tf_op jit(solution)/shard_map/all_to_all | solution.py:449
  16.0 39.1 %copy-start.2 = (s32[1,1,256]{2,1,0:T(1,128)S(1)}, s32[1,1,256]{2,1,0:T(1,128)}, u32[]{:S(2)}) copy-start(s32[1,1,256]{2,1,0:T(1,128)} %param.8) | copy-start | bytes 3076
  17.8 10.7 %collective-permute-start = (f32[25,4,256]{2,1,0:T(4,128)}, f32[25,4,256]{2,1,0:T(4,128)S(1)}, u32[]{:S(2)}, u32[]{:S(2)}) collective-permute-start(f32[25,4,256]{2,1,0:T(4,128)} %get-tuple-element.11), channel_id=1, source_target_pairs={{0,1},{1,2},{2,3},{3,4},{4,5},{5,6},{6,7},{7,8},{8,9},{9,10},{10,1... | collective-permute-start | bytes 307208 | tf_op jit(solution)/shard_map/ppermute | solution.py:423
  20.9 43.9 %copy-start.3 = (f32[1,1,256]{2,1,0:T(1,128)S(1)}, f32[1,1,256]{2,1,0:T(1,128)}, u32[]{:S(2)}) copy-start(f32[1,1,256]{2,1,0:T(1,128)} %param.10) | copy-start | bytes 3076
  20.9 43.9 %copy-start.4 = (f32[1,1,256]{2,1,0:T(1,128)S(1)}, f32[1,1,256]{2,1,0:T(1,128)}, u32[]{:S(2)}) copy-start(f32[1,1,256]{2,1,0:T(1,128)} %param.11) | copy-start | bytes 3076
  20.9 8.6 %collective-permute-start.1 = (f32[25,4,256]{2,1,0:T(4,128)}, f32[25,4,256]{2,1,0:T(4,128)S(1)}, u32[]{:S(2)}, u32[]{:S(2)}) collective-permute-start(f32[25,4,256]{2,1,0:T(4,128)} %get-tuple-element.12), channel_id=1, source_target_pairs={{1,0},{2,1},{3,2},{4,3},{5,4},{6,5},{7,6},{8,7},{9,8},{10,9},{11,1... | collective-permute-start | bytes 307208 | tf_op jit(solution)/shard_map/ppermute | solution.py:424
  50.5 14.3 %all-to-all-start = ((f32[16,24,128]{2,1,0:T(8,128)}), f32[16,24,128]{2,1,0:T(8,128)S(1)}, u32[]{:S(2)}, u32[]{:S(2)}) async-start(f32[16,24,128]{2,1,0:T(8,128)} %get-tuple-element.13), calls=%async_computation | async-start | bytes 393216 | tf_op jit(solution)/shard_map/all_to_all | solution.py:450

commit v9 on v8

--- a/solution.py
+++ b/solution.py
@@ -302,17 +302,15 @@
         return coarse + fine
 
     def over_slots(a, b):
-        return lax.dot_general(
-            a,
-            jnp.concatenate([b, b], axis=0),
-            (((1,), (1,)), ((), ())),
-            preferred_element_type=jnp.float32,
-        )
-
-    (ah, am, al), (bh, bm, bl) = parts(scaled), parts(spread)
-    gram = over_slots(ah, bh) + (
-        (over_slots(ah, bm) + over_slots(am, bh))
-        + (over_slots(am, bm) + over_slots(ah, bl) + over_slots(al, bh))
+        return jnp.dot(a, b, preferred_element_type=jnp.float32)
+
+    ah, am, al = parts(scaled)
+    bh, bm, bl = parts(jnp.concatenate([spread, spread], axis=0).T)
+    first = over_slots(jnp.concatenate([ah, am, al], axis=0), bh)
+    second = over_slots(jnp.concatenate([ah, am], axis=0), bm)
+    gram = first[0:members] + (
+        (first[members : 2 * members] + second[0:members])
+        + (first[2 * members :] + second[members:] + over_slots(ah, bl))
     )
     moved = jnp.sum(once * jnp.sum(scaled * innovation, axis=1, keepdims=True), axis=0, keepdims=True)
     system = (members - 1.0) * twice + gram

time: 113 us -> 113 us (level)
  no operation moved by 1% of the time
where the time goes in v9:
time: 113 us; the launch traced here: 112 us
  blocking collectives  42.5 us (38%)
  waiting for transfers between devices  29.7 us (26%)
  starting transfers between devices  25.2 us (22%)
  Pallas kernels  14.3 us (13%)
    all_to_all x1, blocking collectives, local(): lax.all_to_all(increment.reshape(16, 192, 128), 'member', split_axis=0, c...  42.5 us
    all_to_all x1, waiting for transfers between devices, local(): lax.all_to_all(inner, 'member', split_axis=0, concat_axis=0, tiled=True)  18.7 us
    all_to_all x1, starting transfers between devices, local(): lax.all_to_all(inner, 'member', split_axis=0, concat_axis=0, tiled=True)  12 us
    all_to_all x1, waiting for transfers between devices, local(): lax.all_to_all(outer, 'member', split_axis=0, concat_axis=0, tiled=True)  8.46 us
    ppermute x1, starting transfers between devices, local(): from_high = lax.ppermute(to_low, 'domain', backward)  6.09 us
    pallas_call x1, Pallas kernels, local(): pl.pallas_call(inner_kernel, out_shape=shape(16, 4 * INNER_ROWS, 128), in...  3.99 us
    all_to_all x1, starting transfers between devices, local(): lax.all_to_all(outer, 'member', split_axis=0, concat_axis=0, tiled=True)  3.98 us
    pallas_call x1, Pallas kernels, local(): pl.pallas_call(analysis_kernel, out_shape=shape(3072, 128), in_specs=[who...  3.65 us
  transfers between devices with their start and end apart: 4, of which 4 were waited for; matrix products, arithmetic and copies ran while one was open for 0% of the time, Pallas kernels for 5%

profile of v9, /device:TPU:1, one launch (start us, length us, event | category | flops | bytes accessed | tf_op | source)
XLA Modules:
  0.0 112.3 jit_solution(12429176419158151951)
XLA Ops:
  0.0 4.0 %shard_map.66 = f32[16,168,128]{2,1,0:T(8,128)} custom-call(f32[4,6,64,256]{3,2,1,0:T(8,128)} %state.5, s32[64,256]{1,0:T(8,128)} %land.5), custom_call_target="tpu_custom_call" | custom-call | flops 20000000 | bytes 3000000 | tf_op jit(solution)/shard_map/pallas_call | solution.py:423
  4.0 0.0 copy-start
  4.0 0.0 copy-start.1
  4.0 12.0 %all-to-all-start.1 = ((f32[16,168,128]{2,1,0:T(8,128)}), f32[16,168,128]{2,1,0:T(8,128)S(1)}, u32[]{:S(2)}, u32[]{:S(2)}) async-start(f32[16,168,128]{2,1,0:T(8,128)} %shard_map.66), calls=%async_computation.1 | async-start | bytes 2752512 | tf_op jit(solution)/shard_map/all_to_all | solution.py:447
  16.0 0.0 copy-start.2
  16.0 1.8 %shard_map.64 = (f32[25,4,256]{2,1,0:T(4,128)}, f32[25,4,256]{2,1,0:T(4,128)}) custom-call(f32[4,6,64,256]{3,2,1,0:T(8,128)} %state.5, s32[64,256]{1,0:T(8,128)} %land.5), custom_call_target="tpu_custom_call" | custom-call | flops 100000 | bytes 800000 | tf_op jit(solution)/shard_map/pallas_call | solution.py:404
  17.8 3.1 %collective-permute-start = (f32[25,4,256]{2,1,0:T(4,128)}, f32[25,4,256]{2,1,0:T(4,128)S(1)}, u32[]{:S(2)}, u32[]{:S(2)}) collective-permute-start(f32[25,4,256]{2,1,0:T(4,128)} %get-tuple-element.11), channel_id=1, source_target_pairs={{0,1},{1,2},{2,3},{3,4},{4,5},{5,6},{6,7},{7,8},{8,9},{9,10},{10,1... | collective-permute-start | bytes 307208 | tf_op jit(solution)/shard_map/ppermute | solution.py:421
  20.9 0.0 copy-start.3
  20.9 0.0 copy-start.4
  20.9 6.1 %collective-permute-start.1 = (f32[25,4,256]{2,1,0:T(4,128)}, f32[25,4,256]{2,1,0:T(4,128)S(1)}, u32[]{:S(2)}, u32[]{:S(2)}) collective-permute-start(f32[25,4,256]{2,1,0:T(4,128)} %get-tuple-element.12), channel_id=1, source_target_pairs={{1,0},{2,1},{3,2},{4,3},{5,4},{6,5},{7,6},{8,7},{9,8},{10,9},{11,1... | collective-permute-start | bytes 307208 | tf_op jit(solution)/shard_map/ppermute | solution.py:422
  27.0 1.4 %collective-permute-done.from_low = f32[25,4,256]{2,1,0:T(4,128)S(1)} collective-permute-done((f32[25,4,256]{2,1,0:T(4,128)}, f32[25,4,256]{2,1,0:T(4,128)S(1)}, u32[]{:S(2)}, u32[]{:S(2)}) %collective-permute-start) | collective-permute-done | bytes 102432 | tf_op jit(solution)/shard_map/ppermute | solution.py:421
  28.4 1.1 %collective-permute-done.1.from_high = f32[25,4,256]{2,1,0:T(4,128)S(1)} collective-permute-done((f32[25,4,256]{2,1,0:T(4,128)}, f32[25,4,256]{2,1,0:T(4,128)S(1)}, u32[]{:S(2)}, u32[]{:S(2)}) %collective-permute-start.1) | collective-permute-done | bytes 102432 | tf_op jit(solution)/shard_map/ppermute | solution.py:422
  29.6 0.0 copy-done
  29.6 0.0 copy-done.1
  29.6 2.3 %shard_map.65 = (f32[16,24,128]{2,1,0:T(8,128)}, f32[2,64,128]{2,1,0:T(8,128)S(1)}) custom-call(f32[4,6,64,256]{3,2,1,0:T(8,128)S(1)} %copy-done, s32[64,256]{1,0:T(8,128)S(1)} %copy-done.1, f32[25,4,256]{2,1,0:T(4,128)S(1)} %collective-permute-done.from_low, f32[25,4,256]{2,1,0:T(4,128)S(1)} %collective-permute-done.1.from_high), custom_call_target="tpu_custom_call" | custom-call | flops 10000000 | bytes 3000000 | tf_op jit(solution)/shard_map/pallas_call | solution.py:438
  31.8 18.7 %all-to-all-done.1 = f32[16,168,128]{2,1,0:T(8,128)S(1)} async-done(((f32[16,168,128]{2,1,0:T(8,128)}), f32[16,168,128]{2,1,0:T(8,128)S(1)}, u32[]{:S(2)}, u32[]{:S(2)}) %all-to-all-start.1) | async-done | bytes 1376288 | tf_op jit(solution)/shard_map/all_to_all | solution.py:447
  50.5 4.0 %all-to-all-start = ((f32[16,24,128]{2,1,0:T(8,128)}), f32[16,24,128]{2,1,0:T(8,128)S(1)}, u32[]{:S(2)}, u32[]{:S(2)}) async-start(f32[16,24,128]{2,1,0:T(8,128)} %get-tuple-element.13), calls=%async_computation | async-start | bytes 393216 | tf_op jit(solution)/shard_map/all_to_all | solution.py:448
  55.1 0.0 copy-done.2
  55.1 1.2 %shard_map.67 = (f32[64,256]{1,0:T(8,128)S(1)}, bf16[42,128,128]{2,1,0:T(8,128)(2,1)S(1)}) custom-call(f32[2688,128]{1,0:T(8,128)S(1)} %bitcast.7, s32[1,256]{1,0:T(1,128)S(1)} %bitcast.9), custom_call_target="tpu_custom_call" | custom-call | flops 10000000 | bytes 3000000 | tf_op jit(solution)/shard_map/pallas_call | solution.py:449
  56.3 8.5 %all-to-all-done = f32[16,24,128]{2,1,0:T(8,128)S(1)} async-done(((f32[16,24,128]{2,1,0:T(8,128)}), f32[16,24,128]{2,1,0:T(8,128)S(1)}, u32[]{:S(2)}, u32[]{:S(2)}) %all-to-all-start) | async-done | bytes 196640 | tf_op jit(solution)/shard_map/all_to_all | solution.py:448
  64.8 0.0 copy-done.3
  64.8 0.0 copy-done.4
  64.8 3.7 %shard_map.68 = f32[3072,128]{1,0:T(8,128)S(1)} custom-call(f32[384,128]{1,0:T(8,128)S(1)} %bitcast.8, f32[64,256]{1,0:T(8,128)S(1)} %get-tuple-element.14.picked, bf16[42,128,128]{2,1,0:T(8,128)(2,1)S(1)} %get-tuple-element.15.dev_ref, s32[1,256]{1,0:T(1,128)S(1)} %bitcast.10, s32[1,1]{1,0:T(1,128)S(6)} %copy.7.count, f32[1,256]{1,0:T(1,128)S(1)} %bitcast.11, ...), custom_call_target="tpu_custom_call" | custom-call | flops 60000000 | bytes 3000000 | tf_op jit(solution)/shard_map/pallas_call | solution.py:457
  68.5 42.5 %all_to_all.15.packed = f32[16,192,128]{2,1,0:T(8,128)S(1)} all-to-all(f32[16,192,128]{2,1,0:T(8,128)S(1)} %bitcast.6), channel_id=1, replica_groups=mesh['member'=16,'domain'=32] {'member'}, dimensions={0} | all-to-all | bytes 3145728 | tf_op jit(solution)/shard_map/all_to_all | solution.py:474
  110.9 1.4 %shard_map.69 = f32[4,6,64,256]{3,2,1,0:T(8,128)} custom-call(f32[16,192,128]{2,1,0:T(8,128)S(1)} %all_to_all.15.packed, f32[2,64,128]{2,1,0:T(8,128)S(1)} %get-tuple-element.16.land), custom_call_target="tpu_custom_call" | custom-call | tf_op jit(solution)/shard_map/pallas_call | solution.py:477
Async XLA Ops:
  4.0 25.6 %copy-start = (f32[4,6,64,256]{3,2,1,0:T(8,128)S(1)}, f32[4,6,64,256]{3,2,1,0:T(8,128)}, u32[]{:S(2)}) copy-start(f32[4,6,64,256]{3,2,1,0:T(8,128)} %state.5) | copy-start | bytes 4718596
  4.0 25.6 %copy-start.1 = (s32[64,256]{1,0:T(8,128)S(1)}, s32[64,256]{1,0:T(8,128)}, u32[]{:S(2)}) copy-start(s32[64,256]{1,0:T(8,128)} %land.5) | copy-start | bytes 196612
  4.0 46.5 %all-to-all-start.1 = ((f32[16,168,128]{2,1,0:T(8,128)}), f32[16,168,128]{2,1,0:T(8,128)S(1)}, u32[]{:S(2)}, u32[]{:S(2)}) async-start(f32[16,168,128]{2,1,0:T(8,128)} %shard_map.66), calls=%async_computation.1 | async-start | bytes 2752512 | tf_op jit(solution)/shard_map/all_to_all | solution.py:447
  16.0 39.1 %copy-start.2 = (s32[1,1,256]{2,1,0:T(1,128)S(1)}, s32[1,1,256]{2,1,0:T(1,128)}, u32[]{:S(2)}) copy-start(s32[1,1,256]{2,1,0:T(1,128)} %param.8) | copy-start | bytes 3076
  17.8 10.7 %collective-permute-start = (f32[25,4,256]{2,1,0:T(4,128)}, f32[25,4,256]{2,1,0:T(4,128)S(1)}, u32[]{:S(2)}, u32[]{:S(2)}) collective-permute-start(f32[25,4,256]{2,1,0:T(4,128)} %get-tuple-element.11), channel_id=1, source_target_pairs={{0,1},{1,2},{2,3},{3,4},{4,5},{5,6},{6,7},{7,8},{8,9},{9,10},{10,1... | collective-permute-start | bytes 307208 | tf_op jit(solution)/shard_map/ppermute | solution.py:421
  20.9 43.9 %copy-start.3 = (f32[1,1,256]{2,1,0:T(1,128)S(1)}, f32[1,1,256]{2,1,0:T(1,128)}, u32[]{:S(2)}) copy-start(f32[1,1,256]{2,1,0:T(1,128)} %param.10) | copy-start | bytes 3076
  20.9 43.9 %copy-start.4 = (f32[1,1,256]{2,1,0:T(1,128)S(1)}, f32[1,1,256]{2,1,0:T(1,128)}, u32[]{:S(2)}) copy-start(f32[1,1,256]{2,1,0:T(1,128)} %param.11) | copy-start | bytes 3076
  20.9 8.6 %collective-permute-start.1 = (f32[25,4,256]{2,1,0:T(4,128)}, f32[25,4,256]{2,1,0:T(4,128)S(1)}, u32[]{:S(2)}, u32[]{:S(2)}) collective-permute-start(f32[25,4,256]{2,1,0:T(4,128)} %get-tuple-element.12), channel_id=1, source_target_pairs={{1,0},{2,1},{3,2},{4,3},{5,4},{6,5},{7,6},{8,7},{9,8},{10,9},{11,1... | collective-permute-start | bytes 307208 | tf_op jit(solution)/shard_map/ppermute | solution.py:422
  50.5 14.3 %all-to-all-start = ((f32[16,24,128]{2,1,0:T(8,128)}), f32[16,24,128]{2,1,0:T(8,128)S(1)}, u32[]{:S(2)}, u32[]{:S(2)}) async-start(f32[16,24,128]{2,1,0:T(8,128)} %get-tuple-element.13), calls=%async_computation | async-start | bytes 393216 | tf_op jit(solution)/shard_map/all_to_all | solution.py:448
